TPU v7x, 128 devices: a whole 4x4x4 slice. The times are simulated.
128 devices in a mesh: rows: 32 (over z, y, core), cols: 4 (over x).
Axes of the slice: x: 4, y: 4, z: 4, core: 2. Of those that a mesh axis runs over, the one named last changes fastest.
Arguments:
- basis: float32 [64, 262144], P('cols', 'rows'), may hold values from -450 to 450
- blocks: bfloat16 [1024, 4, 256, 256], P('rows'), may hold values from -16 to 1, as said below
- far_cols: int32 [1024], P('rows'), may hold values from 0 to 1023, as said below
Outputs:
- basis_out: float32 [64, 262144], P('cols', 'rows')
- ritz: float32 [64, 64], P(None, 'cols')
Inputs may be any that keep to these rules, and one draw needn't show every extreme that they name: Off-diagonal entries are positive; each diagonal entry of a diagonal block is minus the sum of the other entries of its row over the four blocks, rounded to bfloat16. `far_cols`: the block rows of one device name at most 2 far columns among the block rows of any one device; the block rows of some device are named by exactly 2 block rows of every device.
All inputs are finite; a program needn't handle non-finite values.
Results may differ from a plain program's by a relative error of at most 0.0036.
Values may be sent and summed in bfloat16 or wider, within the bound.
No kernel may reach another device: no remote copies, remote signals or barrier semaphores. Data moves between devices by JAX's collectives and lax.ppermute only.
A program may use at most 128 MiB of HBM per device.

v0:
```python
import jax
import jax.numpy as jnp
from jax import lax
from jax.sharding import PartitionSpec as P

ITERS = 4


def with_halo(block, sides, width):
    for axis, dim in sides:
        count = lax.axis_size(axis)
        forward = [(i, i + 1) for i in range(count - 1)]
        forward.append((count - 1, 0))
        backward = [(target, source) for source, target in forward]
        low = lax.ppermute(
            lax.slice_in_dim(block, block.shape[dim] - width, None, axis=dim), axis, forward
        )
        high = lax.ppermute(lax.slice_in_dim(block, 0, width, axis=dim), axis, backward)
        block = jnp.concatenate([low, block, high], axis=dim)
    return block


def block_product(pieces, blocks, position):
    return jnp.einsum(
        "jbt,bst->jbs", pieces, blocks[:, position], preferred_element_type=jnp.float32
    )


def body(basis, blocks, far_cols):
    width = basis.shape[0]
    block_rows = blocks.shape[0]
    block_size = blocks.shape[2]
    row_devices = lax.axis_size("rows")
    total_states = block_rows * block_size * row_devices
    modes = width * lax.axis_size("cols")
    highest = lax.Precision.HIGHEST

    def apply_generator(iterate_bf):
        shaped = iterate_bf.reshape(width, block_rows, block_size)
        result = block_product(shaped, blocks, 0)
        empty = jnp.zeros((width, block_rows, block_size), jnp.bfloat16)
        piece = lax.all_gather(shaped, "rows", axis=1, tiled=True)
        inside = jnp.logical_and(far_cols >= 0, far_cols < piece.shape[1])
        taken = jnp.take(piece, jnp.clip(far_cols, 0, piece.shape[1] - 1), axis=1)
        remote = jnp.where(inside[None, :, None], taken, empty)
        extended = with_halo(shaped, (("rows", 1),), 1)
        result = result + block_product(extended[:, :-2], blocks, 1)
        result = result + block_product(extended[:, 2:], blocks, 2)
        result = result + block_product(remote, blocks, 3)
        return result.reshape(width, block_rows * block_size)

    iterate = basis
    for step in range(ITERS):
        iterate = iterate + 0.2 * apply_generator(iterate.astype(jnp.bfloat16))
    whole_iterate = lax.all_gather(iterate, "cols", axis=0, tiled=True)
    contract = (((1,), (1,)), ((), ()))
    gram_part = lax.dot_general(whole_iterate, iterate, contract, precision=highest)
    column_start = lax.axis_index("cols") * width
    gram_mine = lax.psum(gram_part, "rows")
    gram = lax.all_gather(gram_mine, "cols", axis=1, tiled=True) / total_states
    applied = apply_generator(iterate.astype(jnp.bfloat16))
    product_part = lax.dot_general(whole_iterate, applied, contract, precision=highest)
    product_mine = lax.psum(product_part, "rows")
    product = lax.all_gather(product_mine, "cols", axis=1, tiled=True) / total_states
    factor = jnp.linalg.cholesky(gram)
    identity_square = jnp.eye(modes, dtype=factor.dtype)
    inverse_factor = lax.linalg.triangular_solve(
        factor, identity_square, left_side=True, lower=True
    )
    own_rows = lax.dynamic_slice_in_dim(inverse_factor, column_start, width, 0)
    basis_out = jnp.dot(own_rows, whole_iterate, precision=highest)
    left_part = jnp.dot(inverse_factor, product, precision=highest)
    ritz_whole = jnp.dot(left_part, inverse_factor.T, precision=highest)
    ritz = lax.dynamic_slice_in_dim(ritz_whole, column_start, width, 1)
    return (basis_out, ritz)


def solution(mesh):
    in_specs = (P("cols", "rows"), P("rows", None, None, None), P("rows"))
    out_specs = (P("cols", "rows"), P(None, "cols"))
    return jax.shard_map(body, mesh=mesh, in_specs=in_specs, out_specs=out_specs, check_vma=False)
```

profile of v0, /device:TPU:0, one launch (start us, length us, event | category | flops | bytes accessed | tf_op | source)
XLA Modules:
  0.0 539.1 jit_solution(13265493274930220181)
XLA Ops:
  9.8 6.0 %collective-permute-start.1 = (bf16[16,1,256]{2,0,1:T(8,128)(2,1)S(1)}, bf16[16,1,256]{2,0,1:T(8,128)(2,1)S(1)}, u32[]{:S(2)}, u32[]{:S(2)}) collective-permute-start(bf16[16,1,256]{2,0,1:T(8,128)(2,1)S(1)} %get-tuple-element.23), channel_id=1, source_target_pairs={{4,0},{8,4},{12,8},{16,12},{20,16},{24,20},{28,24},{32,28},{36,32}... | collective-permute-start | bytes 24584 | tf_op jit(solution)/shard_map/ppermute | solution.py:18
  19.9 3.6 fusion.84
  23.5 3.5 fusion.81
  27.0 39.3 %all-gather.7.cloned.1.call-done = bf16[16,1024,256]{2,0,1:T(8,128)(2,1)} async-done(((bf16[16,32,256]{2,0,1:T(8,128)(2,1)}), bf16[16,1024,256]{2,0,1:T(8,128)(2,1)}) %all-gather.7.cloned.1.call-update) | async-done | bytes 8388624 | tf_op jit(solution)/shard_map/all_gather | solution.py:42
  66.4 3.9 gather_fusion
  70.3 3.4 fusion.72
  81.6 3.6 fusion.16
  85.2 42.1 %all-gather.9.cloned.1.call-done = bf16[16,1024,256]{2,0,1:T(8,128)(2,1)} async-done(((bf16[16,32,256]{2,0,1:T(8,128)(2,1)}), bf16[16,1024,256]{2,0,1:T(8,128)(2,1)}) %all-gather.9.cloned.1.call-update) | async-done | bytes 8388624 | tf_op jit(solution)/shard_map/all_gather | solution.py:42
  127.3 3.9 gather_fusion.1
  131.2 3.4 fusion.6
  134.7 3.4 fusion.141
  145.9 3.6 fusion.14
  149.6 42.1 %all-gather.11.cloned.1.call-done = bf16[16,1024,256]{2,0,1:T(8,128)(2,1)} async-done(((bf16[16,32,256]{2,0,1:T(8,128)(2,1)}), bf16[16,1024,256]{2,0,1:T(8,128)(2,1)}) %all-gather.11.cloned.1.call-update) | async-done | bytes 8388624 | tf_op jit(solution)/shard_map/all_gather | solution.py:42
  191.6 3.9 gather_fusion.2
  195.6 3.4 fusion.4
  199.0 3.4 fusion.129
  210.3 3.6 fusion.12
  213.9 42.1 %all-gather.13.cloned.1.call-done = bf16[16,1024,256]{2,0,1:T(8,128)(2,1)} async-done(((bf16[16,32,256]{2,0,1:T(8,128)(2,1)}), bf16[16,1024,256]{2,0,1:T(8,128)(2,1)}) %all-gather.13.cloned.1.call-update) | async-done | bytes 8388624 | tf_op jit(solution)/shard_map/all_gather | solution.py:42
  256.0 3.9 gather_fusion.3
  259.9 3.4 fusion.2
  263.3 3.4 fusion.117
  275.5 3.8 fusion.10
  279.3 18.8 %all-gather.15.cloned.1.call-done = f32[64,8192]{1,0:T(8,128)} async-done(((f32[16,8192]{1,0:T(8,128)}), f32[64,8192]{1,0:T(8,128)}) %all-gather.15.cloned.1.call-update) | async-done | bytes 2097168 | tf_op jit(solution)/shard_map/all_gather | solution.py:55
  301.5 51.9 %all-gather.17.cloned.1.call-done = bf16[16,1024,256]{2,0,1:T(8,128)(2,1)} async-done(((bf16[16,32,256]{2,0,1:T(8,128)(2,1)}), bf16[16,1024,256]{2,0,1:T(8,128)(2,1)}) %all-gather.17.cloned.1.call-update) | async-done | bytes 8388624 | tf_op jit(solution)/shard_map/all_gather | solution.py:42
  353.3 3.9 gather_fusion.4
  357.3 3.4 fusion
  360.7 3.6 fusion.105
  366.1 126.6 %all-reduce = (f32[64,16]{0,1:T(8,128)S(1)}, f32[64,16]{0,1:T(8,128)S(1)}) all-reduce(f32[64,16]{0,1:T(8,128)S(1)} %fusion.239, f32[64,16]{0,1:T(8,128)S(1)} %fusion.240), channel_id=1, replica_groups=mesh['rows'=32,'cols'=4] {'rows'}, use_global_device_ids=true, to_apply=%region_0.2 | all-reduce | flops 2048 | bytes 16384 | tf_op jit(solution)/shard_map/psum | solution.py:59
  492.6 12.4 %all_gather.29 = f32[64,64]{0,1:T(8,128)S(1)} all-gather(f32[64,16]{0,1:T(8,128)S(1)} %get-tuple-element.3), channel_id=1, replica_groups=mesh['rows'=32,'cols'=4] {'cols'}, dimensions={1}, use_global_device_ids=true | all-gather | bytes 20480 | tf_op jit(solution)/shard_map/all_gather | solution.py:60
  505.2 5.8 %cholesky.17 = f32[64,64]{1,0:T(8,128)S(1)} custom-call(f32[64,64]{1,0:T(8,128)S(1)} %fusion.202), custom_call_target="Cholesky" | custom-call | tf_op jit(solution)/shard_map/jit(cholesky)/cholesky | solution.py:65
  512.4 4.9 custom-call.6
  517.5 11.9 %all_gather.31 = f32[64,64]{0,1:T(8,128)S(1)} all-gather(f32[64,16]{0,1:T(8,128)S(1)} %get-tuple-element.4), channel_id=1, replica_groups=mesh['rows'=32,'cols'=4] {'cols'}, dimensions={1}, use_global_device_ids=true | all-gather | bytes 20480 | tf_op jit(solution)/shard_map/all_gather | solution.py:64
  (87 shorter events, 48.5 us)
Async XLA Ops:
  7.2 59.2 %all-gather.7.cloned.1.call-start = ((), (), s32[]{:S(2)}) async-start(), calls=%async_computation | async-start | bytes 8650752 | tf_op jit(solution)/shard_map/all_gather | solution.py:42
  9.0 118.3 %all-gather.9.cloned.1.call-start = ((), (), s32[]{:S(2)}) async-start(), calls=%async_computation.1 | async-start | bytes 8650752 | tf_op jit(solution)/shard_map/all_gather | solution.py:42
  9.8 10.1 %collective-permute-start = (bf16[16,1,256]{2,0,1:T(8,128)(2,1)S(1)}, bf16[16,1,256]{2,0,1:T(8,128)(2,1)S(1)}, u32[]{:S(2)}, u32[]{:S(2)}) collective-permute-start(bf16[16,1,256]{2,0,1:T(8,128)(2,1)S(1)} %get-tuple-element.24), channel_id=1, source_target_pairs={{0,4},{4,8},{8,12},{12,16},{16,20},{20,24},{24,28},{28,32},{32,36}... | collective-permute-start | bytes 24584 | tf_op jit(solution)/shard_map/ppermute | solution.py:15
  9.8 13.7 %collective-permute-start.1 = (bf16[16,1,256]{2,0,1:T(8,128)(2,1)S(1)}, bf16[16,1,256]{2,0,1:T(8,128)(2,1)S(1)}, u32[]{:S(2)}, u32[]{:S(2)}) collective-permute-start(bf16[16,1,256]{2,0,1:T(8,128)(2,1)S(1)} %get-tuple-element.23), channel_id=1, source_target_pairs={{4,0},{8,4},{12,8},{16,12},{20,16},{24,20},{28,24},{32,28},{36,32}... | collective-permute-start | bytes 24584 | tf_op jit(solution)/shard_map/ppermute | solution.py:18
  19.9 3.6 copy-start.4
  23.5 50.3 %copy-start.2 = (f32[16,8192]{1,0:T(8,128)S(1)}, f32[16,8192]{1,0:T(8,128)}, u32[]{:S(2)}) copy-start(f32[16,8192]{1,0:T(8,128)} %param.5) | copy-start | bytes 1572868
  74.6 117.0 %all-gather.11.cloned.1.call-start = ((), (), s32[]{:S(2)}) async-start(), calls=%async_computation.2 | async-start | bytes 8650752 | tf_op jit(solution)/shard_map/all_gather | solution.py:42
  75.4 6.2 %collective-permute-start.3 = (bf16[16,1,256]{2,0,1:T(8,128)(2,1)S(1)}, bf16[16,1,256]{2,0,1:T(8,128)(2,1)S(1)}, u32[]{:S(2)}, u32[]{:S(2)}) collective-permute-start(bf16[16,1,256]{2,0,1:T(8,128)(2,1)S(1)} %get-tuple-element.22), channel_id=1, source_target_pairs={{4,0},{8,4},{12,8},{16,12},{20,16},{24,20},{28,24},{32,28},{36,32}... | collective-permute-start | bytes 24584 | tf_op jit(solution)/shard_map/ppermute | solution.py:18
  81.6 53.1 %copy-start.5 = (bf16[2,32,8,256]{3,2,0,1:T(8,128)(2,1)S(1)}, bf16[2,32,8,256]{3,2,0,1:T(8,128)(2,1)}, u32[]{:S(2)}) copy-start(bf16[2,32,8,256]{3,2,0,1:T(8,128)(2,1)} %copy.157) | copy-start | bytes 786436
  81.6 53.1 %collective-permute-start.2 = (bf16[16,1,256]{2,0,1:T(8,128)(2,1)S(1)}, bf16[16,1,256]{2,0,1:T(8,128)(2,1)S(1)}, u32[]{:S(2)}, u32[]{:S(2)}) collective-permute-start(bf16[16,1,256]{2,0,1:T(8,128)(2,1)S(1)} %get-tuple-element.21), channel_id=1, source_target_pairs={{0,4},{4,8},{8,12},{12,16},{16,20},{20,24},{24,28},{28,32},{32,36}... | collective-permute-start | bytes 24584 | tf_op jit(solution)/shard_map/ppermute | solution.py:15
  138.9 117.0 %all-gather.13.cloned.1.call-start = ((), (), s32[]{:S(2)}) async-start(), calls=%async_computation.3 | async-start | bytes 8650752 | tf_op jit(solution)/shard_map/all_gather | solution.py:42
  139.7 6.2 %collective-permute-start.5 = (bf16[16,1,256]{2,0,1:T(8,128)(2,1)S(1)}, bf16[16,1,256]{2,0,1:T(8,128)(2,1)S(1)}, u32[]{:S(2)}, u32[]{:S(2)}) collective-permute-start(bf16[16,1,256]{2,0,1:T(8,128)(2,1)S(1)} %get-tuple-element.20), channel_id=1, source_target_pairs={{4,0},{8,4},{12,8},{16,12},{20,16},{24,20},{28,24},{32,28},{36,32}... | collective-permute-start | bytes 24584 | tf_op jit(solution)/shard_map/ppermute | solution.py:18
  145.9 53.1 %copy-start.6 = (bf16[2,32,8,256]{3,2,0,1:T(8,128)(2,1)S(1)}, bf16[2,32,8,256]{3,2,0,1:T(8,128)(2,1)}, u32[]{:S(2)}) copy-start(bf16[2,32,8,256]{3,2,0,1:T(8,128)(2,1)} %copy.156) | copy-start | bytes 786436
  145.9 53.1 %collective-permute-start.4 = (bf16[16,1,256]{2,0,1:T(8,128)(2,1)S(1)}, bf16[16,1,256]{2,0,1:T(8,128)(2,1)S(1)}, u32[]{:S(2)}, u32[]{:S(2)}) collective-permute-start(bf16[16,1,256]{2,0,1:T(8,128)(2,1)S(1)} %get-tuple-element.19), channel_id=1, source_target_pairs={{0,4},{4,8},{8,12},{12,16},{16,20},{20,24},{24,28},{28,32},{32,36}... | collective-permute-start | bytes 24584 | tf_op jit(solution)/shard_map/ppermute | solution.py:15
  203.3 94.9 %all-gather.15.cloned.1.call-start = ((), (), s32[]{:S(2)}) async-start(), calls=%async_computation.4 | async-start | bytes 2621440 | tf_op jit(solution)/shard_map/all_gather | solution.py:55
  204.0 6.2 %collective-permute-start.7 = (bf16[16,1,256]{2,0,1:T(8,128)(2,1)S(1)}, bf16[16,1,256]{2,0,1:T(8,128)(2,1)S(1)}, u32[]{:S(2)}, u32[]{:S(2)}) collective-permute-start(bf16[16,1,256]{2,0,1:T(8,128)(2,1)S(1)} %get-tuple-element.18), channel_id=1, source_target_pairs={{4,0},{8,4},{12,8},{16,12},{20,16},{24,20},{28,24},{32,28},{36,32}... | collective-permute-start | bytes 24584 | tf_op jit(solution)/shard_map/ppermute | solution.py:18
  210.3 53.1 %copy-start.7 = (bf16[2,32,8,256]{3,2,0,1:T(8,128)(2,1)S(1)}, bf16[2,32,8,256]{3,2,0,1:T(8,128)(2,1)}, u32[]{:S(2)}) copy-start(bf16[2,32,8,256]{3,2,0,1:T(8,128)(2,1)} %copy.155) | copy-start | bytes 786436
  210.3 53.1 %collective-permute-start.6 = (bf16[16,1,256]{2,0,1:T(8,128)(2,1)S(1)}, bf16[16,1,256]{2,0,1:T(8,128)(2,1)S(1)}, u32[]{:S(2)}, u32[]{:S(2)}) collective-permute-start(bf16[16,1,256]{2,0,1:T(8,128)(2,1)S(1)} %get-tuple-element.17), channel_id=1, source_target_pairs={{0,4},{4,8},{8,12},{12,16},{16,20},{20,24},{24,28},{28,32},{32,36}... | collective-permute-start | bytes 24584 | tf_op jit(solution)/shard_map/ppermute | solution.py:15
  267.7 85.7 %all-gather.17.cloned.1.call-start = ((), (), s32[]{:S(2)}) async-start(), calls=%async_computation.5 | async-start | bytes 8650752 | tf_op jit(solution)/shard_map/all_gather | solution.py:42
  269.2 6.2 %collective-permute-start.9 = (bf16[16,1,256]{2,0,1:T(8,128)(2,1)S(1)}, bf16[16,1,256]{2,0,1:T(8,128)(2,1)S(1)}, u32[]{:S(2)}, u32[]{:S(2)}) collective-permute-start(bf16[16,1,256]{2,0,1:T(8,128)(2,1)S(1)} %get-tuple-element.16), channel_id=1, source_target_pairs={{4,0},{8,4},{12,8},{16,12},{20,16},{24,20},{28,24},{32,28},{36,32}... | collective-permute-start | bytes 24584 | tf_op jit(solution)/shard_map/ppermute | solution.py:18
  275.4 22.7 %copy-start.1 = (f32[16,8192]{1,0:T(8,128)S(1)}, f32[16,8192]{1,0:T(8,128)}, u32[]{:S(2)}) copy-start(f32[16,8192]{1,0:T(8,128)} %get-tuple-element.6) | copy-start | bytes 1572868
  275.4 85.3 %copy-start.3 = (bf16[2,32,8,256]{3,2,0,1:T(8,128)(2,1)S(1)}, bf16[2,32,8,256]{3,2,0,1:T(8,128)(2,1)}, u32[]{:S(2)}) copy-start(bf16[2,32,8,256]{3,2,0,1:T(8,128)(2,1)} %copy.154) | copy-start | bytes 786436
  275.4 85.3 %collective-permute-start.8 = (bf16[16,1,256]{2,0,1:T(8,128)(2,1)S(1)}, bf16[16,1,256]{2,0,1:T(8,128)(2,1)S(1)}, u32[]{:S(2)}, u32[]{:S(2)}) collective-permute-start(bf16[16,1,256]{2,0,1:T(8,128)(2,1)S(1)} %get-tuple-element.15), channel_id=1, source_target_pairs={{0,4},{4,8},{8,12},{12,16},{16,20},{20,24},{24,28},{28,32},{32,36}... | collective-permute-start | bytes 24584 | tf_op jit(solution)/shard_map/ppermute | solution.py:15
  360.7 3.6 copy-start
Sparse Core Ops, SparseCore 0:
  10.8 55.4 all-gather.6
  74.7 52.5 all-gather.8
  139.1 52.5 all-gather.10
  203.4 52.5 all-gather.12
  267.8 30.2 all-gather.14
  300.2 53.0 all-gather.16
where the time goes:
time: 540 us; the launch traced here: 539 us
  waiting for transfers between devices  236 us (44%)
  blocking collectives  151 us (28%)
  matrix products  77.1 us (14%)
  local copies, waits for them, and re-layouts  27.9 us (5%)
  starting transfers between devices  17.6 us (3%)
  other arithmetic  14.9 us (3%)
  between operations  14.4 us (3%)
    all_gather x5, waiting for transfers between devices, apply_generator(): piece = lax.all_gather(shaped, 'rows', axis=1, tiled=True)  217 us
    psum x1, blocking collectives, body(): gram_mine = lax.psum(gram_part, 'rows')  127 us
    dot_general x20, matrix products, block_product(): jnp.einsum('jbt,bst->jbs', pieces, blocks[:, position], preferred_element...  69.5 us
    gather x5, local copies, waits for them, and re-layouts, apply_generator(): taken = jnp.take(piece, jnp.clip(far_cols, 0, piece.shape[1] - 1), axis=1)  19.7 us
    all_gather x1, waiting for transfers between devices, body(): whole_iterate = lax.all_gather(iterate, 'cols', axis=0, tiled=True)  18.8 us
    ppermute x5, starting transfers between devices, with_halo(): lax.ppermute(lax.slice_in_dim(block, 0, width, axis=dim), axis, backward)  17.3 us
    all_gather x1, blocking collectives, body(): gram = lax.all_gather(gram_mine, 'cols', axis=1, tiled=True) / total_states  12.4 us
    all_gather x1, blocking collectives, body(): lax.all_gather(product_mine, 'cols', axis=1, tiled=True) / total_states  11.9 us
  transfers between devices with their start and end apart: 16, of which 6 were waited for; matrix products, arithmetic and copies ran while one was open for 14% of the time, Pallas kernels for 0%

commit v1 on v0

v1 whole, which is shorter than its diff:
```python
import functools

import jax
import jax.numpy as jnp
from jax import lax
from jax.experimental import pallas as pl
from jax.experimental.pallas import tpu as pltpu
from jax.sharding import PartitionSpec as P

ITERS = 4
CAP = 2
STEP = 0.2
NT = (((1,), (1,)), ((), ()))
NN = (((1,), (0,)), ((), ()))
BF = jnp.bfloat16
F32 = jnp.float32
VMEM = pl.BlockSpec(memory_space=pltpu.VMEM)
SMEM = pl.BlockSpec(memory_space=pltpu.SMEM)


def dot(a, b, dims):
    return lax.dot_general(a, b, dims, preferred_element_type=F32)


def exchange(x, axes):
    return lax.all_to_all(x, axes, split_axis=0, concat_axis=0, tiled=True)


def local_kernel(group, rows, size, base, x_ref, w_ref, d_ref, p_ref, n_ref, o_ref):
    step = pl.program_id(0)
    steps = rows // group

    def block(index):
        return x_ref[:, pl.ds(pl.multiple_of(index * size, size), size)]

    for r in range(group):
        b = step * group + r
        low = block(jnp.maximum(b - 1, 0))
        if r == 0:
            low = jnp.where(step > 0, low, jnp.zeros_like(low))
        high = block(jnp.minimum(b + 1, rows - 1))
        if r == group - 1:
            high = jnp.where(step < steps - 1, high, jnp.zeros_like(high))
        acc = dot(block(b), d_ref[r, 0], NT)
        acc += dot(low, p_ref[r, 0], NT)
        acc += dot(high, n_ref[r, 0], NT)
        at = pl.ds(r * size, size)
        o_ref[:, at] = w_ref[:, at] + STEP * acc if base else acc


def local_part(x, w, blocks, base):
    width, states = x.shape
    rows, _, size, _ = blocks.shape
    group = 8
    spec = [pl.BlockSpec((group, 1, size, size), lambda i, k=k: (i, k, 0, 0)) for k in range(3)]
    strip = pl.BlockSpec((width, group * size), lambda i: (0, i))
    return pl.pallas_call(
        functools.partial(local_kernel, group, rows, size, base),
        grid=(rows // group,),
        out_shape=jax.ShapeDtypeStruct((width, states), F32),
        in_specs=[pl.BlockSpec((width, states), lambda i: (0, 0)), strip, *spec],
        out_specs=strip,
        compiler_params=pltpu.CompilerParams(vmem_limit_bytes=16 << 20),
        cost_estimate=pl.CostEstimate(
            flops=6 * width * rows * size * size, bytes_accessed=6 * rows * size * size, transcendentals=0
        ),
    )(x, w, blocks, blocks, blocks)


def far_sum(b, rows, loc_ref, recv_ref, low_ref, high_ref, far_ref):
    acc = dot(recv_ref[loc_ref[b]], far_ref[b], NT)
    if b == 0:
        acc += dot(low_ref[...], far_ref[rows], NT)
    if b == rows - 1:
        acc += dot(high_ref[...], far_ref[rows + 1], NT)
    return acc


def pack(want_ref, x_ref, send_ref, size):
    for s in range(send_ref.shape[0]):
        at = pl.multiple_of(want_ref[s] * size, size)
        send_ref[s] = x_ref[:, pl.ds(at, size)]


def far_kernel(rows, size, copies, want_ref, loc_ref, t_ref, recv_ref, low_ref, high_ref, far_ref,
               w_ref, x_ref, send_ref, first_ref, last_ref, *all_ref):
    for b in range(rows):
        acc = far_sum(b, rows, loc_ref, recv_ref, low_ref, high_ref, far_ref)
        at = pl.ds(b * size, size)
        new = t_ref[:, at] + STEP * acc
        w_ref[:, at] = new
        rounded = new.astype(BF)
        x_ref[:, at] = rounded
        for c in range(copies):
            all_ref[0][c, :, at] = rounded
    first_ref[...] = x_ref[:, :size]
    last_ref[...] = x_ref[:, (rows - 1) * size:]
    pack(want_ref, x_ref, send_ref, size)


def far_part(want, loc, t, recv, low, high, far, copies):
    width, states = t.shape
    size = far.shape[1]
    rows = states // size
    shapes = [
        jax.ShapeDtypeStruct((width, states), F32),
        jax.ShapeDtypeStruct((width, states), BF),
        jax.ShapeDtypeStruct(recv.shape, BF),
        jax.ShapeDtypeStruct((width, size), BF),
        jax.ShapeDtypeStruct((width, size), BF),
    ]
    if copies:
        shapes.append(jax.ShapeDtypeStruct((copies, width, states), BF))
    return pl.pallas_call(
        functools.partial(far_kernel, rows, size, copies),
        out_shape=shapes,
        in_specs=[SMEM, SMEM] + [VMEM] * 5,
        out_specs=[VMEM] * len(shapes),
        compiler_params=pltpu.CompilerParams(vmem_limit_bytes=24 << 20),
        cost_estimate=pl.CostEstimate(
            flops=2 * width * rows * size * size, bytes_accessed=2 * rows * size * size, transcendentals=0
        ),
    )(want, loc, t, recv, low, high, far)


def pack_kernel(size, want_ref, x_ref, send_ref):
    pack(want_ref, x_ref, send_ref, size)


def product_kernel(rows, size, copies, loc_ref, t_ref, recv_ref, low_ref, high_ref, far_ref, all_ref, o_ref, z_ref):
    width = t_ref.shape[0]
    modes = all_ref.shape[0] * width
    for b in range(rows):
        acc = far_sum(b, rows, loc_ref, recv_ref, low_ref, high_ref, far_ref)
        at = pl.ds(b * size, size)
        z = t_ref[:, at] + acc
        top = z.astype(BF)
        z_ref[:width, at] = top
        z_ref[width:, at] = (z - top.astype(F32)).astype(BF)
    total = jnp.zeros((2 * width, modes), F32)
    wide = 2048
    for b in range(rows * size // wide):
        at = pl.ds(b * wide, wide)
        total += dot(z_ref[:, at], all_ref[:, :, at].reshape(modes, wide), NT)
    part = total[:width] + total[width:]
    for c in range(copies):
        o_ref[c] = part


def product_part(loc, t, recv, low, high, far, everyone, copies):
    width, states = t.shape
    size = far.shape[1]
    modes = everyone.shape[0] * width
    rows = states // size
    return pl.pallas_call(
        functools.partial(product_kernel, rows, size, copies),
        out_shape=jax.ShapeDtypeStruct((copies, width, modes), F32),
        in_specs=[SMEM] + [VMEM] * 6,
        out_specs=VMEM,
        scratch_shapes=[pltpu.VMEM((2 * width, states), BF)],
        compiler_params=pltpu.CompilerParams(vmem_limit_bytes=24 << 20),
        cost_estimate=pl.CostEstimate(
            flops=2 * width * rows * size * size, bytes_accessed=2 * rows * size * size, transcendentals=0
        ),
    )(loc, t, recv, low, high, far, everyone)


def gram_kernel(copies, all_ref, o_ref):
    groups, width, states = all_ref.shape
    modes = groups * width
    total = jnp.zeros((modes, modes), F32)
    wide = 2048
    for b in range(states // wide):
        w = all_ref[:, :, pl.ds(b * wide, wide)].reshape(modes, wide)
        total += dot(w, w, NT)
    half = modes // 2
    folded = jnp.concatenate([total[:half], total[half:]], axis=1)
    for c in range(copies):
        o_ref[c] = folded


def gram_part(everyone, copies):
    modes = everyone.shape[0] * everyone.shape[1]
    return pl.pallas_call(
        functools.partial(gram_kernel, copies),
        out_shape=jax.ShapeDtypeStruct((copies, modes // 2, 2 * modes), F32),
        in_specs=[VMEM],
        out_specs=VMEM,
        compiler_params=pltpu.CompilerParams(vmem_limit_bytes=16 << 20),
        cost_estimate=pl.CostEstimate(
            flops=2 * modes * modes * everyone.shape[2], bytes_accessed=2 * everyone.size, transcendentals=0
        ),
    )(everyone)


def inverse_factor(gram):
    n = gram.shape[0]
    row_id = lax.broadcasted_iota(jnp.int32, (n, 2 * n), 0)
    lane = lax.broadcasted_iota(jnp.int32, (n, 2 * n), 1)
    unit = jnp.where(lane == row_id + n, 1.0, 0.0)
    work = jnp.concatenate([gram, unit[:, n:]], axis=1)
    column_id = lax.broadcasted_iota(jnp.int32, (n, 1), 0)
    roots = jnp.zeros((n, 1), F32)
    for j in range(n):
        row = work[j:j + 1]
        pivot = row[:, j:j + 1]
        column = work[:, j:j + 1]
        roots = jnp.where(column_id == j, pivot, roots)
        factor = jnp.where(column_id > j, column / pivot, 0.0)
        work = work - factor * row
    return work[:, n:] * lax.rsqrt(roots)


def finish_kernel(scale, own_ref, parts_ref, all_ref, w_ref, out_ref, inv_ref):
    groups, width, states = all_ref.shape
    modes = groups * width
    total = jnp.sum(parts_ref[...], axis=0) * scale
    gram = jnp.concatenate([total[:, :modes], total[:, modes:]], axis=0)
    inverse = inverse_factor(gram)
    inv_ref[...] = inverse
    start = pl.multiple_of(own_ref[0] * width, width)
    mine = inv_ref[pl.ds(start, width)]
    place = lax.broadcasted_iota(jnp.int32, (modes, width), 0) - lax.broadcasted_iota(jnp.int32, (modes, width), 1)
    pick = jnp.where(place == start, 1.0, 0.0)
    within = lax.dot_general(mine, pick, NN, precision=lax.Precision.HIGHEST, preferred_element_type=F32)
    top = mine.astype(BF)
    rest = (mine - top.astype(F32)).astype(BF)
    left = jnp.concatenate([top, rest], axis=1)
    small = within.astype(BF)
    wide = 1024
    for b in range(states // wide):
        at = pl.ds(b * wide, wide)
        w = all_ref[:, :, at].reshape(modes, wide)
        own = w_ref[:, at]
        low = (own - own.astype(BF).astype(F32)).astype(BF)
        acc = dot(left, jnp.concatenate([w, w], axis=0), NN)
        out_ref[:, at] = acc + dot(small, low, NN)


def finish(own, parts, everyone, w, scale):
    width, states = w.shape
    modes = everyone.shape[0] * width
    return pl.pallas_call(
        functools.partial(finish_kernel, scale),
        out_shape=[jax.ShapeDtypeStruct((width, states), F32), jax.ShapeDtypeStruct((modes, modes), F32)],
        in_specs=[SMEM] + [VMEM] * 3,
        out_specs=[VMEM] * 2,
        compiler_params=pltpu.CompilerParams(vmem_limit_bytes=24 << 20),
        cost_estimate=pl.CostEstimate(flops=1 << 30, bytes_accessed=16 << 20, transcendentals=0),
    )(own, parts, everyone, w)


def ritz_kernel(groups, scale, parts_ref, inv_ref, mine_ref, o_ref):
    copies, width, modes = parts_ref.shape
    parts = parts_ref[...].reshape(copies // groups, modes, modes)
    turned = jnp.sum(parts, axis=0) * scale
    highest = lax.Precision.HIGHEST
    inverse = inv_ref[...]
    half = lax.dot_general(inverse, turned, NT, precision=highest, preferred_element_type=F32)
    o_ref[...] = lax.dot_general(half, mine_ref[...], NT, precision=highest, preferred_element_type=F32)


def body(basis, blocks, far_cols):
    width, states = basis.shape
    rows, _, size, _ = blocks.shape
    devices = lax.axis_size("rows")
    groups = lax.axis_size("cols")
    scale = 1.0 / (states * devices)
    both = ("rows", "cols")

    owner = far_cols // rows
    inside = far_cols % rows
    match = owner[None, :] == jnp.arange(devices, dtype=jnp.int32)[:, None]
    first = jnp.min(jnp.where(match, inside[None, :], rows - 1), axis=1)
    second = jnp.max(jnp.where(match, inside[None, :], 0), axis=1)
    lane = jnp.arange(128, dtype=jnp.int32)[None, None, :]
    asked = jnp.where(lane == 0, first[:, None, None], second[:, None, None])
    answer = exchange(asked, "rows")
    want = jnp.clip(answer[:, 0, :CAP].reshape(devices * CAP), 0, rows - 1)
    earlier = jnp.logical_and(owner[None, :] == owner[:, None], inside[None, :] < inside[:, None])
    loc = owner * CAP + jnp.any(earlier, axis=1).astype(jnp.int32)
    loc = jnp.clip(loc, 0, devices * CAP - 1)

    far = jnp.concatenate([blocks[:, 3], blocks[:1, 1], blocks[-1:, 2]], axis=0)
    up = [(i, (i + 1) % devices) for i in range(devices)]
    down = [(target, source) for source, target in up]

    w = basis
    x = w.astype(BF)
    send = pl.pallas_call(
        functools.partial(pack_kernel, size),
        out_shape=jax.ShapeDtypeStruct((devices * CAP, width, size), BF),
        in_specs=[SMEM, VMEM],
        out_specs=VMEM,
    )(want, x)
    edge_first, edge_last = x[:, :size], x[:, states - size:]
    everyone = None
    for step in range(ITERS):
        recv = exchange(send, "rows")
        low = lax.ppermute(edge_last, "rows", up)
        high = lax.ppermute(edge_first, "rows", down)
        t = local_part(x, w, blocks, True)
        made = far_part(want, loc, t, recv, low, high, far, groups if step == ITERS - 1 else 0)
        w, x, send, edge_first, edge_last = made[:5]
        if step == ITERS - 1:
            everyone = exchange(made[5], "cols")
    recv = exchange(send, "rows")
    low = lax.ppermute(edge_last, "rows", up)
    high = lax.ppermute(edge_first, "rows", down)
    t = local_part(x, w, blocks, False)
    gram_parts = exchange(gram_part(everyone, devices), "rows")
    parts = product_part(loc, t, recv, low, high, far, everyone, devices * groups)
    parts = exchange(parts, both)
    own = lax.axis_index("cols")
    basis_out, inverse = finish(own.reshape(1), gram_parts, everyone, w, scale)
    mine = lax.dynamic_slice_in_dim(inverse, own * width, width, 0)
    modes = groups * width
    ritz = pl.pallas_call(
        functools.partial(ritz_kernel, groups, scale),
        out_shape=jax.ShapeDtypeStruct((modes, width), F32),
        in_specs=[VMEM] * 3,
        out_specs=VMEM,
    )(parts, inverse, mine)
    return (basis_out, ritz)


def solution(mesh):
    in_specs = (P("cols", "rows"), P("rows", None, None, None), P("rows"))
    out_specs = (P("cols", "rows"), P(None, "cols"))
    return jax.shard_map(body, mesh=mesh, in_specs=in_specs, out_specs=out_specs, check_vma=False)
```

time: 540 us -> 213 us (0.39)
  waiting for transfers between devices: 236 us -> 14.8 us
  blocking collectives: 151 us -> 16 us
  matrix products: 77.1 us -> 0 us
  starting transfers between devices: 17.6 us -> 70.2 us
  Pallas kernels: 0 us -> 50 us
  local copies, waits for them, and re-layouts: 27.9 us -> 49.4 us
  between operations: 14.4 us -> 0.99 us
  other arithmetic: 14.9 us -> 8.77 us
    all_gather x6 -> x0, waiting for transfers between devices: 236 us -> none  [the longest x5 217 us: apply_generator(): piece = lax.all_gather(shaped, 'rows', axis=1, tiled=True)]
    psum x1 -> x0, blocking collectives: 127 us -> none  [body(): gram_mine = lax.psum(gram_part, 'rows')]
    dot_general x25 -> x0, matrix products: 76.9 us -> none  [the longest x20 69.5 us: block_product(): jnp.einsum('jbt,bst->jbs', pieces, blocks[:, position], preferred_element...]
    pallas_call x0 -> x14, Pallas kernels: none -> 50 us  [the longest x5 23.1 us: local_part(): pl.pallas_call(functools.partial(local_kernel, group, rows, size, base),...]
    all_to_all x0 -> x8, starting transfers between devices: none -> 44.4 us  [exchange(): return lax.all_to_all(x, axes, split_axis=0, concat_axis=0, tiled=True)]
    unnamed x16 -> x35, local copies, waits for them, and re-layouts: 0.07 us -> 42 us
    all_gather x2 -> x0, blocking collectives: 24.3 us -> none  [the longest x1 12.4 us: body(): gram = lax.all_gather(gram_mine, 'cols', axis=1, tiled=True) / total_states]
    gather x5 -> x0, local copies, waits for them, and re-layouts: 19.7 us -> none  [apply_generator(): taken = jnp.take(piece, jnp.clip(far_cols, 0, piece.shape[1] - 1), axis=1)]
  transfers between devices with their start and end apart: 16 -> 18, of which waited for: 6 -> 2; matrix products, arithmetic and copies ran while one was open for 14% -> 7% of each run, Pallas kernels for 0% -> 18%
where the time goes in v1:
time: 213 us; the launch traced here: 210 us
  starting transfers between devices  70.2 us (33%)
  Pallas kernels  50 us (23%)
  local copies, waits for them, and re-layouts  49.4 us (23%)
  blocking collectives  16 us (8%)
  waiting for transfers between devices  14.8 us (7%)
  other arithmetic  8.77 us (4%)
    all_to_all x8, starting transfers between devices, exchange(): return lax.all_to_all(x, axes, split_axis=0, concat_axis=0, tiled=True)  44.4 us
    unnamed x35, local copies, waits for them, and re-layouts  42 us
    ppermute x5, starting transfers between devices, body(): high = lax.ppermute(edge_first, 'rows', down)  24.3 us
    pallas_call x5, Pallas kernels, local_part(): pl.pallas_call(functools.partial(local_kernel, group, rows, size, base),...  23.1 us
    all_to_all x1, blocking collectives, exchange(): return lax.all_to_all(x, axes, split_axis=0, concat_axis=0, tiled=True)  16 us
    all_to_all x8, waiting for transfers between devices, exchange(): return lax.all_to_all(x, axes, split_axis=0, concat_axis=0, tiled=True)  14.7 us
    pallas_call x4, Pallas kernels, far_part(): pl.pallas_call(functools.partial(far_kernel, rows, size, copies), out_sha...  10.8 us
    pallas_call x1, Pallas kernels, finish(): pl.pallas_call(functools.partial(finish_kernel, scale), out_shape=[jax.Sh...  8.43 us
  transfers between devices with their start and end apart: 18, of which 2 were waited for; matrix products, arithmetic and copies ran while one was open for 7% of the time, Pallas kernels for 18%

profile of v1, /device:TPU:0, one launch (start us, length us, event | category | flops | bytes accessed | tf_op | source)
XLA Modules:
  0.0 210.2 jit_solution(7769035821065132382)
XLA Ops:
  2.2 8.4 %all-to-all-start = ((s32[32,1,128]{2,1,0:T(1,128)}), s32[32,1,128]{2,1,0:T(1,128)S(1)}, u32[]{:S(2)}, u32[]{:S(2)}) async-start(s32[32,1,128]{2,1,0:T(1,128)} %broadcast_select_fusion), calls=%async_computation | async-start | bytes 32768 | tf_op jit(solution)/shard_map/all_to_all | solution.py:26
  12.0 4.8 %collective-permute-start.1 = (bf16[16,256]{1,0:T(8,128)(2,1)S(1)}, bf16[16,256]{1,0:T(8,128)(2,1)S(1)}, u32[]{:S(2)}, u32[]{:S(2)}) collective-permute-start(bf16[16,256]{1,0:T(8,128)(2,1)S(1)} %get-tuple-element.60), channel_id=1, source_target_pairs={{4,0},{8,4},{12,8},{16,12},{20,16},{24,20},{28,24},{32,28},{36,32}... | collective-permute-start | bytes 24584 | tf_op jit(solution)/shard_map/ppermute | solution.py:301
  17.8 4.7 %slice_bitcast_fusion = bf16[32,256,256]{2,1,0:T(8,128)(2,1)} fusion(bf16[32,4,256,256]{3,2,1,0:T(8,128)(2,1)} %n_ref.9), kind=kLoop, calls=%fused_computation.1 | loop fusion | bytes 8388608 | tf_op jit(solution)/shard_map/squeeze | solution.py:284
  25.2 4.1 %all-to-all-start.1 = ((bf16[64,16,256]{2,1,0:T(8,128)(2,1)}), bf16[64,16,256]{2,1,0:T(8,128)(2,1)S(1)}, u32[]{:S(2)}, u32[]{:S(2)}) async-start(bf16[64,16,256]{2,1,0:T(8,128)(2,1)} %shard_map.51), calls=%async_computation.1 | async-start | bytes 1048576 | tf_op jit(solution)/shard_map/all_to_all | solution.py:26
  29.3 4.1 %pad_maximum_fusion.far_ref = bf16[34,256,256]{2,1,0:T(8,128)(2,1)} fusion(bf16[1,256,256]{2,1,0:T(8,128)(2,1)S(1)} %get-tuple-element.59, bf16[1,256,256]{2,1,0:T(8,128)(2,1)S(1)} %get-tuple-element.58, bf16[32,256,256]{2,1,0:T(8,128)(2,1)} %slice_bitcast_fusion), kind=kLoop, calls=%fused_computation | loop fusion | flops 4456448 | bytes 8912896 | tf_op jit(solution)/shard_map/concatenate | solution.py:284
  33.4 5.8 %copy-done = bf16[32,4,256,256]{3,2,1,0:T(8,128)(2,1)S(1)} copy-done((bf16[32,4,256,256]{3,2,1,0:T(8,128)(2,1)S(1)}, bf16[32,4,256,256]{3,2,1,0:T(8,128)(2,1)}, u32[]{:S(2)}) %copy-start) | copy-done | bytes 16777240
  39.2 4.6 %shard_map.50.t_ref = f32[16,8192]{1,0:T(8,128)S(1)} custom-call(bf16[16,8192]{1,0:T(8,128)(2,1)S(1)} %copy-done.10, f32[16,8192]{1,0:T(8,128)S(1)} %copy-done.11, bf16[32,4,256,256]{3,2,1,0:T(8,128)(2,1)S(1)} %copy-done, bf16[32,4,256,256]{3,2,1,0:T(8,128)(2,1)S(1)} %copy-done, bf16[32,4,256,256]{3,2,1,0:T(8,128)(2,1)S(1)} %copy-done), custom_call_target="tpu_custom_call" | custom-call | flops 201326592 | bytes 12582912 | tf_op jit(solution)/shard_map/pallas_call | solution.py:57
  48.8 7.4 %all-to-all-start.2 = ((bf16[64,16,256]{2,1,0:T(8,128)(2,1)}), bf16[64,16,256]{2,1,0:T(8,128)(2,1)S(1)}, u32[]{:S(2)}, u32[]{:S(2)}) async-start(bf16[64,16,256]{2,1,0:T(8,128)(2,1)} %get-tuple-element.27), calls=%async_computation.2 | async-start | bytes 1048576 | tf_op jit(solution)/shard_map/all_to_all | solution.py:26
  56.5 4.8 %collective-permute-start.3 = (bf16[16,256]{1,0:T(8,128)(2,1)S(1)}, bf16[16,256]{1,0:T(8,128)(2,1)S(1)}, u32[]{:S(2)}, u32[]{:S(2)}) collective-permute-start(bf16[16,256]{1,0:T(8,128)(2,1)S(1)} %get-tuple-element.29), channel_id=1, source_target_pairs={{4,0},{8,4},{12,8},{16,12},{20,16},{24,20},{28,24},{32,28},{36,32}... | collective-permute-start | bytes 24584 | tf_op jit(solution)/shard_map/ppermute | solution.py:301
  61.3 5.8 %copy-done.1 = bf16[32,4,256,256]{3,2,1,0:T(8,128)(2,1)S(1)} copy-done((bf16[32,4,256,256]{3,2,1,0:T(8,128)(2,1)S(1)}, bf16[32,4,256,256]{3,2,1,0:T(8,128)(2,1)}, u32[]{:S(2)}) %copy-start.1) | copy-done | bytes 16777240
  67.1 4.6 %shard_map.53.t_ref = f32[16,8192]{1,0:T(8,128)S(1)} custom-call(bf16[16,8192]{1,0:T(8,128)(2,1)S(1)} %get-tuple-element.25.x_ref, f32[16,8192]{1,0:T(8,128)S(1)} %get-tuple-element.26.w_ref, bf16[32,4,256,256]{3,2,1,0:T(8,128)(2,1)S(1)} %copy-done.1, bf16[32,4,256,256]{3,2,1,0:T(8,128)(2,1)S(1)} %copy-done.1, bf16[32,4,256,256]{3,2,1,0:T(8,128)(2,1)S(1)} %copy-done.1), custom_call_target="tpu_custom_call" | custom-call | flops 201326592 | bytes 12582912 | tf_op jit(solution)/shard_map/pallas_call | solution.py:57
  74.0 2.7 %shard_map.54 = (f32[16,8192]{1,0:T(8,128)S(1)}, bf16[16,8192]{1,0:T(8,128)(2,1)S(1)}, bf16[64,16,256]{2,1,0:T(8,128)(2,1)}, bf16[16,256]{1,0:T(8,128)(2,1)S(1)}, bf16[16,256]{1,0:T(8,128)(2,1)S(1)}) custom-call(s32[64]{0:T(128)S(1)} %copy-done.13, s32[32]{0:T(128)S(1)} %add_clamp_fusion.loc_ref, f32[16,8192]{1,0:T(8,128)S(1)} %shard_map.53.t_ref, ...), custom_call_target="tpu_custom_call" | custom-call | flops 67108864 | bytes 4194304 | tf_op jit(solution)/shard_map/pallas_call | solution.py:114
  76.7 4.1 %all-to-all-start.3 = ((bf16[64,16,256]{2,1,0:T(8,128)(2,1)}), bf16[64,16,256]{2,1,0:T(8,128)(2,1)S(1)}, u32[]{:S(2)}, u32[]{:S(2)}) async-start(bf16[64,16,256]{2,1,0:T(8,128)(2,1)} %get-tuple-element.32), calls=%async_computation.3 | async-start | bytes 1048576 | tf_op jit(solution)/shard_map/all_to_all | solution.py:26
  81.1 4.8 %collective-permute-start.5 = (bf16[16,256]{1,0:T(8,128)(2,1)S(1)}, bf16[16,256]{1,0:T(8,128)(2,1)S(1)}, u32[]{:S(2)}, u32[]{:S(2)}) collective-permute-start(bf16[16,256]{1,0:T(8,128)(2,1)S(1)} %get-tuple-element.34), channel_id=1, source_target_pairs={{4,0},{8,4},{12,8},{16,12},{20,16},{24,20},{28,24},{32,28},{36,32}... | collective-permute-start | bytes 24584 | tf_op jit(solution)/shard_map/ppermute | solution.py:301
  85.9 5.8 %copy-done.2 = bf16[32,4,256,256]{3,2,1,0:T(8,128)(2,1)S(1)} copy-done((bf16[32,4,256,256]{3,2,1,0:T(8,128)(2,1)S(1)}, bf16[32,4,256,256]{3,2,1,0:T(8,128)(2,1)}, u32[]{:S(2)}) %copy-start.2) | copy-done | bytes 16777240
  91.7 4.6 %shard_map.55.t_ref = f32[16,8192]{1,0:T(8,128)S(1)} custom-call(bf16[16,8192]{1,0:T(8,128)(2,1)S(1)} %get-tuple-element.30.x_ref, f32[16,8192]{1,0:T(8,128)S(1)} %get-tuple-element.31.w_ref, bf16[32,4,256,256]{3,2,1,0:T(8,128)(2,1)S(1)} %copy-done.2, bf16[32,4,256,256]{3,2,1,0:T(8,128)(2,1)S(1)} %copy-done.2, bf16[32,4,256,256]{3,2,1,0:T(8,128)(2,1)S(1)} %copy-done.2), custom_call_target="tpu_custom_call" | custom-call | flops 201326592 | bytes 12582912 | tf_op jit(solution)/shard_map/pallas_call | solution.py:57
  98.6 2.7 %shard_map.56 = (f32[16,8192]{1,0:T(8,128)S(1)}, bf16[16,8192]{1,0:T(8,128)(2,1)S(1)}, bf16[64,16,256]{2,1,0:T(8,128)(2,1)}, bf16[16,256]{1,0:T(8,128)(2,1)S(1)}, bf16[16,256]{1,0:T(8,128)(2,1)S(1)}) custom-call(s32[64]{0:T(128)S(1)} %copy-done.13, s32[32]{0:T(128)S(1)} %add_clamp_fusion.loc_ref, f32[16,8192]{1,0:T(8,128)S(1)} %shard_map.55.t_ref, ...), custom_call_target="tpu_custom_call" | custom-call | flops 67108864 | bytes 4194304 | tf_op jit(solution)/shard_map/pallas_call | solution.py:114
  101.3 4.1 %all-to-all-start.4 = ((bf16[64,16,256]{2,1,0:T(8,128)(2,1)}), bf16[64,16,256]{2,1,0:T(8,128)(2,1)S(1)}, u32[]{:S(2)}, u32[]{:S(2)}) async-start(bf16[64,16,256]{2,1,0:T(8,128)(2,1)} %get-tuple-element.37), calls=%async_computation.4 | async-start | bytes 1048576 | tf_op jit(solution)/shard_map/all_to_all | solution.py:26
  105.7 4.9 %collective-permute-start.7 = (bf16[16,256]{1,0:T(8,128)(2,1)S(1)}, bf16[16,256]{1,0:T(8,128)(2,1)S(1)}, u32[]{:S(2)}, u32[]{:S(2)}) collective-permute-start(bf16[16,256]{1,0:T(8,128)(2,1)S(1)} %get-tuple-element.39), channel_id=1, source_target_pairs={{4,0},{8,4},{12,8},{16,12},{20,16},{24,20},{28,24},{32,28},{36,32}... | collective-permute-start | bytes 24584 | tf_op jit(solution)/shard_map/ppermute | solution.py:301
  110.7 5.8 %copy-done.3 = bf16[32,4,256,256]{3,2,1,0:T(8,128)(2,1)S(1)} copy-done((bf16[32,4,256,256]{3,2,1,0:T(8,128)(2,1)S(1)}, bf16[32,4,256,256]{3,2,1,0:T(8,128)(2,1)}, u32[]{:S(2)}) %copy-start.3) | copy-done | bytes 16777240
  116.4 4.6 %shard_map.57.t_ref = f32[16,8192]{1,0:T(8,128)S(1)} custom-call(bf16[16,8192]{1,0:T(8,128)(2,1)S(1)} %get-tuple-element.35.x_ref, f32[16,8192]{1,0:T(8,128)S(1)} %get-tuple-element.36.w_ref, bf16[32,4,256,256]{3,2,1,0:T(8,128)(2,1)S(1)} %copy-done.3, bf16[32,4,256,256]{3,2,1,0:T(8,128)(2,1)S(1)} %copy-done.3, bf16[32,4,256,256]{3,2,1,0:T(8,128)(2,1)S(1)} %copy-done.3), custom_call_target="tpu_custom_call" | custom-call | flops 201326592 | bytes 12582912 | tf_op jit(solution)/shard_map/pallas_call | solution.py:57
  123.4 2.7 %shard_map.58 = (f32[16,8192]{1,0:T(8,128)S(1)}, bf16[16,8192]{1,0:T(8,128)(2,1)S(1)}, bf16[64,16,256]{2,1,0:T(8,128)(2,1)}, bf16[16,256]{1,0:T(8,128)(2,1)S(1)}...) custom-call(s32[64]{0:T(128)S(1)} %copy-done.13, s32[32]{0:T(128)S(1)} %add_clamp_fusion.loc_ref, ...), custom_call_target="tpu_custom_call" | custom-call | flops 67108864 | bytes 4194304 | tf_op jit(solution)/shard_map/pallas_call | solution.py:114
  126.1 16.0 %all_to_all.45.all_ref = bf16[4,16,8192]{2,1,0:T(8,128)(2,1)S(1)} all-to-all(bf16[4,16,8192]{2,1,0:T(8,128)(2,1)S(1)} %get-tuple-element.40), channel_id=1, replica_groups=mesh['rows'=32,'cols'=4] {'cols'}, dimensions={0} | all-to-all | bytes 2097152 | tf_op jit(solution)/shard_map/all_to_all | solution.py:26
  142.1 6.9 %all-to-all-start.7 = ((bf16[64,16,256]{2,1,0:T(8,128)(2,1)}), bf16[64,16,256]{2,1,0:T(8,128)(2,1)S(1)}, u32[]{:S(2)}, u32[]{:S(2)}) async-start(bf16[64,16,256]{2,1,0:T(8,128)(2,1)} %get-tuple-element.44), calls=%async_computation.7 | async-start | bytes 1048576 | tf_op jit(solution)/shard_map/all_to_all | solution.py:26
  150.4 10.4 %all-to-all-done.7.recv_ref = bf16[64,16,256]{2,1,0:T(8,128)(2,1)S(1)} async-done(((bf16[64,16,256]{2,1,0:T(8,128)(2,1)}), bf16[64,16,256]{2,1,0:T(8,128)(2,1)S(1)}, u32[]{:S(2)}, u32[]{:S(2)}) %all-to-all-start.7) | async-done | bytes 524320 | tf_op jit(solution)/shard_map/all_to_all | solution.py:26
  160.8 4.6 %all-to-all-start.6 = ((f32[32,32,128]{2,1,0:T(8,128)}), f32[32,32,128]{2,1,0:T(8,128)}, u32[]{:S(2)}, u32[]{:S(2)}) async-start(f32[32,32,128]{2,1,0:T(8,128)} %shard_map.59), calls=%async_computation.6 | async-start | bytes 1048576 | tf_op jit(solution)/shard_map/all_to_all | solution.py:26
  165.6 5.0 %collective-permute-start.9 = (bf16[16,256]{1,0:T(8,128)(2,1)S(1)}, bf16[16,256]{1,0:T(8,128)(2,1)S(1)}, u32[]{:S(2)}, u32[]{:S(2)}) collective-permute-start(bf16[16,256]{1,0:T(8,128)(2,1)S(1)} %get-tuple-element.46), channel_id=1, source_target_pairs={{4,0},{8,4},{12,8},{16,12},{20,16},{24,20},{28,24},{32,28},{36,32}... | collective-permute-start | bytes 24584 | tf_op jit(solution)/shard_map/ppermute | solution.py:309
  170.5 5.8 %copy-done.4 = bf16[32,4,256,256]{3,2,1,0:T(8,128)(2,1)S(1)} copy-done((bf16[32,4,256,256]{3,2,1,0:T(8,128)(2,1)S(1)}, bf16[32,4,256,256]{3,2,1,0:T(8,128)(2,1)}, u32[]{:S(2)}) %copy-start.4) | copy-done | bytes 16777240
  176.3 4.6 %shard_map.61.t_ref = f32[16,8192]{1,0:T(8,128)S(1)} custom-call(bf16[16,8192]{1,0:T(8,128)(2,1)S(1)} %get-tuple-element.43.x_ref, f32[16,8192]{1,0:T(8,128)S(1)} %get-tuple-element.41.w_ref, bf16[32,4,256,256]{3,2,1,0:T(8,128)(2,1)S(1)} %copy-done.4, bf16[32,4,256,256]{3,2,1,0:T(8,128)(2,1)S(1)} %copy-done.4, bf16[32,4,256,256]{3,2,1,0:T(8,128)(2,1)S(1)} %copy-done.4), custom_call_target="tpu_custom_call" | custom-call | flops 201326592 | bytes 12582912 | tf_op jit(solution)/shard_map/pallas_call | solution.py:57
  184.7 4.9 %all-to-all-start.8 = ((f32[128,1,1024]{2,1,0:T(1,128)}), f32[128,1,1024]{2,1,0:T(1,128)S(1)}, u32[]{:S(2)}, u32[]{:S(2)}) async-start(f32[128,1,1024]{2,1,0:T(1,128)} %reshape.92), calls=%async_computation.8 | async-start | bytes 1048576 | tf_op jit(solution)/shard_map/all_to_all | solution.py:26
  189.6 8.4 %shard_map.60 = (f32[16,8192]{1,0:T(8,128)}, f32[64,64]{1,0:T(8,128)S(1)}) custom-call(s32[1]{0:T(128)} %bitcast.own_ref, f32[32,32,128]{2,1,0:T(8,128)} %all-to-all-done.6.parts_ref, bf16[4,16,8192]{2,1,0:T(8,128)(2,1)S(1)} %all_to_all.45.all_ref, f32[16,8192]{1,0:T(8,128)S(1)} %get-tuple-element.41.w_ref), custom_call_target="tpu_custom_call" | custom-call | flops 1073741824 | bytes 16777216 | tf_op jit(solution)/shard_map/pallas_call | solution.py:243
  198.6 4.3 %all-to-all-done.8 = f32[128,1,1024]{2,1,0:T(1,128)S(1)} async-done(((f32[128,1,1024]{2,1,0:T(1,128)}), f32[128,1,1024]{2,1,0:T(1,128)S(1)}, u32[]{:S(2)}, u32[]{:S(2)}) %all-to-all-start.8) | async-done | bytes 524320 | tf_op jit(solution)/shard_map/all_to_all | solution.py:26
  (71 shorter events, 32.6 us)
Async XLA Ops:
  2.2 20.5 %all-to-all-start = ((s32[32,1,128]{2,1,0:T(1,128)}), s32[32,1,128]{2,1,0:T(1,128)S(1)}, u32[]{:S(2)}, u32[]{:S(2)}) async-start(s32[32,1,128]{2,1,0:T(1,128)} %broadcast_select_fusion), calls=%async_computation | async-start | bytes 32768 | tf_op jit(solution)/shard_map/all_to_all | solution.py:26
  11.7 10.8 %copy-start.9 = (bf16[16,8192]{1,0:T(8,128)(2,1)}, bf16[16,8192]{1,0:T(8,128)(2,1)S(1)}, u32[]{:S(2)}) copy-start(bf16[16,8192]{1,0:T(8,128)(2,1)S(1)} %convert_element_type.7.x_ref) | copy-start | bytes 786436
  11.7 32.1 %collective-permute-start = (bf16[16,256]{1,0:T(8,128)(2,1)S(1)}, bf16[16,256]{1,0:T(8,128)(2,1)S(1)}, u32[]{:S(2)}, u32[]{:S(2)}) collective-permute-start(bf16[16,256]{1,0:T(8,128)(2,1)S(1)} %get-tuple-element.61), channel_id=1, source_target_pairs={{0,4},{4,8},{8,12},{12,16},{16,20},{20,24},{24,28},{28,32},{32,36}... | collective-permute-start | bytes 24584 | tf_op jit(solution)/shard_map/ppermute | solution.py:300
  12.0 31.8 %collective-permute-start.1 = (bf16[16,256]{1,0:T(8,128)(2,1)S(1)}, bf16[16,256]{1,0:T(8,128)(2,1)S(1)}, u32[]{:S(2)}, u32[]{:S(2)}) collective-permute-start(bf16[16,256]{1,0:T(8,128)(2,1)S(1)} %get-tuple-element.60), channel_id=1, source_target_pairs={{4,0},{8,4},{12,8},{16,12},{20,16},{24,20},{28,24},{32,28},{36,32}... | collective-permute-start | bytes 24584 | tf_op jit(solution)/shard_map/ppermute | solution.py:301
  25.2 18.7 %all-to-all-start.1 = ((bf16[64,16,256]{2,1,0:T(8,128)(2,1)}), bf16[64,16,256]{2,1,0:T(8,128)(2,1)S(1)}, u32[]{:S(2)}, u32[]{:S(2)}) async-start(bf16[64,16,256]{2,1,0:T(8,128)(2,1)} %shard_map.51), calls=%async_computation.1 | async-start | bytes 1048576 | tf_op jit(solution)/shard_map/all_to_all | solution.py:26
  29.3 4.1 %copy-start.10 = (bf16[16,8192]{1,0:T(8,128)(2,1)S(1)}, bf16[16,8192]{1,0:T(8,128)(2,1)}, u32[]{:S(2)}) copy-start(bf16[16,8192]{1,0:T(8,128)(2,1)} %copy-done.9) | copy-start | bytes 786436
  29.3 4.1 %copy-start.11 = (f32[16,8192]{1,0:T(8,128)S(1)}, f32[16,8192]{1,0:T(8,128)}, u32[]{:S(2)}) copy-start(f32[16,8192]{1,0:T(8,128)} %w_ref.1) | copy-start | bytes 1572868
  33.4 5.8 %copy-start = (bf16[32,4,256,256]{3,2,1,0:T(8,128)(2,1)S(1)}, bf16[32,4,256,256]{3,2,1,0:T(8,128)(2,1)}, u32[]{:S(2)}) copy-start(bf16[32,4,256,256]{3,2,1,0:T(8,128)(2,1)} %n_ref.9) | copy-start | bytes 50331652
  39.2 4.7 %copy-start.13 = (s32[64]{0:T(128)S(1)}, s32[64]{0:T(128)}, u32[]{:S(2)}) copy-start(s32[64]{0:T(128)} %min.20.want_ref) | copy-start | bytes 772
  48.8 23.0 %all-to-all-start.2 = ((bf16[64,16,256]{2,1,0:T(8,128)(2,1)}), bf16[64,16,256]{2,1,0:T(8,128)(2,1)S(1)}, u32[]{:S(2)}, u32[]{:S(2)}) async-start(bf16[64,16,256]{2,1,0:T(8,128)(2,1)} %get-tuple-element.27), calls=%async_computation.2 | async-start | bytes 1048576 | tf_op jit(solution)/shard_map/all_to_all | solution.py:26
  56.2 15.5 %collective-permute-start.2 = (bf16[16,256]{1,0:T(8,128)(2,1)S(1)}, bf16[16,256]{1,0:T(8,128)(2,1)S(1)}, u32[]{:S(2)}, u32[]{:S(2)}) collective-permute-start(bf16[16,256]{1,0:T(8,128)(2,1)S(1)} %get-tuple-element.28), channel_id=1, source_target_pairs={{0,4},{4,8},{8,12},{12,16},{16,20},{20,24},{24,28},{28,32},{32,36}... | collective-permute-start | bytes 24584 | tf_op jit(solution)/shard_map/ppermute | solution.py:300
  56.5 15.2 %collective-permute-start.3 = (bf16[16,256]{1,0:T(8,128)(2,1)S(1)}, bf16[16,256]{1,0:T(8,128)(2,1)S(1)}, u32[]{:S(2)}, u32[]{:S(2)}) collective-permute-start(bf16[16,256]{1,0:T(8,128)(2,1)S(1)} %get-tuple-element.29), channel_id=1, source_target_pairs={{4,0},{8,4},{12,8},{16,12},{20,16},{24,20},{28,24},{32,28},{36,32}... | collective-permute-start | bytes 24584 | tf_op jit(solution)/shard_map/ppermute | solution.py:301
  61.3 5.8 %copy-start.1 = (bf16[32,4,256,256]{3,2,1,0:T(8,128)(2,1)S(1)}, bf16[32,4,256,256]{3,2,1,0:T(8,128)(2,1)}, u32[]{:S(2)}) copy-start(bf16[32,4,256,256]{3,2,1,0:T(8,128)(2,1)} %n_ref.9) | copy-start | bytes 50331652
  71.8 2.3 %copy-start.6 = (bf16[34,256,256]{2,1,0:T(8,128)(2,1)S(1)}, bf16[34,256,256]{2,1,0:T(8,128)(2,1)}, u32[]{:S(2)}) copy-start(bf16[34,256,256]{2,1,0:T(8,128)(2,1)} %pad_maximum_fusion.far_ref) | copy-start | bytes 13369348
  76.7 19.6 %all-to-all-start.3 = ((bf16[64,16,256]{2,1,0:T(8,128)(2,1)}), bf16[64,16,256]{2,1,0:T(8,128)(2,1)S(1)}, u32[]{:S(2)}, u32[]{:S(2)}) async-start(bf16[64,16,256]{2,1,0:T(8,128)(2,1)} %get-tuple-element.32), calls=%async_computation.3 | async-start | bytes 1048576 | tf_op jit(solution)/shard_map/all_to_all | solution.py:26
  80.8 15.5 %collective-permute-start.4 = (bf16[16,256]{1,0:T(8,128)(2,1)S(1)}, bf16[16,256]{1,0:T(8,128)(2,1)S(1)}, u32[]{:S(2)}, u32[]{:S(2)}) collective-permute-start(bf16[16,256]{1,0:T(8,128)(2,1)S(1)} %get-tuple-element.33), channel_id=1, source_target_pairs={{0,4},{4,8},{8,12},{12,16},{16,20},{20,24},{24,28},{28,32},{32,36}... | collective-permute-start | bytes 24584 | tf_op jit(solution)/shard_map/ppermute | solution.py:300
  81.1 15.2 %collective-permute-start.5 = (bf16[16,256]{1,0:T(8,128)(2,1)S(1)}, bf16[16,256]{1,0:T(8,128)(2,1)S(1)}, u32[]{:S(2)}, u32[]{:S(2)}) collective-permute-start(bf16[16,256]{1,0:T(8,128)(2,1)S(1)} %get-tuple-element.34), channel_id=1, source_target_pairs={{4,0},{8,4},{12,8},{16,12},{20,16},{24,20},{28,24},{32,28},{36,32}... | collective-permute-start | bytes 24584 | tf_op jit(solution)/shard_map/ppermute | solution.py:301
  85.9 5.8 %copy-start.2 = (bf16[32,4,256,256]{3,2,1,0:T(8,128)(2,1)S(1)}, bf16[32,4,256,256]{3,2,1,0:T(8,128)(2,1)}, u32[]{:S(2)}) copy-start(bf16[32,4,256,256]{3,2,1,0:T(8,128)(2,1)} %n_ref.9) | copy-start | bytes 50331652
  96.4 2.3 %copy-start.7 = (bf16[34,256,256]{2,1,0:T(8,128)(2,1)S(1)}, bf16[34,256,256]{2,1,0:T(8,128)(2,1)}, u32[]{:S(2)}) copy-start(bf16[34,256,256]{2,1,0:T(8,128)(2,1)} %pad_maximum_fusion.far_ref) | copy-start | bytes 13369348
  101.3 19.8 %all-to-all-start.4 = ((bf16[64,16,256]{2,1,0:T(8,128)(2,1)}), bf16[64,16,256]{2,1,0:T(8,128)(2,1)S(1)}, u32[]{:S(2)}, u32[]{:S(2)}) async-start(bf16[64,16,256]{2,1,0:T(8,128)(2,1)} %get-tuple-element.37), calls=%async_computation.4 | async-start | bytes 1048576 | tf_op jit(solution)/shard_map/all_to_all | solution.py:26
  105.4 15.7 %collective-permute-start.6 = (bf16[16,256]{1,0:T(8,128)(2,1)S(1)}, bf16[16,256]{1,0:T(8,128)(2,1)S(1)}, u32[]{:S(2)}, u32[]{:S(2)}) collective-permute-start(bf16[16,256]{1,0:T(8,128)(2,1)S(1)} %get-tuple-element.38), channel_id=1, source_target_pairs={{0,4},{4,8},{8,12},{12,16},{16,20},{20,24},{24,28},{28,32},{32,36}... | collective-permute-start | bytes 24584 | tf_op jit(solution)/shard_map/ppermute | solution.py:300
  105.7 15.4 %collective-permute-start.7 = (bf16[16,256]{1,0:T(8,128)(2,1)S(1)}, bf16[16,256]{1,0:T(8,128)(2,1)S(1)}, u32[]{:S(2)}, u32[]{:S(2)}) collective-permute-start(bf16[16,256]{1,0:T(8,128)(2,1)S(1)} %get-tuple-element.39), channel_id=1, source_target_pairs={{4,0},{8,4},{12,8},{16,12},{20,16},{24,20},{28,24},{32,28},{36,32}... | collective-permute-start | bytes 24584 | tf_op jit(solution)/shard_map/ppermute | solution.py:301
  110.7 5.8 %copy-start.3 = (bf16[32,4,256,256]{3,2,1,0:T(8,128)(2,1)S(1)}, bf16[32,4,256,256]{3,2,1,0:T(8,128)(2,1)}, u32[]{:S(2)}) copy-start(bf16[32,4,256,256]{3,2,1,0:T(8,128)(2,1)} %n_ref.9) | copy-start | bytes 50331652
  142.1 38.8 %slice-start = ((s8[4456448]{0:T(1024)(128)(4,1)}), s8[262144]{0:T(1024)(128)(4,1)S(1)}, s32[]{:S(2)}) async-start(s8[4456448]{0:T(1024)(128)(4,1)} %bitcast.9), calls=%async_computation.9 | async-start | bytes 524288
  142.1 18.7 %all-to-all-start.7 = ((bf16[64,16,256]{2,1,0:T(8,128)(2,1)}), bf16[64,16,256]{2,1,0:T(8,128)(2,1)S(1)}, u32[]{:S(2)}, u32[]{:S(2)}) async-start(bf16[64,16,256]{2,1,0:T(8,128)(2,1)} %get-tuple-element.44), calls=%async_computation.7 | async-start | bytes 1048576 | tf_op jit(solution)/shard_map/all_to_all | solution.py:26
  160.8 23.9 %all-to-all-start.6 = ((f32[32,32,128]{2,1,0:T(8,128)}), f32[32,32,128]{2,1,0:T(8,128)}, u32[]{:S(2)}, u32[]{:S(2)}) async-start(f32[32,32,128]{2,1,0:T(8,128)} %shard_map.59), calls=%async_computation.6 | async-start | bytes 1048576 | tf_op jit(solution)/shard_map/all_to_all | solution.py:26
  165.4 15.5 %collective-permute-start.8 = (bf16[16,256]{1,0:T(8,128)(2,1)S(1)}, bf16[16,256]{1,0:T(8,128)(2,1)S(1)}, u32[]{:S(2)}, u32[]{:S(2)}) collective-permute-start(bf16[16,256]{1,0:T(8,128)(2,1)S(1)} %get-tuple-element.45), channel_id=1, source_target_pairs={{0,4},{4,8},{8,12},{12,16},{16,20},{20,24},{24,28},{28,32},{32,36}... | collective-permute-start | bytes 24584 | tf_op jit(solution)/shard_map/ppermute | solution.py:308
  165.6 15.3 %collective-permute-start.9 = (bf16[16,256]{1,0:T(8,128)(2,1)S(1)}, bf16[16,256]{1,0:T(8,128)(2,1)S(1)}, u32[]{:S(2)}, u32[]{:S(2)}) collective-permute-start(bf16[16,256]{1,0:T(8,128)(2,1)S(1)} %get-tuple-element.46), channel_id=1, source_target_pairs={{4,0},{8,4},{12,8},{16,12},{20,16},{24,20},{28,24},{32,28},{36,32}... | collective-permute-start | bytes 24584 | tf_op jit(solution)/shard_map/ppermute | solution.py:309
  170.5 5.8 %copy-start.4 = (bf16[32,4,256,256]{3,2,1,0:T(8,128)(2,1)S(1)}, bf16[32,4,256,256]{3,2,1,0:T(8,128)(2,1)}, u32[]{:S(2)}) copy-start(bf16[32,4,256,256]{3,2,1,0:T(8,128)(2,1)} %n_ref.9) | copy-start | bytes 50331652
  176.3 4.6 %slice-start.1 = ((s8[4456448]{0:T(1024)(128)(4,1)}), s8[4194304]{0:T(1024)(128)(4,1)S(1)}, s32[]{:S(2)}) async-start(s8[4456448]{0:T(1024)(128)(4,1)} %bitcast.9), calls=%async_computation.10 | async-start | bytes 8388608
  184.7 18.2 %all-to-all-start.8 = ((f32[128,1,1024]{2,1,0:T(1,128)}), f32[128,1,1024]{2,1,0:T(1,128)S(1)}, u32[]{:S(2)}, u32[]{:S(2)}) async-start(f32[128,1,1024]{2,1,0:T(1,128)} %reshape.92), calls=%async_computation.8 | async-start | bytes 1048576 | tf_op jit(solution)/shard_map/all_to_all | solution.py:26
  198.0 8.4 %copy-start.12 = (f32[64,64]{1,0:T(8,128)}, f32[64,64]{1,0:T(8,128)S(1)}, u32[]{:S(2)}) copy-start(f32[64,64]{1,0:T(8,128)S(1)} %get-tuple-element.47.inv_ref) | copy-start | bytes 49156
  (2 other events, 4.5 us)

commit v2 on v1

v2 whole, which is shorter than its diff:
```python
import functools

import jax
import jax.numpy as jnp
from jax import lax
from jax.experimental import pallas as pl
from jax.experimental.pallas import tpu as pltpu
from jax.sharding import PartitionSpec as P

ITERS = 4
CAP = 2
GROUPS = 4
AHEAD = 8
LATER = 2
STEP = 0.2
NT = (((1,), (1,)), ((), ()))
NN = (((1,), (0,)), ((), ()))
BF = jnp.bfloat16
F32 = jnp.float32
VMEM = pl.BlockSpec(memory_space=pltpu.VMEM)
SMEM = pl.BlockSpec(memory_space=pltpu.SMEM)
HBM = pl.BlockSpec(memory_space=pltpu.HBM)


def dot(a, b, dims):
    return lax.dot_general(a, b, dims, preferred_element_type=F32)


def exchange(x, axes):
    return lax.all_to_all(x, axes, split_axis=0, concat_axis=0, tiled=True)


def fetch(blocks_ref, first, held_ref, sems):
    rows, count = held_ref.shape[:2]
    group = rows // GROUPS
    copies = []
    for g in range(GROUPS):
        at = pl.ds(g * group, group)
        copies.append(pltpu.make_async_copy(blocks_ref.at[at, pl.ds(first, count)], held_ref.at[at], sems.at[g]))
    for copy in copies:
        copy.start()
    return copies


def local_kernel(rows, size, last, x_ref, *refs):
    if last:
        blocks_ref, o_ref, held_ref, sems = refs
    else:
        w_ref, blocks_ref, o_ref, far_ref, edge_ref, held_ref, sems, far_sems, edge_sems = refs
    copies = fetch(blocks_ref, 0, held_ref, sems)
    if not last:
        later = copy_edges(blocks_ref, edge_ref, edge_sems)
        later.append(pltpu.make_async_copy(blocks_ref.at[pl.ds(0, AHEAD), 3], far_ref, far_sems))
        later[-1].start()
    for b in range(rows):
        if b % (rows // GROUPS) == 0:
            copies[b // (rows // GROUPS)].wait()
        acc = dot(x_ref[:, b * size:(b + 1) * size], held_ref[b, 0], NT)
        if b > 0:
            acc += dot(x_ref[:, (b - 1) * size:b * size], held_ref[b, 1], NT)
        if b < rows - 1:
            acc += dot(x_ref[:, (b + 1) * size:(b + 2) * size], held_ref[b, 2], NT)
        at = pl.ds(b * size, size)
        o_ref[:, at] = acc if last else w_ref[:, at] + STEP * acc
    if not last:
        for copy in later:
            copy.wait()


def local_part(blocks, x, *w):
    width, states = x.shape
    rows, _, size, _ = blocks.shape
    out = [jax.ShapeDtypeStruct((width, states), F32)]
    scratch = [pltpu.VMEM((rows, 3, size, size), BF), pltpu.SemaphoreType.DMA((GROUPS,))]
    if w:
        out += [pltpu.VMEM((AHEAD, size, size), BF), pltpu.VMEM((2, size, size), BF)]
        scratch += [pltpu.SemaphoreType.DMA, pltpu.SemaphoreType.DMA((2,))]
    return pl.pallas_call(
        functools.partial(local_kernel, rows, size, not w),
        out_shape=out,
        in_specs=[VMEM] * (1 + len(w)) + [HBM],
        out_specs=[VMEM] * len(out),
        scratch_shapes=scratch,
        compiler_params=pltpu.CompilerParams(vmem_limit_bytes=24 << 20),
        cost_estimate=pl.CostEstimate(
            flops=6 * width * rows * size * size, bytes_accessed=6 * rows * size * size, transcendentals=0
        ),
    )(x, *w, blocks)


def copy_edges(blocks_ref, edge_ref, sems):
    rows = blocks_ref.shape[0]
    copies = [
        pltpu.make_async_copy(blocks_ref.at[0, 1], edge_ref.at[0], sems.at[0]),
        pltpu.make_async_copy(blocks_ref.at[rows - 1, 2], edge_ref.at[1], sems.at[1]),
    ]
    for copy in copies:
        copy.start()
    return copies


def stream_far(blocks_ref, held_ref, sems):
    ahead = blocks_ref.shape[0] - held_ref.shape[0]
    group = held_ref.shape[0] // LATER
    copies = []
    for g in range(LATER):
        source = blocks_ref.at[pl.ds(ahead + g * group, group), 3]
        copies.append(pltpu.make_async_copy(source, held_ref.at[pl.ds(g * group, group)], sems.at[g]))
    for copy in copies:
        copy.start()

    def wait(b):
        if b >= ahead and (b - ahead) % group == 0:
            copies[(b - ahead) // group].wait()
    return wait


def far_sum(b, rows, loc_ref, recv_ref, low_ref, high_ref, edge_ref, block):
    acc = dot(recv_ref[loc_ref[b]], block, NT)
    if b == 0:
        acc += dot(low_ref[...], edge_ref[0], NT)
    if b == rows - 1:
        acc += dot(high_ref[...], edge_ref[1], NT)
    return acc


def pack(want_ref, x_ref, send_ref, size):
    for s in range(send_ref.shape[0]):
        at = pl.multiple_of(want_ref[s] * size, size)
        send_ref[s] = x_ref[:, pl.ds(at, size)]


def far_kernel(rows, size, want_ref, loc_ref, t_ref, recv_ref, low_ref, high_ref, far_ref, edge_ref,
               blocks_ref, w_ref, x_ref, send_ref, first_ref, last_ref, held_ref, sems):
    wait = stream_far(blocks_ref, held_ref, sems)
    for b in range(rows):
        wait(b)
        block = far_ref[b] if b < AHEAD else held_ref[b - AHEAD]
        acc = far_sum(b, rows, loc_ref, recv_ref, low_ref, high_ref, edge_ref, block)
        at = pl.ds(b * size, size)
        new = t_ref[:, at] + STEP * acc
        w_ref[:, at] = new
        rounded = new.astype(BF)
        x_ref[:, at] = rounded
    first_ref[...] = x_ref[:, :size]
    last_ref[...] = x_ref[:, (rows - 1) * size:]
    pack(want_ref, x_ref, send_ref, size)


def far_part(want, loc, t, recv, low, high, far, edge, blocks):
    width, states = t.shape
    size = far.shape[2]
    rows = states // size
    shapes = [
        jax.ShapeDtypeStruct((width, states), F32),
        jax.ShapeDtypeStruct((width, states), BF),
        jax.ShapeDtypeStruct(recv.shape, BF),
        jax.ShapeDtypeStruct((width, size), BF),
        jax.ShapeDtypeStruct((width, size), BF),
    ]
    return pl.pallas_call(
        functools.partial(far_kernel, rows, size),
        out_shape=shapes,
        in_specs=[SMEM, SMEM] + [VMEM] * 6 + [HBM],
        out_specs=[VMEM] * len(shapes),
        scratch_shapes=[pltpu.VMEM((rows - AHEAD, size, size), BF), pltpu.SemaphoreType.DMA((LATER,))],
        compiler_params=pltpu.CompilerParams(vmem_limit_bytes=16 << 20),
        cost_estimate=pl.CostEstimate(
            flops=2 * width * rows * size * size, bytes_accessed=2 * rows * size * size, transcendentals=0
        ),
    )(want, loc, t, recv, low, high, far, edge, blocks)


def product_kernel(rows, size, copies, loc_ref, t_ref, recv_ref, low_ref, high_ref, blocks_ref,
                   all_ref, o_ref, z_ref, held_ref, edge_ref, sems, edge_sems):
    width = t_ref.shape[0]
    modes = all_ref.shape[0] * width
    edges = copy_edges(blocks_ref, edge_ref, edge_sems)
    wait = stream_far(blocks_ref, held_ref, sems)
    for edge in edges:
        edge.wait()
    for b in range(rows):
        wait(b)
        acc = far_sum(b, rows, loc_ref, recv_ref, low_ref, high_ref, edge_ref, held_ref[b])
        at = pl.ds(b * size, size)
        z = t_ref[:, at] + acc
        top = z.astype(BF)
        z_ref[:width, at] = top
        z_ref[width:, at] = (z - top.astype(F32)).astype(BF)
    total = jnp.zeros((2 * width, modes), F32)
    for start, w in strips(all_ref):
        total += dot(z_ref[:, start:start + w.shape[1]], w, NT)
    part = total[:width] + total[width:]
    folded = jnp.concatenate([part[:width // 2], part[width // 2:]], axis=1)
    for c in range(copies):
        o_ref[c] = folded


def strips(all_ref, wide=2048):
    groups, width, states = all_ref.shape
    for start in range(0, states, wide):
        yield start, all_ref[:, :, start:start + wide].reshape(groups * width, wide)


def product_part(loc, t, recv, low, high, blocks, everyone, copies):
    width, states = t.shape
    size = blocks.shape[2]
    modes = everyone.shape[0] * width
    rows = states // size
    return pl.pallas_call(
        functools.partial(product_kernel, rows, size, copies),
        out_shape=jax.ShapeDtypeStruct((copies, width // 2, 2 * modes), F32),
        in_specs=[SMEM] + [VMEM] * 4 + [HBM, VMEM],
        out_specs=VMEM,
        scratch_shapes=[
            pltpu.VMEM((2 * width, states), BF),
            pltpu.VMEM((rows, size, size), BF),
            pltpu.VMEM((2, size, size), BF),
            pltpu.SemaphoreType.DMA((LATER,)),
            pltpu.SemaphoreType.DMA((2,)),
        ],
        compiler_params=pltpu.CompilerParams(vmem_limit_bytes=16 << 20),
        cost_estimate=pl.CostEstimate(
            flops=2 * width * rows * size * size, bytes_accessed=2 * rows * size * size, transcendentals=0
        ),
    )(loc, t, recv, low, high, blocks, everyone)


def gram_kernel(own_ref, *refs):
    pieces, (o_ref, all_ref) = refs[:-2], refs[-2:]
    groups = len(pieces)
    for k, piece in enumerate(pieces):
        all_ref[lax.rem(own_ref[0] + groups - k, groups)] = piece[...]
    modes = groups * all_ref.shape[1]
    total = jnp.zeros((modes, modes), F32)
    for _, w in strips(all_ref):
        total += dot(w, w, NT)
    folded = jnp.concatenate([total[:modes // 2], total[modes // 2:]], axis=1)
    for c in range(o_ref.shape[0]):
        o_ref[c] = folded


def gram_part(own, pieces, copies):
    groups = len(pieces)
    width, states = pieces[0].shape
    modes = groups * width
    return pl.pallas_call(
        gram_kernel,
        out_shape=[
            jax.ShapeDtypeStruct((copies, modes // 2, 2 * modes), F32),
            jax.ShapeDtypeStruct((groups, width, states), BF),
        ],
        in_specs=[SMEM] + [VMEM] * groups,
        out_specs=[VMEM] * 2,
        compiler_params=pltpu.CompilerParams(vmem_limit_bytes=16 << 20),
        cost_estimate=pl.CostEstimate(
            flops=2 * modes * modes * states, bytes_accessed=4 * modes * states, transcendentals=0
        ),
    )(own, *pieces)


def inverse_factor(gram):
    n = gram.shape[0]
    row_id = lax.broadcasted_iota(jnp.int32, (n, 2 * n), 0)
    lane = lax.broadcasted_iota(jnp.int32, (n, 2 * n), 1)
    unit = jnp.where(lane == row_id + n, 1.0, 0.0)
    work = jnp.concatenate([gram, unit[:, n:]], axis=1)
    column_id = lax.broadcasted_iota(jnp.int32, (n, 1), 0)
    roots = jnp.zeros((n, 1), F32)
    for j in range(n):
        row = work[j:j + 1]
        pivot = row[:, j:j + 1]
        column = work[:, j:j + 1]
        roots = jnp.where(column_id == j, pivot, roots)
        factor = jnp.where(column_id > j, column / pivot, 0.0)
        work = work - factor * row
    return work[:, n:] * lax.rsqrt(roots)


def finish_kernel(scale, own_ref, parts_ref, all_ref, w_ref, out_ref, inv_ref):
    groups, width, _ = all_ref.shape
    modes = groups * width
    total = jnp.sum(parts_ref[...], axis=0) * scale
    gram = jnp.concatenate([total[:, :modes], total[:, modes:]], axis=0)
    inv_ref[...] = inverse_factor(gram)
    start = pl.multiple_of(own_ref[0] * width, width)
    mine = inv_ref[pl.ds(start, width)]
    place = lax.broadcasted_iota(jnp.int32, (modes, width), 0) - lax.broadcasted_iota(jnp.int32, (modes, width), 1)
    pick = jnp.where(place == start, 1.0, 0.0)
    within = lax.dot_general(mine, pick, NN, precision=lax.Precision.HIGHEST, preferred_element_type=F32)
    top = mine.astype(BF)
    rest = (mine - top.astype(F32)).astype(BF)
    left = jnp.concatenate([top, rest], axis=1)
    small = within.astype(BF)
    for first, w in strips(all_ref, 1024):
        at = pl.ds(first, w.shape[1])
        own = w_ref[:, at]
        low = (own - own.astype(BF).astype(F32)).astype(BF)
        acc = dot(left, jnp.concatenate([w, w], axis=0), NN)
        out_ref[:, at] = acc + dot(small, low, NN)


def finish(own, parts, everyone, w, scale):
    width, states = w.shape
    modes = everyone.shape[0] * width
    return pl.pallas_call(
        functools.partial(finish_kernel, scale),
        out_shape=[jax.ShapeDtypeStruct((width, states), F32), jax.ShapeDtypeStruct((modes, modes), F32)],
        in_specs=[SMEM] + [VMEM] * 3,
        out_specs=[VMEM] * 2,
        compiler_params=pltpu.CompilerParams(vmem_limit_bytes=16 << 20),
        cost_estimate=pl.CostEstimate(flops=1 << 30, bytes_accessed=16 << 20, transcendentals=0),
    )(own, parts, everyone, w)


def ritz_kernel(groups, scale, own_ref, parts_ref, inv_ref, o_ref):
    copies, half, wide = parts_ref.shape
    modes = wide // 2
    width = 2 * half
    turned = []
    for c in range(groups):
        total = parts_ref[c]
        for r in range(1, copies // groups):
            total = total + parts_ref[r * groups + c]
        turned += [total[:, :modes], total[:, modes:]]
    turned = jnp.concatenate(turned, axis=0) * scale
    highest = lax.Precision.HIGHEST
    start = pl.multiple_of(own_ref[0] * width, width)
    mine = inv_ref[pl.ds(start, width)]
    part = lax.dot_general(mine, turned, NN, precision=highest, preferred_element_type=F32)
    o_ref[...] = lax.dot_general(part, inv_ref[...], NT, precision=highest, preferred_element_type=F32)


def ask_kernel(rows, far_ref, o_ref):
    devices, lanes = o_ref.shape
    far = far_ref[...]
    owner = lax.broadcasted_iota(jnp.int32, (devices, rows), 0)
    inside = jnp.broadcast_to(far, (devices, rows)) - owner * rows
    match = jnp.logical_and(inside >= 0, inside < rows)
    first = jnp.min(jnp.where(match, inside, rows - 1), axis=1, keepdims=True)
    second = jnp.max(jnp.where(match, inside, 0), axis=1, keepdims=True)
    lane = lax.broadcasted_iota(jnp.int32, (devices, lanes), 1)
    o_ref[...] = jnp.where(lane == 0, first, second)


def first_pack_kernel(size, rows, answer_ref, x_ref, send_ref):
    for s in range(send_ref.shape[0]):
        block = jnp.clip(answer_ref[s // CAP, 0, s % CAP], 0, rows - 1)
        at = pl.multiple_of(block * size, size)
        send_ref[s] = x_ref[:, pl.ds(at, size)]


def body(basis, blocks, far_cols):
    width, states = basis.shape
    rows, _, size, _ = blocks.shape
    devices = lax.axis_size("rows")
    groups = lax.axis_size("cols")
    scale = 1.0 / (states * devices)
    both = ("rows", "cols")

    asked = pl.pallas_call(
        functools.partial(ask_kernel, rows),
        out_shape=jax.ShapeDtypeStruct((devices, 128), jnp.int32),
        in_specs=[VMEM],
        out_specs=VMEM,
        compiler_params=pltpu.CompilerParams(vmem_limit_bytes=1 << 20),
    )(far_cols.reshape(1, rows))
    answer = exchange(asked.reshape(devices, 1, 128), "rows")
    want = jnp.clip(answer[:, 0, :CAP].reshape(devices * CAP), 0, rows - 1)
    owner = far_cols // rows
    inside = far_cols % rows
    earlier = jnp.logical_and(owner[None, :] == owner[:, None], inside[None, :] < inside[:, None])
    loc = owner * CAP + jnp.any(earlier, axis=1).astype(jnp.int32)
    loc = jnp.clip(loc, 0, devices * CAP - 1)

    up = [(i, (i + 1) % devices) for i in range(devices)]
    down = [(target, source) for source, target in up]

    blocks = pltpu.with_memory_space_constraint(blocks, pltpu.HBM)
    w = basis
    x = w.astype(BF)
    send = pl.pallas_call(
        functools.partial(first_pack_kernel, size, rows),
        out_shape=jax.ShapeDtypeStruct((devices * CAP, width, size), BF),
        in_specs=[SMEM, VMEM],
        out_specs=VMEM,
        compiler_params=pltpu.CompilerParams(vmem_limit_bytes=2 << 20),
    )(answer, x)
    edge_first, edge_last = x[:, :size], x[:, states - size:]
    for _ in range(ITERS):
        recv = exchange(send, "rows")
        low = lax.ppermute(edge_last, "rows", up)
        high = lax.ppermute(edge_first, "rows", down)
        t, far, edge = local_part(blocks, x, w)
        w, x, send, edge_first, edge_last = far_part(want, loc, t, recv, low, high, far, edge, blocks)
    recv = exchange(send, "rows")
    pieces = [x]
    for k in range(1, groups):
        pieces.append(lax.ppermute(x, "cols", [(i, (i + k) % groups) for i in range(groups)]))
    low = lax.ppermute(edge_last, "rows", up)
    high = lax.ppermute(edge_first, "rows", down)
    t, = local_part(blocks, x)
    own = lax.axis_index("cols").reshape(1)
    pieces, t, low, high = lax.optimization_barrier((pieces, t, low, high))
    grams, everyone = gram_part(own, pieces, devices)
    w, t, everyone = (pltpu.with_memory_space_constraint(a, pltpu.HBM) for a in (w, t, everyone))
    gram_parts = exchange(grams, "rows")
    parts = product_part(loc, t, recv, low, high, blocks, everyone, devices * groups)
    parts = exchange(parts, both)
    basis_out, inverse = finish(own, gram_parts, everyone, w, scale)
    turned = pl.pallas_call(
        functools.partial(ritz_kernel, groups, scale),
        out_shape=jax.ShapeDtypeStruct((width, groups * width), F32),
        in_specs=[SMEM, VMEM, VMEM],
        out_specs=VMEM,
        compiler_params=pltpu.CompilerParams(vmem_limit_bytes=4 << 20),
    )(own, parts, inverse)
    ritz = turned.T
    return (basis_out, ritz)


def solution(mesh):
    in_specs = (P("cols", "rows"), P("rows", None, None, None), P("rows"))
    out_specs = (P("cols", "rows"), P(None, "cols"))
    return jax.shard_map(body, mesh=mesh, in_specs=in_specs, out_specs=out_specs, check_vma=False)
```

time: 213 us -> 168 us (0.79)
  local copies, waits for them, and re-layouts: 49.4 us -> 6.85 us
  blocking collectives: 16 us -> 0 us
  Pallas kernels: 50 us -> 65.3 us
  other arithmetic: 8.77 us -> 1.99 us
  waiting for transfers between devices: 14.8 us -> 19.1 us
    unnamed x35 -> x18, local copies, waits for them, and re-layouts: 42 us -> 6.75 us
    all_to_all x1 -> x0, blocking collectives: 16 us -> none  [exchange(): return lax.all_to_all(x, axes, split_axis=0, concat_axis=0, tiled=True)]
    pallas_call x11 -> x12, Pallas kernels: 37 us -> 49.4 us  [the longest x5 28.5 us: local_part(): pl.pallas_call(functools.partial(local_kernel, rows, size, not w), out_sh...]
    squeeze x2 -> x0, local copies, waits for them, and re-layouts: 5.64 us -> none  [body(): far = jnp.concatenate([blocks[:, 3], blocks[:1, 1], blocks[-1:, 2]], axis=0)]
    ppermute x0 -> x3, starting transfers between devices: none -> 4.51 us  [body(): lax.ppermute(x, 'cols', [(i, (i + k) % groups) for i in range(groups)])]
    concatenate x1 -> x0, other arithmetic: 4.11 us -> none  [body(): far = jnp.concatenate([blocks[:, 3], blocks[:1, 1], blocks[-1:, 2]], axis=0)]
    pallas_call x1, Pallas kernels: 2.28 us -> 6.16 us  [product_part(): pl.pallas_call(functools.partial(product_kernel, rows, size, copies), out...]
    all_to_all x8, starting transfers between devices: 44.4 us -> 41.9 us  [exchange(): return lax.all_to_all(x, axes, split_axis=0, concat_axis=0, tiled=True)]
  transfers between devices with their start and end apart: 18 -> 21, of which waited for: 2 -> 9; matrix products, arithmetic and copies ran while one was open for 7% -> 1% of each run, Pallas kernels for 18% -> 28%
where the time goes in v2:
time: 168 us; the launch traced here: 166 us
  starting transfers between devices  71.9 us (43%)
  Pallas kernels  65.3 us (39%)
  waiting for transfers between devices  19.1 us (11%)
  local copies, waits for them, and re-layouts  6.85 us (4%)
  other arithmetic  1.99 us (1%)
    all_to_all x8, starting transfers between devices, exchange(): return lax.all_to_all(x, axes, split_axis=0, concat_axis=0, tiled=True)  41.9 us
    pallas_call x5, Pallas kernels, local_part(): pl.pallas_call(functools.partial(local_kernel, rows, size, not w), out_sh...  28.5 us
    ppermute x5, starting transfers between devices, body(): high = lax.ppermute(edge_first, 'rows', down)  24.7 us
    pallas_call x4, Pallas kernels, far_part(): pl.pallas_call(functools.partial(far_kernel, rows, size), out_shape=shape...  16.9 us
    all_to_all x8, waiting for transfers between devices, exchange(): return lax.all_to_all(x, axes, split_axis=0, concat_axis=0, tiled=True)  16.3 us
    pallas_call x1, Pallas kernels, finish(): pl.pallas_call(functools.partial(finish_kernel, scale), out_shape=[jax.Sh...  8.74 us
    unnamed x18, local copies, waits for them, and re-layouts  6.75 us
    pallas_call x1, Pallas kernels, product_part(): pl.pallas_call(functools.partial(product_kernel, rows, size, copies), out...  6.16 us
  transfers between devices with their start and end apart: 21, of which 9 were waited for; matrix products, arithmetic and copies ran while one was open for 1% of the time, Pallas kernels for 28%

profile of v2, /device:TPU:0, one launch (start us, length us, event | category | flops | bytes accessed | tf_op | source)
XLA Modules:
  0.0 166.1 jit_solution(11593536883389351538)
XLA Ops:
  2.1 8.4 %all-to-all-start = ((s32[32,1,128]{2,1,0:T(1,128)}), s32[32,1,128]{2,1,0:T(1,128)S(1)}, u32[]{:S(2)}, u32[]{:S(2)}) async-start(s32[32,1,128]{2,1,0:T(1,128)} %bitcast.2), calls=%async_computation | async-start | bytes 32768 | tf_op jit(solution)/shard_map/all_to_all | solution.py:30
  11.6 5.0 %collective-permute-start.1 = (bf16[16,256]{1,0:T(8,128)(2,1)S(1)}, bf16[16,256]{1,0:T(8,128)(2,1)S(1)}, u32[]{:S(2)}, u32[]{:S(2)}) collective-permute-start(bf16[16,256]{1,0:T(8,128)(2,1)S(1)} %get-tuple-element.88), channel_id=1, source_target_pairs={{4,0},{8,4},{12,8},{16,12},{20,16},{24,20},{28,24},{32,28},{36,32}... | collective-permute-start | bytes 24584 | tf_op jit(solution)/shard_map/ppermute | solution.py:393
  16.6 1.2 all-to-all-done.answer_ref
  17.8 1.8 %shard_map.52 = bf16[64,16,256]{2,1,0:T(8,128)(2,1)} custom-call(s32[32,1,128]{2,1,0:T(1,128)S(1)} %all-to-all-done.answer_ref, bf16[16,8192]{1,0:T(8,128)(2,1)S(1)} %convert_element_type.7.x_ref), custom_call_target="tpu_custom_call" | custom-call | tf_op jit(solution)/shard_map/pallas_call | solution.py:382
  19.5 5.6 %all-to-all-start.1 = ((bf16[64,16,256]{2,1,0:T(8,128)(2,1)}), bf16[64,16,256]{2,1,0:T(8,128)(2,1)S(1)}, u32[]{:S(2)}, u32[]{:S(2)}) async-start(bf16[64,16,256]{2,1,0:T(8,128)(2,1)} %shard_map.52), calls=%async_computation.1 | async-start | bytes 1048576 | tf_op jit(solution)/shard_map/all_to_all | solution.py:30
  26.8 5.7 %shard_map.51 = (f32[16,8192]{1,0:T(8,128)S(1)}, bf16[8,256,256]{2,1,0:T(8,128)(2,1)S(1)}, bf16[2,256,256]{2,1,0:T(8,128)(2,1)S(1)}) custom-call(bf16[16,8192]{1,0:T(8,128)(2,1)S(1)} %convert_element_type.7.x_ref, f32[16,8192]{1,0:T(8,128)S(1)} %copy-done.1, bf16[32,4,256,256]{3,2,1,0:T(8,128)(2,1)} %blocks_ref.9), custom_call_target="tpu_custom_call" | custom-call | flops 201326592 | bytes 12582912 | tf_op jit(solution)/shard_map/pallas_call | solution.py:78
  32.9 4.0 %all-to-all-done.1.recv_ref = bf16[64,16,256]{2,1,0:T(8,128)(2,1)S(1)} async-done(((bf16[64,16,256]{2,1,0:T(8,128)(2,1)}), bf16[64,16,256]{2,1,0:T(8,128)(2,1)S(1)}, u32[]{:S(2)}, u32[]{:S(2)}) %all-to-all-start.1) | async-done | bytes 524320 | tf_op jit(solution)/shard_map/all_to_all | solution.py:30
  36.9 4.2 %shard_map.53 = (f32[16,8192]{1,0:T(8,128)S(1)}, bf16[16,8192]{1,0:T(8,128)(2,1)S(1)}, bf16[64,16,256]{2,1,0:T(8,128)(2,1)}, bf16[16,256]{1,0:T(8,128)(2,1)S(1)}, bf16[16,256]{1,0:T(8,128)(2,1)S(1)}) custom-call(s32[64]{0:T(128)S(1)} %min.20.want_ref, s32[32]{0:T(128)S(1)} %add_clamp_fusion.loc_ref, f32[16,8192]{1,0:T(8,128)S(1)} %get-tuple-element.45.t_ref, ...), custom_call_target="tpu_custom_call" | custom-call | flops 67108864 | bytes 4194304 | tf_op jit(solution)/shard_map/pallas_call | solution.py:161
  41.8 3.9 %all-to-all-start.2 = ((bf16[64,16,256]{2,1,0:T(8,128)(2,1)}), bf16[64,16,256]{2,1,0:T(8,128)(2,1)S(1)}, u32[]{:S(2)}, u32[]{:S(2)}) async-start(bf16[64,16,256]{2,1,0:T(8,128)(2,1)} %get-tuple-element.51), calls=%async_computation.2 | async-start | bytes 1048576 | tf_op jit(solution)/shard_map/all_to_all | solution.py:30
  45.9 4.9 %collective-permute-start.3 = (bf16[16,256]{1,0:T(8,128)(2,1)S(1)}, bf16[16,256]{1,0:T(8,128)(2,1)S(1)}, u32[]{:S(2)}, u32[]{:S(2)}) collective-permute-start(bf16[16,256]{1,0:T(8,128)(2,1)S(1)} %get-tuple-element.53), channel_id=1, source_target_pairs={{4,0},{8,4},{12,8},{16,12},{20,16},{24,20},{28,24},{32,28},{36,32}... | collective-permute-start | bytes 24584 | tf_op jit(solution)/shard_map/ppermute | solution.py:393
  51.8 5.7 %shard_map.54 = (f32[16,8192]{1,0:T(8,128)S(1)}, bf16[8,256,256]{2,1,0:T(8,128)(2,1)S(1)}, bf16[2,256,256]{2,1,0:T(8,128)(2,1)S(1)}) custom-call(bf16[16,8192]{1,0:T(8,128)(2,1)S(1)} %copy-done.4, f32[16,8192]{1,0:T(8,128)S(1)} %get-tuple-element.49.refs_0_, bf16[32,4,256,256]{3,2,1,0:T(8,128)(2,1)} %blocks_ref.9), custom_call_target="tpu_custom_call" | custom-call | flops 201326592 | bytes 12582912 | tf_op jit(solution)/shard_map/pallas_call | solution.py:78
  59.2 4.2 %shard_map.55 = (f32[16,8192]{1,0:T(8,128)S(1)}, bf16[16,8192]{1,0:T(8,128)(2,1)S(1)}, bf16[64,16,256]{2,1,0:T(8,128)(2,1)}, bf16[16,256]{1,0:T(8,128)(2,1)S(1)}, bf16[16,256]{1,0:T(8,128)(2,1)S(1)}) custom-call(s32[64]{0:T(128)S(1)} %min.20.want_ref, s32[32]{0:T(128)S(1)} %add_clamp_fusion.loc_ref, f32[16,8192]{1,0:T(8,128)S(1)} %get-tuple-element.50.t_ref, ...), custom_call_target="tpu_custom_call" | custom-call | flops 67108864 | bytes 4194304 | tf_op jit(solution)/shard_map/pallas_call | solution.py:161
  63.4 4.1 %all-to-all-start.3 = ((bf16[64,16,256]{2,1,0:T(8,128)(2,1)}), bf16[64,16,256]{2,1,0:T(8,128)(2,1)S(1)}, u32[]{:S(2)}, u32[]{:S(2)}) async-start(bf16[64,16,256]{2,1,0:T(8,128)(2,1)} %get-tuple-element.59), calls=%async_computation.3 | async-start | bytes 1048576 | tf_op jit(solution)/shard_map/all_to_all | solution.py:30
  67.8 4.8 %collective-permute-start.5 = (bf16[16,256]{1,0:T(8,128)(2,1)S(1)}, bf16[16,256]{1,0:T(8,128)(2,1)S(1)}, u32[]{:S(2)}, u32[]{:S(2)}) collective-permute-start(bf16[16,256]{1,0:T(8,128)(2,1)S(1)} %get-tuple-element.61), channel_id=1, source_target_pairs={{4,0},{8,4},{12,8},{16,12},{20,16},{24,20},{28,24},{32,28},{36,32}... | collective-permute-start | bytes 24584 | tf_op jit(solution)/shard_map/ppermute | solution.py:393
  72.6 5.7 %shard_map.56 = (f32[16,8192]{1,0:T(8,128)S(1)}, bf16[8,256,256]{2,1,0:T(8,128)(2,1)S(1)}, bf16[2,256,256]{2,1,0:T(8,128)(2,1)S(1)}) custom-call(bf16[16,8192]{1,0:T(8,128)(2,1)S(1)} %get-tuple-element.56.x_ref, f32[16,8192]{1,0:T(8,128)S(1)} %get-tuple-element.57.refs_0_, bf16[32,4,256,256]{3,2,1,0:T(8,128)(2,1)} %blocks_ref.9), custom_call_target="tpu_custom_call" | custom-call | flops 201326592 | bytes 12582912 | tf_op jit(solution)/shard_map/pallas_call | solution.py:78
  79.2 4.2 %shard_map.57 = (f32[16,8192]{1,0:T(8,128)S(1)}, bf16[16,8192]{1,0:T(8,128)(2,1)S(1)}, bf16[64,16,256]{2,1,0:T(8,128)(2,1)}, bf16[16,256]{1,0:T(8,128)(2,1)S(1)}, bf16[16,256]{1,0:T(8,128)(2,1)S(1)}) custom-call(s32[64]{0:T(128)S(1)} %min.20.want_ref, s32[32]{0:T(128)S(1)} %add_clamp_fusion.loc_ref, f32[16,8192]{1,0:T(8,128)S(1)} %get-tuple-element.58.t_ref, ...), custom_call_target="tpu_custom_call" | custom-call | flops 67108864 | bytes 4194304 | tf_op jit(solution)/shard_map/pallas_call | solution.py:161
  83.5 4.1 %all-to-all-start.4 = ((bf16[64,16,256]{2,1,0:T(8,128)(2,1)}), bf16[64,16,256]{2,1,0:T(8,128)(2,1)S(1)}, u32[]{:S(2)}, u32[]{:S(2)}) async-start(bf16[64,16,256]{2,1,0:T(8,128)(2,1)} %get-tuple-element.67), calls=%async_computation.4 | async-start | bytes 1048576 | tf_op jit(solution)/shard_map/all_to_all | solution.py:30
  87.8 4.9 %collective-permute-start.7 = (bf16[16,256]{1,0:T(8,128)(2,1)S(1)}, bf16[16,256]{1,0:T(8,128)(2,1)S(1)}, u32[]{:S(2)}, u32[]{:S(2)}) collective-permute-start(bf16[16,256]{1,0:T(8,128)(2,1)S(1)} %get-tuple-element.69), channel_id=1, source_target_pairs={{4,0},{8,4},{12,8},{16,12},{20,16},{24,20},{28,24},{32,28},{36,32}... | collective-permute-start | bytes 24584 | tf_op jit(solution)/shard_map/ppermute | solution.py:393
  92.7 5.7 %shard_map.58 = (f32[16,8192]{1,0:T(8,128)S(1)}, bf16[8,256,256]{2,1,0:T(8,128)(2,1)S(1)}, bf16[2,256,256]{2,1,0:T(8,128)(2,1)S(1)}) custom-call(bf16[16,8192]{1,0:T(8,128)(2,1)S(1)} %get-tuple-element.64.x_ref, f32[16,8192]{1,0:T(8,128)S(1)} %get-tuple-element.65.refs_0_, bf16[32,4,256,256]{3,2,1,0:T(8,128)(2,1)} %blocks_ref.9), custom_call_target="tpu_custom_call" | custom-call | flops 201326592 | bytes 12582912 | tf_op jit(solution)/shard_map/pallas_call | solution.py:78
  99.3 4.2 %shard_map.59 = (f32[16,8192]{1,0:T(8,128)S(1)}, bf16[16,8192]{1,0:T(8,128)(2,1)S(1)}, bf16[64,16,256]{2,1,0:T(8,128)(2,1)}, bf16[16,256]{1,0:T(8,128)(2,1)S(1)}, bf16[16,256]{1,0:T(8,128)(2,1)S(1)}) custom-call(s32[64]{0:T(128)S(1)} %min.20.want_ref, s32[32]{0:T(128)S(1)} %add_clamp_fusion.loc_ref, f32[16,8192]{1,0:T(8,128)S(1)} %get-tuple-element.66.t_ref, ...), custom_call_target="tpu_custom_call" | custom-call | flops 67108864 | bytes 4194304 | tf_op jit(solution)/shard_map/pallas_call | solution.py:161
  103.6 3.9 %all-to-all-start.6 = ((bf16[64,16,256]{2,1,0:T(8,128)(2,1)}), bf16[64,16,256]{2,1,0:T(8,128)(2,1)S(1)}, u32[]{:S(2)}, u32[]{:S(2)}) async-start(bf16[64,16,256]{2,1,0:T(8,128)(2,1)} %get-tuple-element.84), calls=%async_computation.6 | async-start | bytes 1048576 | tf_op jit(solution)/shard_map/all_to_all | solution.py:30
  107.5 2.8 %collective-permute-start.10 = (bf16[16,8192]{1,0:T(8,128)(2,1)S(1)}, bf16[16,8192]{1,0:T(8,128)(2,1)S(1)}, u32[]{:S(2)}, u32[]{:S(2)}) collective-permute-start(bf16[16,8192]{1,0:T(8,128)(2,1)S(1)} %get-tuple-element.75.x_ref.refs_0_), channel_id=1, source_target_pairs={{0,3},{1,0},{2,1},{3,2},{4,7},{5,4},{6,5},{7,6},{8,11},{9,8},{10,9... | collective-permute-start | bytes 786440 | tf_op jit(solution)/shard_map/ppermute | solution.py:399
  112.0 5.1 %collective-permute-start.12 = (bf16[16,256]{1,0:T(8,128)(2,1)S(1)}, bf16[16,256]{1,0:T(8,128)(2,1)S(1)}, u32[]{:S(2)}, u32[]{:S(2)}) collective-permute-start(bf16[16,256]{1,0:T(8,128)(2,1)S(1)} %get-tuple-element.74), channel_id=1, source_target_pairs={{4,0},{8,4},{12,8},{16,12},{20,16},{24,20},{28,24},{32,28},{36,32}... | collective-permute-start | bytes 24584 | tf_op jit(solution)/shard_map/ppermute | solution.py:401
  117.1 5.7 %shard_map.60.t_ref = f32[16,8192]{1,0:T(8,128)S(1)} custom-call(bf16[16,8192]{1,0:T(8,128)(2,1)S(1)} %get-tuple-element.75.x_ref.refs_0_, bf16[32,4,256,256]{3,2,1,0:T(8,128)(2,1)} %blocks_ref.9), custom_call_target="tpu_custom_call" | custom-call | flops 201326592 | bytes 12582912 | tf_op jit(solution)/shard_map/pallas_call | solution.py:78
  123.6 1.9 %collective-permute-done.8.refs_1_ = bf16[16,8192]{1,0:T(8,128)(2,1)S(1)} collective-permute-done((bf16[16,8192]{1,0:T(8,128)(2,1)S(1)}, bf16[16,8192]{1,0:T(8,128)(2,1)S(1)}, u32[]{:S(2)}, u32[]{:S(2)}) %collective-permute-start.8) | collective-permute-done | bytes 262176 | tf_op jit(solution)/shard_map/ppermute | solution.py:399
  125.5 1.4 shard_map.61
  127.9 7.4 %all-to-all-start.5 = ((f32[32,32,128]{2,1,0:T(8,128)}), f32[32,32,128]{2,1,0:T(8,128)S(1)}, u32[]{:S(2)}, u32[]{:S(2)}) async-start(f32[32,32,128]{2,1,0:T(8,128)} %get-tuple-element.79), calls=%async_computation.5 | async-start | bytes 1048576 | tf_op jit(solution)/shard_map/all_to_all | solution.py:30
  135.3 6.2 %shard_map.63 = f32[128,8,128]{2,1,0:T(8,128)} custom-call(s32[32]{0:T(128)S(1)} %add_clamp_fusion.loc_ref, f32[16,8192]{1,0:T(8,128)} %copy-done, bf16[64,16,256]{2,1,0:T(8,128)(2,1)S(1)} %all-to-all-done.6.recv_ref, bf16[16,256]{1,0:T(8,128)(2,1)S(1)} %collective-permute-done.11.low_ref, bf16[16,256]{1,0:T(8,128)(2,1)S(1)} %collective-permute-done.12.high_ref, ...), custom_call_target="tpu_custom_call" | custom-call | flops 67108864 | bytes 4194304 | tf_op jit(solution)/shard_map/pallas_call | solution.py:210
  141.5 5.6 %all-to-all-done.5.parts_ref = f32[32,32,128]{2,1,0:T(8,128)S(1)} async-done(((f32[32,32,128]{2,1,0:T(8,128)}), f32[32,32,128]{2,1,0:T(8,128)S(1)}, u32[]{:S(2)}, u32[]{:S(2)}) %all-to-all-start.5) | async-done | bytes 524320 | tf_op jit(solution)/shard_map/all_to_all | solution.py:30
  147.1 4.6 %all-to-all-start.7 = ((f32[128,8,128]{2,1,0:T(8,128)}), f32[128,8,128]{2,1,0:T(8,128)S(1)}, u32[]{:S(2)}, u32[]{:S(2)}) async-start(f32[128,8,128]{2,1,0:T(8,128)} %shard_map.63), calls=%async_computation.7 | async-start | bytes 1048576 | tf_op jit(solution)/shard_map/all_to_all | solution.py:30
  151.7 8.7 %shard_map.62 = (f32[16,8192]{1,0:T(8,128)}, f32[64,64]{1,0:T(8,128)S(1)}) custom-call(s32[1]{0:T(128)} %bitcast.own_ref, f32[32,32,128]{2,1,0:T(8,128)S(1)} %all-to-all-done.5.parts_ref, bf16[4,16,8192]{2,1,0:T(8,128)(2,1)} %copy-done.2, f32[16,8192]{1,0:T(8,128)} %copy-done.8), custom_call_target="tpu_custom_call" | custom-call | flops 1073741824 | bytes 16777216 | tf_op jit(solution)/shard_map/pallas_call | solution.py:306
  160.4 4.6 %all-to-all-done.7.parts_ref = f32[128,8,128]{2,1,0:T(8,128)S(1)} async-done(((f32[128,8,128]{2,1,0:T(8,128)}), f32[128,8,128]{2,1,0:T(8,128)S(1)}, u32[]{:S(2)}, u32[]{:S(2)}) %all-to-all-start.7) | async-done | bytes 524320 | tf_op jit(solution)/shard_map/all_to_all | solution.py:30
  (50 shorter events, 15.0 us)
Async XLA Ops:
  0.6 0.7 copy-start.7
  2.1 15.7 %all-to-all-start = ((s32[32,1,128]{2,1,0:T(1,128)}), s32[32,1,128]{2,1,0:T(1,128)S(1)}, u32[]{:S(2)}, u32[]{:S(2)}) async-start(s32[32,1,128]{2,1,0:T(1,128)} %bitcast.2), calls=%async_computation | async-start | bytes 32768 | tf_op jit(solution)/shard_map/all_to_all | solution.py:30
  11.6 21.3 %collective-permute-start.1 = (bf16[16,256]{1,0:T(8,128)(2,1)S(1)}, bf16[16,256]{1,0:T(8,128)(2,1)S(1)}, u32[]{:S(2)}, u32[]{:S(2)}) collective-permute-start(bf16[16,256]{1,0:T(8,128)(2,1)S(1)} %get-tuple-element.88), channel_id=1, source_target_pairs={{4,0},{8,4},{12,8},{16,12},{20,16},{24,20},{28,24},{32,28},{36,32}... | collective-permute-start | bytes 24584 | tf_op jit(solution)/shard_map/ppermute | solution.py:393
  16.6 16.3 %collective-permute-start = (bf16[16,256]{1,0:T(8,128)(2,1)S(1)}, bf16[16,256]{1,0:T(8,128)(2,1)S(1)}, u32[]{:S(2)}, u32[]{:S(2)}) collective-permute-start(bf16[16,256]{1,0:T(8,128)(2,1)S(1)} %get-tuple-element.89), channel_id=1, source_target_pairs={{0,4},{4,8},{8,12},{12,16},{16,20},{20,24},{24,28},{28,32},{32,36}... | collective-permute-start | bytes 24584 | tf_op jit(solution)/shard_map/ppermute | solution.py:392
  19.5 17.3 %all-to-all-start.1 = ((bf16[64,16,256]{2,1,0:T(8,128)(2,1)}), bf16[64,16,256]{2,1,0:T(8,128)(2,1)S(1)}, u32[]{:S(2)}, u32[]{:S(2)}) async-start(bf16[64,16,256]{2,1,0:T(8,128)(2,1)} %shard_map.52), calls=%async_computation.1 | async-start | bytes 1048576 | tf_op jit(solution)/shard_map/all_to_all | solution.py:30
  25.8 1.0 copy-start.1
  41.1 0.7 copy-start.3
  41.8 16.4 %all-to-all-start.2 = ((bf16[64,16,256]{2,1,0:T(8,128)(2,1)}), bf16[64,16,256]{2,1,0:T(8,128)(2,1)S(1)}, u32[]{:S(2)}, u32[]{:S(2)}) async-start(bf16[64,16,256]{2,1,0:T(8,128)(2,1)} %get-tuple-element.51), calls=%async_computation.2 | async-start | bytes 1048576 | tf_op jit(solution)/shard_map/all_to_all | solution.py:30
  45.7 12.5 %collective-permute-start.2 = (bf16[16,256]{1,0:T(8,128)(2,1)S(1)}, bf16[16,256]{1,0:T(8,128)(2,1)S(1)}, u32[]{:S(2)}, u32[]{:S(2)}) collective-permute-start(bf16[16,256]{1,0:T(8,128)(2,1)S(1)} %get-tuple-element.52), channel_id=1, source_target_pairs={{0,4},{4,8},{8,12},{12,16},{16,20},{20,24},{24,28},{28,32},{32,36}... | collective-permute-start | bytes 24584 | tf_op jit(solution)/shard_map/ppermute | solution.py:392
  45.9 12.3 %collective-permute-start.3 = (bf16[16,256]{1,0:T(8,128)(2,1)S(1)}, bf16[16,256]{1,0:T(8,128)(2,1)S(1)}, u32[]{:S(2)}, u32[]{:S(2)}) collective-permute-start(bf16[16,256]{1,0:T(8,128)(2,1)S(1)} %get-tuple-element.53), channel_id=1, source_target_pairs={{4,0},{8,4},{12,8},{16,12},{20,16},{24,20},{28,24},{32,28},{36,32}... | collective-permute-start | bytes 24584 | tf_op jit(solution)/shard_map/ppermute | solution.py:393
  50.8 0.9 copy-start.4
  57.5 0.7 copy-start.5
  58.2 1.0 copy-start.6
  63.4 15.8 %all-to-all-start.3 = ((bf16[64,16,256]{2,1,0:T(8,128)(2,1)}), bf16[64,16,256]{2,1,0:T(8,128)(2,1)S(1)}, u32[]{:S(2)}, u32[]{:S(2)}) async-start(bf16[64,16,256]{2,1,0:T(8,128)(2,1)} %get-tuple-element.59), calls=%async_computation.3 | async-start | bytes 1048576 | tf_op jit(solution)/shard_map/all_to_all | solution.py:30
  67.5 11.2 %collective-permute-start.4 = (bf16[16,256]{1,0:T(8,128)(2,1)S(1)}, bf16[16,256]{1,0:T(8,128)(2,1)S(1)}, u32[]{:S(2)}, u32[]{:S(2)}) collective-permute-start(bf16[16,256]{1,0:T(8,128)(2,1)S(1)} %get-tuple-element.60), channel_id=1, source_target_pairs={{0,4},{4,8},{8,12},{12,16},{16,20},{20,24},{24,28},{28,32},{32,36}... | collective-permute-start | bytes 24584 | tf_op jit(solution)/shard_map/ppermute | solution.py:392
  67.8 10.9 %collective-permute-start.5 = (bf16[16,256]{1,0:T(8,128)(2,1)S(1)}, bf16[16,256]{1,0:T(8,128)(2,1)S(1)}, u32[]{:S(2)}, u32[]{:S(2)}) collective-permute-start(bf16[16,256]{1,0:T(8,128)(2,1)S(1)} %get-tuple-element.61), channel_id=1, source_target_pairs={{4,0},{8,4},{12,8},{16,12},{20,16},{24,20},{28,24},{32,28},{36,32}... | collective-permute-start | bytes 24584 | tf_op jit(solution)/shard_map/ppermute | solution.py:393
  83.5 15.9 %all-to-all-start.4 = ((bf16[64,16,256]{2,1,0:T(8,128)(2,1)}), bf16[64,16,256]{2,1,0:T(8,128)(2,1)S(1)}, u32[]{:S(2)}, u32[]{:S(2)}) async-start(bf16[64,16,256]{2,1,0:T(8,128)(2,1)} %get-tuple-element.67), calls=%async_computation.4 | async-start | bytes 1048576 | tf_op jit(solution)/shard_map/all_to_all | solution.py:30
  87.6 11.2 %collective-permute-start.6 = (bf16[16,256]{1,0:T(8,128)(2,1)S(1)}, bf16[16,256]{1,0:T(8,128)(2,1)S(1)}, u32[]{:S(2)}, u32[]{:S(2)}) collective-permute-start(bf16[16,256]{1,0:T(8,128)(2,1)S(1)} %get-tuple-element.68), channel_id=1, source_target_pairs={{0,4},{4,8},{8,12},{12,16},{16,20},{20,24},{24,28},{28,32},{32,36}... | collective-permute-start | bytes 24584 | tf_op jit(solution)/shard_map/ppermute | solution.py:392
  87.8 11.0 %collective-permute-start.7 = (bf16[16,256]{1,0:T(8,128)(2,1)S(1)}, bf16[16,256]{1,0:T(8,128)(2,1)S(1)}, u32[]{:S(2)}, u32[]{:S(2)}) collective-permute-start(bf16[16,256]{1,0:T(8,128)(2,1)S(1)} %get-tuple-element.69), channel_id=1, source_target_pairs={{4,0},{8,4},{12,8},{16,12},{20,16},{24,20},{28,24},{32,28},{36,32}... | collective-permute-start | bytes 24584 | tf_op jit(solution)/shard_map/ppermute | solution.py:393
  103.6 37.9 %copy-start.8 = (f32[16,8192]{1,0:T(8,128)}, f32[16,8192]{1,0:T(8,128)S(1)}, u32[]{:S(2)}) copy-start(f32[16,8192]{1,0:T(8,128)S(1)} %get-tuple-element.81.w_ref) | copy-start | bytes 1572868
  103.6 24.4 %all-to-all-start.6 = ((bf16[64,16,256]{2,1,0:T(8,128)(2,1)}), bf16[64,16,256]{2,1,0:T(8,128)(2,1)S(1)}, u32[]{:S(2)}, u32[]{:S(2)}) async-start(bf16[64,16,256]{2,1,0:T(8,128)(2,1)} %get-tuple-element.84), calls=%async_computation.6 | async-start | bytes 1048576 | tf_op jit(solution)/shard_map/all_to_all | solution.py:30
  107.5 16.1 %collective-permute-start.10 = (bf16[16,8192]{1,0:T(8,128)(2,1)S(1)}, bf16[16,8192]{1,0:T(8,128)(2,1)S(1)}, u32[]{:S(2)}, u32[]{:S(2)}) collective-permute-start(bf16[16,8192]{1,0:T(8,128)(2,1)S(1)} %get-tuple-element.75.x_ref.refs_0_), channel_id=1, source_target_pairs={{0,3},{1,0},{2,1},{3,2},{4,7},{5,4},{6,5},{7,6},{8,11},{9,8},{10,9... | collective-permute-start | bytes 786440 | tf_op jit(solution)/shard_map/ppermute | solution.py:399
  110.3 13.3 %collective-permute-start.9 = (bf16[16,8192]{1,0:T(8,128)(2,1)S(1)}, bf16[16,8192]{1,0:T(8,128)(2,1)S(1)}, u32[]{:S(2)}, u32[]{:S(2)}) collective-permute-start(bf16[16,8192]{1,0:T(8,128)(2,1)S(1)} %get-tuple-element.75.x_ref.refs_0_), channel_id=1, source_target_pairs={{0,2},{1,3},{2,0},{3,1},{4,6},{5,7},{6,4},{7,5},{8,10},{9,11},{10,... | collective-permute-start | bytes 786440 | tf_op jit(solution)/shard_map/ppermute | solution.py:399
  111.1 14.4 %collective-permute-start.8 = (bf16[16,8192]{1,0:T(8,128)(2,1)S(1)}, bf16[16,8192]{1,0:T(8,128)(2,1)S(1)}, u32[]{:S(2)}, u32[]{:S(2)}) collective-permute-start(bf16[16,8192]{1,0:T(8,128)(2,1)S(1)} %get-tuple-element.75.x_ref.refs_0_), channel_id=1, source_target_pairs={{0,1},{1,2},{2,3},{3,0},{4,5},{5,6},{6,7},{7,4},{8,9},{9,10},{10,1... | collective-permute-start | bytes 786440 | tf_op jit(solution)/shard_map/ppermute | solution.py:399
  112.0 11.6 %collective-permute-start.11 = (bf16[16,256]{1,0:T(8,128)(2,1)S(1)}, bf16[16,256]{1,0:T(8,128)(2,1)S(1)}, u32[]{:S(2)}, u32[]{:S(2)}) collective-permute-start(bf16[16,256]{1,0:T(8,128)(2,1)S(1)} %get-tuple-element.73), channel_id=1, source_target_pairs={{0,4},{4,8},{8,12},{12,16},{16,20},{20,24},{24,28},{28,32},{32,36}... | collective-permute-start | bytes 24584 | tf_op jit(solution)/shard_map/ppermute | solution.py:400
  112.0 11.6 %collective-permute-start.12 = (bf16[16,256]{1,0:T(8,128)(2,1)S(1)}, bf16[16,256]{1,0:T(8,128)(2,1)S(1)}, u32[]{:S(2)}, u32[]{:S(2)}) collective-permute-start(bf16[16,256]{1,0:T(8,128)(2,1)S(1)} %get-tuple-element.74), channel_id=1, source_target_pairs={{4,0},{8,4},{12,8},{16,12},{20,16},{24,20},{28,24},{32,28},{36,32}... | collective-permute-start | bytes 24584 | tf_op jit(solution)/shard_map/ppermute | solution.py:401
  122.8 0.8 copy-start
  126.9 1.0 copy-start.2
  127.9 19.1 %all-to-all-start.5 = ((f32[32,32,128]{2,1,0:T(8,128)}), f32[32,32,128]{2,1,0:T(8,128)S(1)}, u32[]{:S(2)}, u32[]{:S(2)}) async-start(f32[32,32,128]{2,1,0:T(8,128)} %get-tuple-element.79), calls=%async_computation.5 | async-start | bytes 1048576 | tf_op jit(solution)/shard_map/all_to_all | solution.py:30
  147.1 17.9 %all-to-all-start.7 = ((f32[128,8,128]{2,1,0:T(8,128)}), f32[128,8,128]{2,1,0:T(8,128)S(1)}, u32[]{:S(2)}, u32[]{:S(2)}) async-start(f32[128,8,128]{2,1,0:T(8,128)} %shard_map.63), calls=%async_computation.7 | async-start | bytes 1048576 | tf_op jit(solution)/shard_map/all_to_all | solution.py:30

commit v3 on v2

--- a/solution.py
+++ b/solution.py
@@ -46,12 +46,11 @@
     if last:
         blocks_ref, o_ref, held_ref, sems = refs
     else:
-        w_ref, blocks_ref, o_ref, far_ref, edge_ref, held_ref, sems, far_sems, edge_sems = refs
+        w_ref, blocks_ref, o_ref, far_ref, held_ref, sems, far_sem = refs
     copies = fetch(blocks_ref, 0, held_ref, sems)
     if not last:
-        later = copy_edges(blocks_ref, edge_ref, edge_sems)
-        later.append(pltpu.make_async_copy(blocks_ref.at[pl.ds(0, AHEAD), 3], far_ref, far_sems))
-        later[-1].start()
+        later = pltpu.make_async_copy(blocks_ref.at[pl.ds(0, AHEAD), 3], far_ref, far_sem)
+        later.start()
     for b in range(rows):
         if b % (rows // GROUPS) == 0:
             copies[b // (rows // GROUPS)].wait()
@@ -63,8 +62,7 @@
         at = pl.ds(b * size, size)
         o_ref[:, at] = acc if last else w_ref[:, at] + STEP * acc
     if not last:
-        for copy in later:
-            copy.wait()
+        later.wait()
 
 
 def local_part(blocks, x, *w):
@@ -73,8 +71,8 @@
     out = [jax.ShapeDtypeStruct((width, states), F32)]
     scratch = [pltpu.VMEM((rows, 3, size, size), BF), pltpu.SemaphoreType.DMA((GROUPS,))]
     if w:
-        out += [pltpu.VMEM((AHEAD, size, size), BF), pltpu.VMEM((2, size, size), BF)]
-        scratch += [pltpu.SemaphoreType.DMA, pltpu.SemaphoreType.DMA((2,))]
+        out.append(pltpu.VMEM((AHEAD, size, size), BF))
+        scratch.append(pltpu.SemaphoreType.DMA)
     return pl.pallas_call(
         functools.partial(local_kernel, rows, size, not w),
         out_shape=out,
@@ -88,40 +86,53 @@
     )(x, *w, blocks)
 
 
-def copy_edges(blocks_ref, edge_ref, sems):
+def stream_far(blocks_ref, held_ref, edge_ref, sems):
     rows = blocks_ref.shape[0]
-    copies = [
-        pltpu.make_async_copy(blocks_ref.at[0, 1], edge_ref.at[0], sems.at[0]),
-        pltpu.make_async_copy(blocks_ref.at[rows - 1, 2], edge_ref.at[1], sems.at[1]),
-    ]
-    for copy in copies:
-        copy.start()
-    return copies
-
-
-def stream_far(blocks_ref, held_ref, sems):
-    ahead = blocks_ref.shape[0] - held_ref.shape[0]
+    ahead = rows - held_ref.shape[0]
     group = held_ref.shape[0] // LATER
     copies = []
     for g in range(LATER):
         source = blocks_ref.at[pl.ds(ahead + g * group, group), 3]
         copies.append(pltpu.make_async_copy(source, held_ref.at[pl.ds(g * group, group)], sems.at[g]))
+    copies.append(pltpu.make_async_copy(blocks_ref.at[0, 1], edge_ref.at[0], sems.at[LATER]))
+    copies.append(pltpu.make_async_copy(blocks_ref.at[rows - 1, 2], edge_ref.at[1], sems.at[LATER + 1]))
     for copy in copies:
         copy.start()
+    waiting = set(range(LATER + 2))
 
     def wait(b):
-        if b >= ahead and (b - ahead) % group == 0:
-            copies[(b - ahead) // group].wait()
+        needed = []
+        if b >= ahead:
+            needed.append((b - ahead) // group)
+        if b in (0, rows - 1):
+            needed += [LATER, LATER + 1]
+        for k in needed:
+            if k in waiting:
+                waiting.remove(k)
+                copies[k].wait()
     return wait
 
 
-def far_sum(b, rows, loc_ref, recv_ref, low_ref, high_ref, edge_ref, block):
+def stream_scratch(held, size):
+    return [
+        pltpu.VMEM((held, size, size), BF),
+        pltpu.VMEM((2, size, size), BF),
+        pltpu.SemaphoreType.DMA((LATER + 2,)),
+    ]
+
+
+def far_sum(b, rows, odd_ref, loc_ref, recv_ref, pair_ref, other_ref, edge_ref, block):
     acc = dot(recv_ref[loc_ref[b]], block, NT)
+    odd = odd_ref[0] == 1
     if b == 0:
-        acc += dot(low_ref[...], edge_ref[0], NT)
+        acc += dot(jnp.where(odd, pair_ref[...], other_ref[...]), edge_ref[0], NT)
     if b == rows - 1:
-        acc += dot(high_ref[...], edge_ref[1], NT)
+        acc += dot(jnp.where(odd, other_ref[...], pair_ref[...]), edge_ref[1], NT)
     return acc
+
+
+def block_order(rows):
+    return [*range(1, rows), 0]
 
 
 def pack(want_ref, x_ref, send_ref, size):
@@ -130,24 +141,24 @@
         send_ref[s] = x_ref[:, pl.ds(at, size)]
 
 
-def far_kernel(rows, size, want_ref, loc_ref, t_ref, recv_ref, low_ref, high_ref, far_ref, edge_ref,
-               blocks_ref, w_ref, x_ref, send_ref, first_ref, last_ref, held_ref, sems):
-    wait = stream_far(blocks_ref, held_ref, sems)
-    for b in range(rows):
+def far_kernel(rows, size, odd_ref, want_ref, loc_ref, t_ref, recv_ref, pair_ref, other_ref, far_ref, blocks_ref,
+               w_ref, x_ref, send_ref, to_pair_ref, to_other_ref, held_ref, edge_ref, sems):
+    wait = stream_far(blocks_ref, held_ref, edge_ref, sems)
+    for b in block_order(rows):
         wait(b)
         block = far_ref[b] if b < AHEAD else held_ref[b - AHEAD]
-        acc = far_sum(b, rows, loc_ref, recv_ref, low_ref, high_ref, edge_ref, block)
+        acc = far_sum(b, rows, odd_ref, loc_ref, recv_ref, pair_ref, other_ref, edge_ref, block)
         at = pl.ds(b * size, size)
         new = t_ref[:, at] + STEP * acc
         w_ref[:, at] = new
-        rounded = new.astype(BF)
-        x_ref[:, at] = rounded
-    first_ref[...] = x_ref[:, :size]
-    last_ref[...] = x_ref[:, (rows - 1) * size:]
+        x_ref[:, at] = new.astype(BF)
+    last = (rows - 1) * size
+    to_pair_ref[...] = x_ref[:, pl.ds(pl.multiple_of((1 - odd_ref[0]) * last, size), size)]
+    to_other_ref[...] = x_ref[:, pl.ds(pl.multiple_of(odd_ref[0] * last, size), size)]
     pack(want_ref, x_ref, send_ref, size)
 
 
-def far_part(want, loc, t, recv, low, high, far, edge, blocks):
+def far_part(odd, want, loc, t, recv, pair, other, far, blocks):
     width, states = t.shape
     size = far.shape[2]
     rows = states // size
@@ -161,27 +172,24 @@
     return pl.pallas_call(
         functools.partial(far_kernel, rows, size),
         out_shape=shapes,
-        in_specs=[SMEM, SMEM] + [VMEM] * 6 + [HBM],
+        in_specs=[SMEM] * 3 + [VMEM] * 5 + [HBM],
         out_specs=[VMEM] * len(shapes),
-        scratch_shapes=[pltpu.VMEM((rows - AHEAD, size, size), BF), pltpu.SemaphoreType.DMA((LATER,))],
+        scratch_shapes=stream_scratch(rows - AHEAD, size),
         compiler_params=pltpu.CompilerParams(vmem_limit_bytes=16 << 20),
         cost_estimate=pl.CostEstimate(
             flops=2 * width * rows * size * size, bytes_accessed=2 * rows * size * size, transcendentals=0
         ),
-    )(want, loc, t, recv, low, high, far, edge, blocks)
-
-
-def product_kernel(rows, size, copies, loc_ref, t_ref, recv_ref, low_ref, high_ref, blocks_ref,
-                   all_ref, o_ref, z_ref, held_ref, edge_ref, sems, edge_sems):
+    )(odd, want, loc, t, recv, pair, other, far, blocks)
+
+
+def product_kernel(rows, size, copies, odd_ref, loc_ref, t_ref, recv_ref, pair_ref, other_ref, blocks_ref, all_ref,
+                   o_ref, z_ref, held_ref, edge_ref, sems):
     width = t_ref.shape[0]
     modes = all_ref.shape[0] * width
-    edges = copy_edges(blocks_ref, edge_ref, edge_sems)
-    wait = stream_far(blocks_ref, held_ref, sems)
-    for edge in edges:
-        edge.wait()
-    for b in range(rows):
+    wait = stream_far(blocks_ref, held_ref, edge_ref, sems)
+    for b in block_order(rows):
         wait(b)
-        acc = far_sum(b, rows, loc_ref, recv_ref, low_ref, high_ref, edge_ref, held_ref[b])
+        acc = far_sum(b, rows, odd_ref, loc_ref, recv_ref, pair_ref, other_ref, edge_ref, held_ref[b])
         at = pl.ds(b * size, size)
         z = t_ref[:, at] + acc
         top = z.astype(BF)
@@ -202,7 +210,7 @@
         yield start, all_ref[:, :, start:start + wide].reshape(groups * width, wide)
 
 
-def product_part(loc, t, recv, low, high, blocks, everyone, copies):
+def product_part(odd, loc, t, recv, pair, other, blocks, everyone, copies):
     width, states = t.shape
     size = blocks.shape[2]
     modes = everyone.shape[0] * width
@@ -210,20 +218,17 @@
     return pl.pallas_call(
         functools.partial(product_kernel, rows, size, copies),
         out_shape=jax.ShapeDtypeStruct((copies, width // 2, 2 * modes), F32),
-        in_specs=[SMEM] + [VMEM] * 4 + [HBM, VMEM],
+        in_specs=[SMEM] * 2 + [VMEM] * 4 + [HBM, VMEM],
         out_specs=VMEM,
         scratch_shapes=[
             pltpu.VMEM((2 * width, states), BF),
-            pltpu.VMEM((rows, size, size), BF),
-            pltpu.VMEM((2, size, size), BF),
-            pltpu.SemaphoreType.DMA((LATER,)),
-            pltpu.SemaphoreType.DMA((2,)),
+            *stream_scratch(rows, size),
         ],
         compiler_params=pltpu.CompilerParams(vmem_limit_bytes=16 << 20),
         cost_estimate=pl.CostEstimate(
             flops=2 * width * rows * size * size, bytes_accessed=2 * rows * size * size, transcendentals=0
         ),
-    )(loc, t, recv, low, high, blocks, everyone)
+    )(odd, loc, t, recv, pair, other, blocks, everyone)
 
 
 def gram_kernel(own_ref, *refs):
@@ -235,9 +240,29 @@
     total = jnp.zeros((modes, modes), F32)
     for _, w in strips(all_ref):
         total += dot(w, w, NT)
-    folded = jnp.concatenate([total[:modes // 2], total[modes // 2:]], axis=1)
+    packed = pack_lower(total)
     for c in range(o_ref.shape[0]):
-        o_ref[c] = folded
+        o_ref[c] = packed
+
+
+def pack_lower(a):
+    q = a.shape[0] // 4
+    full = jnp.concatenate([a[3 * q:], a[2 * q:3 * q, :3 * q], a[:q, :q]], axis=1)
+    second = a[q:2 * q, :2 * q]
+    rest = jnp.concatenate([second[:q // 2], second[q // 2:], jnp.zeros((q // 2, 4 * q), a.dtype)], axis=1)
+    return jnp.concatenate([full, rest], axis=0)
+
+
+def unpack_lower(p):
+    q = p.shape[1] // 8
+    full, rest = p[:q], p[q:]
+    second = jnp.concatenate([rest[:, :2 * q], rest[:, 2 * q:4 * q]], axis=0)
+    strips = [full[:, 7 * q:], second, full[:, 4 * q:7 * q], full[:, :4 * q]]
+    padded = [jnp.concatenate([s, jnp.zeros((q, 4 * q - s.shape[1]), p.dtype)], axis=1) for s in strips[:3]]
+    lower = jnp.concatenate([*padded, strips[3]], axis=0)
+    row = lax.broadcasted_iota(jnp.int32, lower.shape, 0)
+    column = lax.broadcasted_iota(jnp.int32, lower.shape, 1)
+    return jnp.where(row >= column, lower, lower.T)
 
 
 def gram_part(own, pieces, copies):
@@ -247,7 +272,7 @@
     return pl.pallas_call(
         gram_kernel,
         out_shape=[
-            jax.ShapeDtypeStruct((copies, modes // 2, 2 * modes), F32),
+            jax.ShapeDtypeStruct((copies, 3 * modes // 8, 2 * modes), F32),
             jax.ShapeDtypeStruct((groups, width, states), BF),
         ],
         in_specs=[SMEM] + [VMEM] * groups,
@@ -281,8 +306,7 @@
     groups, width, _ = all_ref.shape
     modes = groups * width
     total = jnp.sum(parts_ref[...], axis=0) * scale
-    gram = jnp.concatenate([total[:, :modes], total[:, modes:]], axis=0)
-    inv_ref[...] = inverse_factor(gram)
+    inv_ref[...] = inverse_factor(unpack_lower(total))
     start = pl.multiple_of(own_ref[0] * width, width)
     mine = inv_ref[pl.ds(start, width)]
     place = lax.broadcasted_iota(jnp.int32, (modes, width), 0) - lax.broadcasted_iota(jnp.int32, (modes, width), 1)
@@ -333,9 +357,8 @@
 
 def ask_kernel(rows, far_ref, o_ref):
     devices, lanes = o_ref.shape
-    far = far_ref[...]
     owner = lax.broadcasted_iota(jnp.int32, (devices, rows), 0)
-    inside = jnp.broadcast_to(far, (devices, rows)) - owner * rows
+    inside = jnp.broadcast_to(far_ref[...], (devices, rows)) - owner * rows
     match = jnp.logical_and(inside >= 0, inside < rows)
     first = jnp.min(jnp.where(match, inside, rows - 1), axis=1, keepdims=True)
     second = jnp.max(jnp.where(match, inside, 0), axis=1, keepdims=True)
@@ -373,8 +396,9 @@
     loc = owner * CAP + jnp.any(earlier, axis=1).astype(jnp.int32)
     loc = jnp.clip(loc, 0, devices * CAP - 1)
 
-    up = [(i, (i + 1) % devices) for i in range(devices)]
-    down = [(target, source) for source, target in up]
+    pairs = [(i, i + 1 - 2 * (i % 2)) for i in range(devices)]
+    others = [(i, (i - 1 + 2 * (i % 2)) % devices) for i in range(devices)]
+    odd = (lax.axis_index("rows") % 2).astype(jnp.int32)
 
     blocks = pltpu.with_memory_space_constraint(blocks, pltpu.HBM)
     w = basis
@@ -386,26 +410,28 @@
         out_specs=VMEM,
         compiler_params=pltpu.CompilerParams(vmem_limit_bytes=2 << 20),
     )(answer, x)
-    edge_first, edge_last = x[:, :size], x[:, states - size:]
+    last = states - size
+    to_pair = lax.dynamic_slice_in_dim(x, (1 - odd) * last, size, 1)
+    to_other = lax.dynamic_slice_in_dim(x, odd * last, size, 1)
+    odd = odd.reshape(1)
     for _ in range(ITERS):
         recv = exchange(send, "rows")
-        low = lax.ppermute(edge_last, "rows", up)
-        high = lax.ppermute(edge_first, "rows", down)
-        t, far, edge = local_part(blocks, x, w)
-        w, x, send, edge_first, edge_last = far_part(want, loc, t, recv, low, high, far, edge, blocks)
+        pair = lax.ppermute(to_pair, "rows", pairs)
+        other = lax.ppermute(to_other, "rows", others)
+        t, far = local_part(blocks, x, w)
+        w, x, send, to_pair, to_other = far_part(odd, want, loc, t, recv, pair, other, far, blocks)
     recv = exchange(send, "rows")
     pieces = [x]
     for k in range(1, groups):
         pieces.append(lax.ppermute(x, "cols", [(i, (i + k) % groups) for i in range(groups)]))
-    low = lax.ppermute(edge_last, "rows", up)
-    high = lax.ppermute(edge_first, "rows", down)
+    pair = lax.ppermute(to_pair, "rows", pairs)
+    other = lax.ppermute(to_other, "rows", others)
     t, = local_part(blocks, x)
     own = lax.axis_index("cols").reshape(1)
-    pieces, t, low, high = lax.optimization_barrier((pieces, t, low, high))
+    pieces, t, pair, other = lax.optimization_barrier((pieces, t, pair, other))
     grams, everyone = gram_part(own, pieces, devices)
-    w, t, everyone = (pltpu.with_memory_space_constraint(a, pltpu.HBM) for a in (w, t, everyone))
     gram_parts = exchange(grams, "rows")
-    parts = product_part(loc, t, recv, low, high, blocks, everyone, devices * groups)
+    parts = product_part(odd, loc, t, recv, pair, other, blocks, everyone, devices * groups)
     parts = exchange(parts, both)
     basis_out, inverse = finish(own, gram_parts, everyone, w, scale)
     turned = pl.pallas_call(

time: 168 us -> 162 us (0.964)
  local copies, waits for them, and re-layouts: 6.85 us -> 2.84 us
    unnamed x18 -> x8, local copies, waits for them, and re-layouts: 6.75 us -> 2.73 us
    all_to_all x8, starting transfers between devices: 41.9 us -> 39.9 us  [exchange(): return lax.all_to_all(x, axes, split_axis=0, concat_axis=0, tiled=True)]
  transfers between devices with their start and end apart: 21 -> 21, of which waited for: 9 -> 10; matrix products, arithmetic and copies ran while one was open for 1% -> 1% of each run, Pallas kernels for 28% -> 28%
where the time goes in v3:
time: 162 us; the launch traced here: 160 us
  starting transfers between devices  71.1 us (44%)
  Pallas kernels  63.7 us (39%)
  waiting for transfers between devices  19.1 us (12%)
  local copies, waits for them, and re-layouts  2.84 us (2%)
  other arithmetic  1.99 us (1%)
    all_to_all x8, starting transfers between devices, exchange(): return lax.all_to_all(x, axes, split_axis=0, concat_axis=0, tiled=True)  39.9 us
    pallas_call x5, Pallas kernels, local_part(): pl.pallas_call(functools.partial(local_kernel, rows, size, not w), out_sh...  28.4 us
    ppermute x5, starting transfers between devices, body(): other = lax.ppermute(to_other, 'rows', others)  25.8 us
    pallas_call x4, Pallas kernels, far_part(): pl.pallas_call(functools.partial(far_kernel, rows, size), out_shape=shape...  17.4 us
    all_to_all x8, waiting for transfers between devices, exchange(): return lax.all_to_all(x, axes, split_axis=0, concat_axis=0, tiled=True)  16.2 us
    pallas_call x1, Pallas kernels, finish(): pl.pallas_call(functools.partial(finish_kernel, scale), out_shape=[jax.Sh...  7.51 us
    pallas_call x1, Pallas kernels, product_part(): pl.pallas_call(functools.partial(product_kernel, rows, size, copies), out...  5.42 us
    ppermute x3, starting transfers between devices, body(): lax.ppermute(x, 'cols', [(i, (i + k) % groups) for i in range(groups)])  4.51 us
  transfers between devices with their start and end apart: 21, of which 10 were waited for; matrix products, arithmetic and copies ran while one was open for 1% of the time, Pallas kernels for 28%

profile of v3, /device:TPU:0, one launch (start us, length us, event | category | flops | bytes accessed | tf_op | source)
XLA Modules:
  0.0 159.6 jit_solution(14145158575842652182)
XLA Ops:
  2.1 8.4 %all-to-all-start = ((s32[32,1,128]{2,1,0:T(1,128)}), s32[32,1,128]{2,1,0:T(1,128)S(1)}, u32[]{:S(2)}, u32[]{:S(2)}) async-start(s32[32,1,128]{2,1,0:T(1,128)} %bitcast.3), calls=%async_computation | async-start | bytes 32768 | tf_op jit(solution)/shard_map/all_to_all | solution.py:30
  11.6 5.0 %collective-permute-start.1 = (bf16[16,256]{1,0:T(8,128)(2,1)S(1)}, bf16[16,256]{1,0:T(8,128)(2,1)S(1)}, u32[]{:S(2)}, u32[]{:S(2)}) collective-permute-start(bf16[16,256]{1,0:T(8,128)(2,1)S(1)} %get-tuple-element.80), channel_id=1, source_target_pairs={{0,124},{4,8},{8,4},{12,16},{16,12},{20,24},{24,20},{28,32},{32,28... | collective-permute-start | bytes 24584 | tf_op jit(solution)/shard_map/ppermute | solution.py:420
  16.6 1.1 all-to-all-done.answer_ref
  17.8 1.8 %shard_map.52 = bf16[64,16,256]{2,1,0:T(8,128)(2,1)} custom-call(s32[32,1,128]{2,1,0:T(1,128)S(1)} %all-to-all-done.answer_ref, bf16[16,8192]{1,0:T(8,128)(2,1)S(1)} %convert_element_type.7.x_ref), custom_call_target="tpu_custom_call" | custom-call | tf_op jit(solution)/shard_map/pallas_call | solution.py:406
  19.5 3.9 %all-to-all-start.1 = ((bf16[64,16,256]{2,1,0:T(8,128)(2,1)}), bf16[64,16,256]{2,1,0:T(8,128)(2,1)S(1)}, u32[]{:S(2)}, u32[]{:S(2)}) async-start(bf16[64,16,256]{2,1,0:T(8,128)(2,1)} %shard_map.52), calls=%async_computation.1 | async-start | bytes 1048576 | tf_op jit(solution)/shard_map/all_to_all | solution.py:30
  25.1 5.7 %shard_map.51 = (f32[16,8192]{1,0:T(8,128)S(1)}, bf16[8,256,256]{2,1,0:T(8,128)(2,1)S(1)}) custom-call(bf16[16,8192]{1,0:T(8,128)(2,1)S(1)} %convert_element_type.7.x_ref, f32[16,8192]{1,0:T(8,128)S(1)} %copy-done, bf16[32,4,256,256]{3,2,1,0:T(8,128)(2,1)} %blocks_ref.9), custom_call_target="tpu_custom_call" | custom-call | flops 201326592 | bytes 12582912 | tf_op jit(solution)/shard_map/pallas_call | solution.py:76
  31.2 4.0 %all-to-all-done.1.recv_ref = bf16[64,16,256]{2,1,0:T(8,128)(2,1)S(1)} async-done(((bf16[64,16,256]{2,1,0:T(8,128)(2,1)}), bf16[64,16,256]{2,1,0:T(8,128)(2,1)S(1)}, u32[]{:S(2)}, u32[]{:S(2)}) %all-to-all-start.1) | async-done | bytes 524320 | tf_op jit(solution)/shard_map/all_to_all | solution.py:30
  35.2 4.4 %shard_map.53 = (f32[16,8192]{1,0:T(8,128)S(1)}, bf16[16,8192]{1,0:T(8,128)(2,1)S(1)}, bf16[64,16,256]{2,1,0:T(8,128)(2,1)}, bf16[16,256]{1,0:T(8,128)(2,1)S(1)}, bf16[16,256]{1,0:T(8,128)(2,1)S(1)}) custom-call(s32[1]{0:T(128)} %bitcast.1.odd_ref, s32[64]{0:T(128)S(1)} %min.20.want_ref, s32[32]{0:T(128)S(1)} %add_clamp_fusion.loc_ref, ...), custom_call_target="tpu_custom_call" | custom-call | flops 67108864 | bytes 4194304 | tf_op jit(solution)/shard_map/pallas_call | solution.py:172
  39.6 3.9 %all-to-all-start.2 = ((bf16[64,16,256]{2,1,0:T(8,128)(2,1)}), bf16[64,16,256]{2,1,0:T(8,128)(2,1)S(1)}, u32[]{:S(2)}, u32[]{:S(2)}) async-start(bf16[64,16,256]{2,1,0:T(8,128)(2,1)} %get-tuple-element.46), calls=%async_computation.2 | async-start | bytes 1048576 | tf_op jit(solution)/shard_map/all_to_all | solution.py:30
  43.7 5.1 %collective-permute-start.3 = (bf16[16,256]{1,0:T(8,128)(2,1)S(1)}, bf16[16,256]{1,0:T(8,128)(2,1)S(1)}, u32[]{:S(2)}, u32[]{:S(2)}) collective-permute-start(bf16[16,256]{1,0:T(8,128)(2,1)S(1)} %get-tuple-element.48), channel_id=1, source_target_pairs={{0,124},{4,8},{8,4},{12,16},{16,12},{20,24},{24,20},{28,32},{32,28... | collective-permute-start | bytes 24584 | tf_op jit(solution)/shard_map/ppermute | solution.py:420
  48.9 5.7 %shard_map.54 = (f32[16,8192]{1,0:T(8,128)S(1)}, bf16[8,256,256]{2,1,0:T(8,128)(2,1)S(1)}) custom-call(bf16[16,8192]{1,0:T(8,128)(2,1)S(1)} %get-tuple-element.43.x_ref, f32[16,8192]{1,0:T(8,128)S(1)} %get-tuple-element.44.refs_0_, bf16[32,4,256,256]{3,2,1,0:T(8,128)(2,1)} %blocks_ref.9), custom_call_target="tpu_custom_call" | custom-call | flops 201326592 | bytes 12582912 | tf_op jit(solution)/shard_map/pallas_call | solution.py:76
  55.2 4.4 %shard_map.55 = (f32[16,8192]{1,0:T(8,128)S(1)}, bf16[16,8192]{1,0:T(8,128)(2,1)S(1)}, bf16[64,16,256]{2,1,0:T(8,128)(2,1)}, bf16[16,256]{1,0:T(8,128)(2,1)S(1)}, bf16[16,256]{1,0:T(8,128)(2,1)S(1)}) custom-call(s32[1]{0:T(128)} %bitcast.1.odd_ref, s32[64]{0:T(128)S(1)} %min.20.want_ref, s32[32]{0:T(128)S(1)} %add_clamp_fusion.loc_ref, ...), custom_call_target="tpu_custom_call" | custom-call | flops 67108864 | bytes 4194304 | tf_op jit(solution)/shard_map/pallas_call | solution.py:172
  59.6 3.9 %all-to-all-start.3 = ((bf16[64,16,256]{2,1,0:T(8,128)(2,1)}), bf16[64,16,256]{2,1,0:T(8,128)(2,1)S(1)}, u32[]{:S(2)}, u32[]{:S(2)}) async-start(bf16[64,16,256]{2,1,0:T(8,128)(2,1)} %get-tuple-element.53), calls=%async_computation.3 | async-start | bytes 1048576 | tf_op jit(solution)/shard_map/all_to_all | solution.py:30
  63.7 5.1 %collective-permute-start.5 = (bf16[16,256]{1,0:T(8,128)(2,1)S(1)}, bf16[16,256]{1,0:T(8,128)(2,1)S(1)}, u32[]{:S(2)}, u32[]{:S(2)}) collective-permute-start(bf16[16,256]{1,0:T(8,128)(2,1)S(1)} %get-tuple-element.55), channel_id=1, source_target_pairs={{0,124},{4,8},{8,4},{12,16},{16,12},{20,24},{24,20},{28,32},{32,28... | collective-permute-start | bytes 24584 | tf_op jit(solution)/shard_map/ppermute | solution.py:420
  68.9 5.7 %shard_map.56 = (f32[16,8192]{1,0:T(8,128)S(1)}, bf16[8,256,256]{2,1,0:T(8,128)(2,1)S(1)}) custom-call(bf16[16,8192]{1,0:T(8,128)(2,1)S(1)} %get-tuple-element.50.x_ref, f32[16,8192]{1,0:T(8,128)S(1)} %get-tuple-element.51.refs_0_, bf16[32,4,256,256]{3,2,1,0:T(8,128)(2,1)} %blocks_ref.9), custom_call_target="tpu_custom_call" | custom-call | flops 201326592 | bytes 12582912 | tf_op jit(solution)/shard_map/pallas_call | solution.py:76
  75.3 4.4 %shard_map.57 = (f32[16,8192]{1,0:T(8,128)S(1)}, bf16[16,8192]{1,0:T(8,128)(2,1)S(1)}, bf16[64,16,256]{2,1,0:T(8,128)(2,1)}, bf16[16,256]{1,0:T(8,128)(2,1)S(1)}, bf16[16,256]{1,0:T(8,128)(2,1)S(1)}) custom-call(s32[1]{0:T(128)} %bitcast.1.odd_ref, s32[64]{0:T(128)S(1)} %min.20.want_ref, s32[32]{0:T(128)S(1)} %add_clamp_fusion.loc_ref, ...), custom_call_target="tpu_custom_call" | custom-call | flops 67108864 | bytes 4194304 | tf_op jit(solution)/shard_map/pallas_call | solution.py:172
  79.6 3.9 %all-to-all-start.4 = ((bf16[64,16,256]{2,1,0:T(8,128)(2,1)}), bf16[64,16,256]{2,1,0:T(8,128)(2,1)S(1)}, u32[]{:S(2)}, u32[]{:S(2)}) async-start(bf16[64,16,256]{2,1,0:T(8,128)(2,1)} %get-tuple-element.60), calls=%async_computation.4 | async-start | bytes 1048576 | tf_op jit(solution)/shard_map/all_to_all | solution.py:30
  83.9 5.1 %collective-permute-start.7 = (bf16[16,256]{1,0:T(8,128)(2,1)S(1)}, bf16[16,256]{1,0:T(8,128)(2,1)S(1)}, u32[]{:S(2)}, u32[]{:S(2)}) collective-permute-start(bf16[16,256]{1,0:T(8,128)(2,1)S(1)} %get-tuple-element.62), channel_id=1, source_target_pairs={{0,124},{4,8},{8,4},{12,16},{16,12},{20,24},{24,20},{28,32},{32,28... | collective-permute-start | bytes 24584 | tf_op jit(solution)/shard_map/ppermute | solution.py:420
  89.1 5.7 %shard_map.58 = (f32[16,8192]{1,0:T(8,128)S(1)}, bf16[8,256,256]{2,1,0:T(8,128)(2,1)S(1)}) custom-call(bf16[16,8192]{1,0:T(8,128)(2,1)S(1)} %get-tuple-element.57.x_ref, f32[16,8192]{1,0:T(8,128)S(1)} %get-tuple-element.58.refs_0_, bf16[32,4,256,256]{3,2,1,0:T(8,128)(2,1)} %blocks_ref.9), custom_call_target="tpu_custom_call" | custom-call | flops 201326592 | bytes 12582912 | tf_op jit(solution)/shard_map/pallas_call | solution.py:76
  95.3 4.4 %shard_map.59 = (f32[16,8192]{1,0:T(8,128)S(1)}, bf16[16,8192]{1,0:T(8,128)(2,1)S(1)}, bf16[64,16,256]{2,1,0:T(8,128)(2,1)}, bf16[16,256]{1,0:T(8,128)(2,1)S(1)}, bf16[16,256]{1,0:T(8,128)(2,1)S(1)}) custom-call(s32[1]{0:T(128)} %bitcast.1.odd_ref, s32[64]{0:T(128)S(1)} %min.20.want_ref, s32[32]{0:T(128)S(1)} %add_clamp_fusion.loc_ref, ...), custom_call_target="tpu_custom_call" | custom-call | flops 67108864 | bytes 4194304 | tf_op jit(solution)/shard_map/pallas_call | solution.py:172
  99.7 3.9 %all-to-all-start.6 = ((bf16[64,16,256]{2,1,0:T(8,128)(2,1)}), bf16[64,16,256]{2,1,0:T(8,128)(2,1)S(1)}, u32[]{:S(2)}, u32[]{:S(2)}) async-start(bf16[64,16,256]{2,1,0:T(8,128)(2,1)} %get-tuple-element.76), calls=%async_computation.6 | async-start | bytes 1048576 | tf_op jit(solution)/shard_map/all_to_all | solution.py:30
  103.6 2.8 %collective-permute-start.10 = (bf16[16,8192]{1,0:T(8,128)(2,1)S(1)}, bf16[16,8192]{1,0:T(8,128)(2,1)S(1)}, u32[]{:S(2)}, u32[]{:S(2)}) collective-permute-start(bf16[16,8192]{1,0:T(8,128)(2,1)S(1)} %get-tuple-element.67.x_ref.refs_0_), channel_id=1, source_target_pairs={{0,3},{1,0},{2,1},{3,2},{4,7},{5,4},{6,5},{7,6},{8,11},{9,8},{10,9... | collective-permute-start | bytes 786440 | tf_op jit(solution)/shard_map/ppermute | solution.py:426
  108.1 5.3 %collective-permute-start.12 = (bf16[16,256]{1,0:T(8,128)(2,1)S(1)}, bf16[16,256]{1,0:T(8,128)(2,1)S(1)}, u32[]{:S(2)}, u32[]{:S(2)}) collective-permute-start(bf16[16,256]{1,0:T(8,128)(2,1)S(1)} %get-tuple-element.66), channel_id=1, source_target_pairs={{0,124},{4,8},{8,4},{12,16},{16,12},{20,24},{24,20},{28,32},{32,28... | collective-permute-start | bytes 24584 | tf_op jit(solution)/shard_map/ppermute | solution.py:428
  113.4 5.7 %shard_map.60.t_ref = f32[16,8192]{1,0:T(8,128)S(1)} custom-call(bf16[16,8192]{1,0:T(8,128)(2,1)S(1)} %get-tuple-element.67.x_ref.refs_0_, bf16[32,4,256,256]{3,2,1,0:T(8,128)(2,1)} %blocks_ref.9), custom_call_target="tpu_custom_call" | custom-call | flops 201326592 | bytes 12582912 | tf_op jit(solution)/shard_map/pallas_call | solution.py:76
  119.1 2.5 %collective-permute-done.8.refs_1_ = bf16[16,8192]{1,0:T(8,128)(2,1)S(1)} collective-permute-done((bf16[16,8192]{1,0:T(8,128)(2,1)S(1)}, bf16[16,8192]{1,0:T(8,128)(2,1)S(1)}, u32[]{:S(2)}, u32[]{:S(2)}) %collective-permute-start.8) | collective-permute-done | bytes 262176 | tf_op jit(solution)/shard_map/ppermute | solution.py:426
  121.6 1.3 shard_map.61
  122.9 7.4 %all-to-all-start.5 = ((f32[32,24,128]{2,1,0:T(8,128)}), f32[32,24,128]{2,1,0:T(8,128)S(1)}, u32[]{:S(2)}, u32[]{:S(2)}) async-start(f32[32,24,128]{2,1,0:T(8,128)} %get-tuple-element.71), calls=%async_computation.5 | async-start | bytes 786432 | tf_op jit(solution)/shard_map/all_to_all | solution.py:30
  130.3 5.4 %shard_map.63 = f32[128,8,128]{2,1,0:T(8,128)} custom-call(s32[1]{0:T(128)} %bitcast.1.odd_ref, s32[32]{0:T(128)S(1)} %add_clamp_fusion.loc_ref, f32[16,8192]{1,0:T(8,128)S(1)} %shard_map.60.t_ref, bf16[64,16,256]{2,1,0:T(8,128)(2,1)S(1)} %all-to-all-done.6.recv_ref, bf16[16,256]{1,0:T(8,128)(2,1)S(1)} %collective-permute-done.11.pair_ref, ...), custom_call_target="tpu_custom_call" | custom-call | flops 67108864 | bytes 4194304 | tf_op jit(solution)/shard_map/pallas_call | solution.py:218
  135.7 4.9 %all-to-all-done.5.parts_ref = f32[32,24,128]{2,1,0:T(8,128)S(1)} async-done(((f32[32,24,128]{2,1,0:T(8,128)}), f32[32,24,128]{2,1,0:T(8,128)S(1)}, u32[]{:S(2)}, u32[]{:S(2)}) %all-to-all-start.5) | async-done | bytes 393248 | tf_op jit(solution)/shard_map/all_to_all | solution.py:30
  140.6 4.6 %all-to-all-start.7 = ((f32[128,8,128]{2,1,0:T(8,128)}), f32[128,8,128]{2,1,0:T(8,128)S(1)}, u32[]{:S(2)}, u32[]{:S(2)}) async-start(f32[128,8,128]{2,1,0:T(8,128)} %shard_map.63), calls=%async_computation.7 | async-start | bytes 1048576 | tf_op jit(solution)/shard_map/all_to_all | solution.py:30
  146.3 7.5 %shard_map.62 = (f32[16,8192]{1,0:T(8,128)}, f32[64,64]{1,0:T(8,128)S(1)}) custom-call(s32[1]{0:T(128)} %bitcast.own_ref, f32[32,24,128]{2,1,0:T(8,128)S(1)} %all-to-all-done.5.parts_ref, bf16[4,16,8192]{2,1,0:T(8,128)(2,1)S(1)} %get-tuple-element.72.all_ref, f32[16,8192]{1,0:T(8,128)S(1)} %copy-done.3), custom_call_target="tpu_custom_call" | custom-call | flops 1073741824 | bytes 16777216 | tf_op jit(solution)/shard_map/pallas_call | solution.py:330
  153.8 4.7 %all-to-all-done.7.parts_ref = f32[128,8,128]{2,1,0:T(8,128)S(1)} async-done(((f32[128,8,128]{2,1,0:T(8,128)}), f32[128,8,128]{2,1,0:T(8,128)S(1)}, u32[]{:S(2)}, u32[]{:S(2)}) %all-to-all-start.7) | async-done | bytes 524320 | tf_op jit(solution)/shard_map/all_to_all | solution.py:30
  (40 shorter events, 11.1 us)
Async XLA Ops:
  0.6 0.7 copy-start.1
  2.1 15.7 %all-to-all-start = ((s32[32,1,128]{2,1,0:T(1,128)}), s32[32,1,128]{2,1,0:T(1,128)S(1)}, u32[]{:S(2)}, u32[]{:S(2)}) async-start(s32[32,1,128]{2,1,0:T(1,128)} %bitcast.3), calls=%async_computation | async-start | bytes 32768 | tf_op jit(solution)/shard_map/all_to_all | solution.py:30
  11.6 19.6 %collective-permute-start.1 = (bf16[16,256]{1,0:T(8,128)(2,1)S(1)}, bf16[16,256]{1,0:T(8,128)(2,1)S(1)}, u32[]{:S(2)}, u32[]{:S(2)}) collective-permute-start(bf16[16,256]{1,0:T(8,128)(2,1)S(1)} %get-tuple-element.80), channel_id=1, source_target_pairs={{0,124},{4,8},{8,4},{12,16},{16,12},{20,24},{24,20},{28,32},{32,28... | collective-permute-start | bytes 24584 | tf_op jit(solution)/shard_map/ppermute | solution.py:420
  16.6 14.6 %collective-permute-start = (bf16[16,256]{1,0:T(8,128)(2,1)S(1)}, bf16[16,256]{1,0:T(8,128)(2,1)S(1)}, u32[]{:S(2)}, u32[]{:S(2)}) collective-permute-start(bf16[16,256]{1,0:T(8,128)(2,1)S(1)} %get-tuple-element.81), channel_id=1, source_target_pairs={{0,4},{4,0},{8,12},{12,8},{16,20},{20,16},{24,28},{28,24},{32,36},... | collective-permute-start | bytes 24584 | tf_op jit(solution)/shard_map/ppermute | solution.py:419
  19.5 15.7 %all-to-all-start.1 = ((bf16[64,16,256]{2,1,0:T(8,128)(2,1)}), bf16[64,16,256]{2,1,0:T(8,128)(2,1)S(1)}, u32[]{:S(2)}, u32[]{:S(2)}) async-start(bf16[64,16,256]{2,1,0:T(8,128)(2,1)} %shard_map.52), calls=%async_computation.1 | async-start | bytes 1048576 | tf_op jit(solution)/shard_map/all_to_all | solution.py:30
  24.1 1.0 copy-start
  39.6 15.7 %all-to-all-start.2 = ((bf16[64,16,256]{2,1,0:T(8,128)(2,1)}), bf16[64,16,256]{2,1,0:T(8,128)(2,1)S(1)}, u32[]{:S(2)}, u32[]{:S(2)}) async-start(bf16[64,16,256]{2,1,0:T(8,128)(2,1)} %get-tuple-element.46), calls=%async_computation.2 | async-start | bytes 1048576 | tf_op jit(solution)/shard_map/all_to_all | solution.py:30
  43.5 11.1 %collective-permute-start.2 = (bf16[16,256]{1,0:T(8,128)(2,1)S(1)}, bf16[16,256]{1,0:T(8,128)(2,1)S(1)}, u32[]{:S(2)}, u32[]{:S(2)}) collective-permute-start(bf16[16,256]{1,0:T(8,128)(2,1)S(1)} %get-tuple-element.47), channel_id=1, source_target_pairs={{0,4},{4,0},{8,12},{12,8},{16,20},{20,16},{24,28},{28,24},{32,36},... | collective-permute-start | bytes 24584 | tf_op jit(solution)/shard_map/ppermute | solution.py:419
  43.7 11.0 %collective-permute-start.3 = (bf16[16,256]{1,0:T(8,128)(2,1)S(1)}, bf16[16,256]{1,0:T(8,128)(2,1)S(1)}, u32[]{:S(2)}, u32[]{:S(2)}) collective-permute-start(bf16[16,256]{1,0:T(8,128)(2,1)S(1)} %get-tuple-element.48), channel_id=1, source_target_pairs={{0,124},{4,8},{8,4},{12,16},{16,12},{20,24},{24,20},{28,32},{32,28... | collective-permute-start | bytes 24584 | tf_op jit(solution)/shard_map/ppermute | solution.py:420
  59.6 15.7 %all-to-all-start.3 = ((bf16[64,16,256]{2,1,0:T(8,128)(2,1)}), bf16[64,16,256]{2,1,0:T(8,128)(2,1)S(1)}, u32[]{:S(2)}, u32[]{:S(2)}) async-start(bf16[64,16,256]{2,1,0:T(8,128)(2,1)} %get-tuple-element.53), calls=%async_computation.3 | async-start | bytes 1048576 | tf_op jit(solution)/shard_map/all_to_all | solution.py:30
  63.5 11.1 %collective-permute-start.4 = (bf16[16,256]{1,0:T(8,128)(2,1)S(1)}, bf16[16,256]{1,0:T(8,128)(2,1)S(1)}, u32[]{:S(2)}, u32[]{:S(2)}) collective-permute-start(bf16[16,256]{1,0:T(8,128)(2,1)S(1)} %get-tuple-element.54), channel_id=1, source_target_pairs={{0,4},{4,0},{8,12},{12,8},{16,20},{20,16},{24,28},{28,24},{32,36},... | collective-permute-start | bytes 24584 | tf_op jit(solution)/shard_map/ppermute | solution.py:419
  63.7 11.0 %collective-permute-start.5 = (bf16[16,256]{1,0:T(8,128)(2,1)S(1)}, bf16[16,256]{1,0:T(8,128)(2,1)S(1)}, u32[]{:S(2)}, u32[]{:S(2)}) collective-permute-start(bf16[16,256]{1,0:T(8,128)(2,1)S(1)} %get-tuple-element.55), channel_id=1, source_target_pairs={{0,124},{4,8},{8,4},{12,16},{16,12},{20,24},{24,20},{28,32},{32,28... | collective-permute-start | bytes 24584 | tf_op jit(solution)/shard_map/ppermute | solution.py:420
  79.6 15.7 %all-to-all-start.4 = ((bf16[64,16,256]{2,1,0:T(8,128)(2,1)}), bf16[64,16,256]{2,1,0:T(8,128)(2,1)S(1)}, u32[]{:S(2)}, u32[]{:S(2)}) async-start(bf16[64,16,256]{2,1,0:T(8,128)(2,1)} %get-tuple-element.60), calls=%async_computation.4 | async-start | bytes 1048576 | tf_op jit(solution)/shard_map/all_to_all | solution.py:30
  83.5 11.3 %collective-permute-start.6 = (bf16[16,256]{1,0:T(8,128)(2,1)S(1)}, bf16[16,256]{1,0:T(8,128)(2,1)S(1)}, u32[]{:S(2)}, u32[]{:S(2)}) collective-permute-start(bf16[16,256]{1,0:T(8,128)(2,1)S(1)} %get-tuple-element.61), channel_id=1, source_target_pairs={{0,4},{4,0},{8,12},{12,8},{16,20},{20,16},{24,28},{28,24},{32,36},... | collective-permute-start | bytes 24584 | tf_op jit(solution)/shard_map/ppermute | solution.py:419
  83.9 10.9 %collective-permute-start.7 = (bf16[16,256]{1,0:T(8,128)(2,1)S(1)}, bf16[16,256]{1,0:T(8,128)(2,1)S(1)}, u32[]{:S(2)}, u32[]{:S(2)}) collective-permute-start(bf16[16,256]{1,0:T(8,128)(2,1)S(1)} %get-tuple-element.62), channel_id=1, source_target_pairs={{0,124},{4,8},{8,4},{12,16},{16,12},{20,24},{24,20},{28,32},{32,28... | collective-permute-start | bytes 24584 | tf_op jit(solution)/shard_map/ppermute | solution.py:420
  99.6 3.9 %copy-start.2 = (f32[16,8192]{1,0:T(8,128)}, f32[16,8192]{1,0:T(8,128)S(1)}, u32[]{:S(2)}) copy-start(f32[16,8192]{1,0:T(8,128)S(1)} %get-tuple-element.73.w_ref) | copy-start | bytes 1572868
  99.7 23.3 %all-to-all-start.6 = ((bf16[64,16,256]{2,1,0:T(8,128)(2,1)}), bf16[64,16,256]{2,1,0:T(8,128)(2,1)S(1)}, u32[]{:S(2)}, u32[]{:S(2)}) async-start(bf16[64,16,256]{2,1,0:T(8,128)(2,1)} %get-tuple-element.76), calls=%async_computation.6 | async-start | bytes 1048576 | tf_op jit(solution)/shard_map/all_to_all | solution.py:30
  103.6 15.5 %collective-permute-start.10 = (bf16[16,8192]{1,0:T(8,128)(2,1)S(1)}, bf16[16,8192]{1,0:T(8,128)(2,1)S(1)}, u32[]{:S(2)}, u32[]{:S(2)}) collective-permute-start(bf16[16,8192]{1,0:T(8,128)(2,1)S(1)} %get-tuple-element.67.x_ref.refs_0_), channel_id=1, source_target_pairs={{0,3},{1,0},{2,1},{3,2},{4,7},{5,4},{6,5},{7,6},{8,11},{9,8},{10,9... | collective-permute-start | bytes 786440 | tf_op jit(solution)/shard_map/ppermute | solution.py:426
  106.4 12.7 %collective-permute-start.9 = (bf16[16,8192]{1,0:T(8,128)(2,1)S(1)}, bf16[16,8192]{1,0:T(8,128)(2,1)S(1)}, u32[]{:S(2)}, u32[]{:S(2)}) collective-permute-start(bf16[16,8192]{1,0:T(8,128)(2,1)S(1)} %get-tuple-element.67.x_ref.refs_0_), channel_id=1, source_target_pairs={{0,2},{1,3},{2,0},{3,1},{4,6},{5,7},{6,4},{7,5},{8,10},{9,11},{10,... | collective-permute-start | bytes 786440 | tf_op jit(solution)/shard_map/ppermute | solution.py:426
  107.2 14.4 %collective-permute-start.8 = (bf16[16,8192]{1,0:T(8,128)(2,1)S(1)}, bf16[16,8192]{1,0:T(8,128)(2,1)S(1)}, u32[]{:S(2)}, u32[]{:S(2)}) collective-permute-start(bf16[16,8192]{1,0:T(8,128)(2,1)S(1)} %get-tuple-element.67.x_ref.refs_0_), channel_id=1, source_target_pairs={{0,1},{1,2},{2,3},{3,0},{4,5},{5,6},{6,7},{7,4},{8,9},{9,10},{10,1... | collective-permute-start | bytes 786440 | tf_op jit(solution)/shard_map/ppermute | solution.py:426
  108.1 11.0 %collective-permute-start.11 = (bf16[16,256]{1,0:T(8,128)(2,1)S(1)}, bf16[16,256]{1,0:T(8,128)(2,1)S(1)}, u32[]{:S(2)}, u32[]{:S(2)}) collective-permute-start(bf16[16,256]{1,0:T(8,128)(2,1)S(1)} %get-tuple-element.65), channel_id=1, source_target_pairs={{0,4},{4,0},{8,12},{12,8},{16,20},{20,16},{24,28},{28,24},{32,36},... | collective-permute-start | bytes 24584 | tf_op jit(solution)/shard_map/ppermute | solution.py:427
  108.1 11.0 %collective-permute-start.12 = (bf16[16,256]{1,0:T(8,128)(2,1)S(1)}, bf16[16,256]{1,0:T(8,128)(2,1)S(1)}, u32[]{:S(2)}, u32[]{:S(2)}) collective-permute-start(bf16[16,256]{1,0:T(8,128)(2,1)S(1)} %get-tuple-element.66), channel_id=1, source_target_pairs={{0,124},{4,8},{8,4},{12,16},{16,12},{20,24},{24,20},{28,32},{32,28... | collective-permute-start | bytes 24584 | tf_op jit(solution)/shard_map/ppermute | solution.py:428
  122.9 17.7 %all-to-all-start.5 = ((f32[32,24,128]{2,1,0:T(8,128)}), f32[32,24,128]{2,1,0:T(8,128)S(1)}, u32[]{:S(2)}, u32[]{:S(2)}) async-start(f32[32,24,128]{2,1,0:T(8,128)} %get-tuple-element.71), calls=%async_computation.5 | async-start | bytes 786432 | tf_op jit(solution)/shard_map/all_to_all | solution.py:30
  140.6 17.9 %all-to-all-start.7 = ((f32[128,8,128]{2,1,0:T(8,128)}), f32[128,8,128]{2,1,0:T(8,128)S(1)}, u32[]{:S(2)}, u32[]{:S(2)}) async-start(f32[128,8,128]{2,1,0:T(8,128)} %shard_map.63), calls=%async_computation.7 | async-start | bytes 1048576 | tf_op jit(solution)/shard_map/all_to_all | solution.py:30
  145.2 1.0 copy-start.3

commit v4 on v3

--- a/solution.py
+++ b/solution.py
@@ -182,10 +182,9 @@
     )(odd, want, loc, t, recv, pair, other, far, blocks)
 
 
-def product_kernel(rows, size, copies, odd_ref, loc_ref, t_ref, recv_ref, pair_ref, other_ref, blocks_ref, all_ref,
-                   o_ref, z_ref, held_ref, edge_ref, sems):
+def applied_kernel(rows, size, odd_ref, loc_ref, t_ref, recv_ref, pair_ref, other_ref, blocks_ref, z_ref,
+                   held_ref, edge_ref, sems):
     width = t_ref.shape[0]
-    modes = all_ref.shape[0] * width
     wait = stream_far(blocks_ref, held_ref, edge_ref, sems)
     for b in block_order(rows):
         wait(b)
@@ -195,13 +194,23 @@
         top = z.astype(BF)
         z_ref[:width, at] = top
         z_ref[width:, at] = (z - top.astype(F32)).astype(BF)
-    total = jnp.zeros((2 * width, modes), F32)
-    for start, w in strips(all_ref):
-        total += dot(z_ref[:, start:start + w.shape[1]], w, NT)
-    part = total[:width] + total[width:]
-    folded = jnp.concatenate([part[:width // 2], part[width // 2:]], axis=1)
-    for c in range(copies):
-        o_ref[c] = folded
+
+
+def applied(odd, loc, t, recv, pair, other, blocks):
+    width, states = t.shape
+    size = blocks.shape[2]
+    rows = states // size
+    return pl.pallas_call(
+        functools.partial(applied_kernel, rows, size),
+        out_shape=jax.ShapeDtypeStruct((2 * width, states), BF),
+        in_specs=[SMEM] * 2 + [VMEM] * 4 + [HBM],
+        out_specs=VMEM,
+        scratch_shapes=stream_scratch(rows, size),
+        compiler_params=pltpu.CompilerParams(vmem_limit_bytes=16 << 20),
+        cost_estimate=pl.CostEstimate(
+            flops=2 * width * rows * size * size, bytes_accessed=2 * rows * size * size, transcendentals=0
+        ),
+    )(odd, loc, t, recv, pair, other, blocks)
 
 
 def strips(all_ref, wide=2048):
@@ -210,108 +219,102 @@
         yield start, all_ref[:, :, start:start + wide].reshape(groups * width, wide)
 
 
-def product_part(odd, loc, t, recv, pair, other, blocks, everyone, copies):
-    width, states = t.shape
-    size = blocks.shape[2]
-    modes = everyone.shape[0] * width
-    rows = states // size
-    return pl.pallas_call(
-        functools.partial(product_kernel, rows, size, copies),
-        out_shape=jax.ShapeDtypeStruct((copies, width // 2, 2 * modes), F32),
-        in_specs=[SMEM] * 2 + [VMEM] * 4 + [HBM, VMEM],
-        out_specs=VMEM,
-        scratch_shapes=[
-            pltpu.VMEM((2 * width, states), BF),
-            *stream_scratch(rows, size),
-        ],
-        compiler_params=pltpu.CompilerParams(vmem_limit_bytes=16 << 20),
-        cost_estimate=pl.CostEstimate(
-            flops=2 * width * rows * size * size, bytes_accessed=2 * rows * size * size, transcendentals=0
-        ),
-    )(odd, loc, t, recv, pair, other, blocks, everyone)
-
-
-def gram_kernel(own_ref, *refs):
+def fold(a):
+    half = a.shape[0] // 2
+    return jnp.concatenate([a[:half], a[half:]], axis=1)
+
+
+def unfold(a):
+    half = a.shape[1] // 2
+    return jnp.concatenate([a[:, :half], a[:, half:]], axis=0)
+
+
+def sums_kernel(own_ref, z_ref, *refs):
     pieces, (o_ref, all_ref) = refs[:-2], refs[-2:]
     groups = len(pieces)
+    width = z_ref.shape[0] // 2
     for k, piece in enumerate(pieces):
         all_ref[lax.rem(own_ref[0] + groups - k, groups)] = piece[...]
-    modes = groups * all_ref.shape[1]
-    total = jnp.zeros((modes, modes), F32)
-    for _, w in strips(all_ref):
-        total += dot(w, w, NT)
-    packed = pack_lower(total)
+    total = jnp.zeros((3 * width, groups * width), F32)
+    for start, w in strips(all_ref):
+        at = pl.ds(start, w.shape[1])
+        total += dot(jnp.concatenate([pieces[0][:, at], z_ref[:, at]], axis=0), w, NT)
+    folded = jnp.concatenate([fold(total[:width]), fold(total[width:2 * width] + total[2 * width:])], axis=0)
     for c in range(o_ref.shape[0]):
-        o_ref[c] = packed
-
-
-def pack_lower(a):
-    q = a.shape[0] // 4
-    full = jnp.concatenate([a[3 * q:], a[2 * q:3 * q, :3 * q], a[:q, :q]], axis=1)
-    second = a[q:2 * q, :2 * q]
-    rest = jnp.concatenate([second[:q // 2], second[q // 2:], jnp.zeros((q // 2, 4 * q), a.dtype)], axis=1)
-    return jnp.concatenate([full, rest], axis=0)
-
-
-def unpack_lower(p):
-    q = p.shape[1] // 8
-    full, rest = p[:q], p[q:]
-    second = jnp.concatenate([rest[:, :2 * q], rest[:, 2 * q:4 * q]], axis=0)
-    strips = [full[:, 7 * q:], second, full[:, 4 * q:7 * q], full[:, :4 * q]]
-    padded = [jnp.concatenate([s, jnp.zeros((q, 4 * q - s.shape[1]), p.dtype)], axis=1) for s in strips[:3]]
-    lower = jnp.concatenate([*padded, strips[3]], axis=0)
-    row = lax.broadcasted_iota(jnp.int32, lower.shape, 0)
-    column = lax.broadcasted_iota(jnp.int32, lower.shape, 1)
-    return jnp.where(row >= column, lower, lower.T)
-
-
-def gram_part(own, pieces, copies):
+        o_ref[c] = folded
+
+
+def sums(own, z, pieces, copies):
     groups = len(pieces)
     width, states = pieces[0].shape
     modes = groups * width
     return pl.pallas_call(
-        gram_kernel,
+        sums_kernel,
         out_shape=[
-            jax.ShapeDtypeStruct((copies, 3 * modes // 8, 2 * modes), F32),
+            jax.ShapeDtypeStruct((copies, width, 2 * modes), F32),
             jax.ShapeDtypeStruct((groups, width, states), BF),
         ],
-        in_specs=[SMEM] + [VMEM] * groups,
+        in_specs=[SMEM] + [VMEM] * (1 + groups),
         out_specs=[VMEM] * 2,
         compiler_params=pltpu.CompilerParams(vmem_limit_bytes=16 << 20),
         cost_estimate=pl.CostEstimate(
-            flops=2 * modes * modes * states, bytes_accessed=4 * modes * states, transcendentals=0
+            flops=6 * width * modes * states, bytes_accessed=4 * modes * states, transcendentals=0
         ),
-    )(own, *pieces)
+    )(own, z, *pieces)
 
 
 def inverse_factor(gram):
     n = gram.shape[0]
+    high = 8
     row_id = lax.broadcasted_iota(jnp.int32, (n, 2 * n), 0)
     lane = lax.broadcasted_iota(jnp.int32, (n, 2 * n), 1)
     unit = jnp.where(lane == row_id + n, 1.0, 0.0)
     work = jnp.concatenate([gram, unit[:, n:]], axis=1)
-    column_id = lax.broadcasted_iota(jnp.int32, (n, 1), 0)
-    roots = jnp.zeros((n, 1), F32)
-    for j in range(n):
-        row = work[j:j + 1]
-        pivot = row[:, j:j + 1]
-        column = work[:, j:j + 1]
-        roots = jnp.where(column_id == j, pivot, roots)
-        factor = jnp.where(column_id > j, column / pivot, 0.0)
-        work = work - factor * row
-    return work[:, n:] * lax.rsqrt(roots)
-
-
-def finish_kernel(scale, own_ref, parts_ref, all_ref, w_ref, out_ref, inv_ref):
+    slabs = [work[i:i + high] for i in range(0, n, high)]
+    within = lax.broadcasted_iota(jnp.int32, (high, 1), 0)
+    for j in range(0, n, 2):
+        at, place = divmod(j, high)
+        ones = [jnp.broadcast_to(slabs[i][:, j:j + 1], (high, 2 * n)) for i in range(at, n // high)]
+        twos = [jnp.broadcast_to(slabs[i][:, j + 1:j + 2], (high, 2 * n)) for i in range(at, n // high)]
+        first, second = slabs[at][place:place + 1], slabs[at][place + 1:place + 2]
+        over = 1.0 / ones[0][place:place + 1]
+        beside = ones[0][place + 1:place + 2]
+        ratio = beside * over
+        over_next = 1.0 / (twos[0][place + 1:place + 2] - beside * ratio)
+        scaled = first * over
+        scaled_next = (second - beside * scaled) * over_next
+        for i in range(at, n // high):
+            one, two = ones[i - at], twos[i - at] - ones[i - at] * ratio
+            if i == at:
+                one = jnp.where(within > place, one, 0.0)
+                two = jnp.where(within > place + 1, two, 0.0)
+            slabs[i] = slabs[i] - one * scaled - two * scaled_next
+    work = jnp.concatenate(slabs, axis=0)
+    pivots = jnp.sum(jnp.where(lane == row_id, work, 0.0), axis=1, keepdims=True)
+    return work[:, n:] * lax.rsqrt(pivots)
+
+
+def finish_kernel(scale, own_ref, parts_ref, all_ref, w_ref, out_ref, ritz_ref, inv_ref):
     groups, width, _ = all_ref.shape
     modes = groups * width
-    total = jnp.sum(parts_ref[...], axis=0) * scale
-    inv_ref[...] = inverse_factor(unpack_lower(total))
+    half = width // 2
+    gram, turned = [], []
+    for c in range(groups):
+        total = parts_ref[c]
+        for r in range(1, parts_ref.shape[0] // groups):
+            total = total + parts_ref[r * groups + c]
+        gram.append(unfold(total[:half]))
+        turned.append(unfold(total[half:]))
+    inv_ref[...] = inverse_factor(jnp.concatenate(gram, axis=0) * scale)
+    turned = jnp.concatenate(turned, axis=0) * scale
     start = pl.multiple_of(own_ref[0] * width, width)
     mine = inv_ref[pl.ds(start, width)]
     place = lax.broadcasted_iota(jnp.int32, (modes, width), 0) - lax.broadcasted_iota(jnp.int32, (modes, width), 1)
     pick = jnp.where(place == start, 1.0, 0.0)
-    within = lax.dot_general(mine, pick, NN, precision=lax.Precision.HIGHEST, preferred_element_type=F32)
+    highest = lax.Precision.HIGHEST
+    within = lax.dot_general(mine, pick, NN, precision=highest, preferred_element_type=F32)
+    part = lax.dot_general(mine, turned, NN, precision=highest, preferred_element_type=F32)
+    ritz_ref[...] = lax.dot_general(part, inv_ref[...], NT, precision=highest, preferred_element_type=F32)
     top = mine.astype(BF)
     rest = (mine - top.astype(F32)).astype(BF)
     left = jnp.concatenate([top, rest], axis=1)
@@ -329,30 +332,13 @@
     modes = everyone.shape[0] * width
     return pl.pallas_call(
         functools.partial(finish_kernel, scale),
-        out_shape=[jax.ShapeDtypeStruct((width, states), F32), jax.ShapeDtypeStruct((modes, modes), F32)],
+        out_shape=[jax.ShapeDtypeStruct((width, states), F32), jax.ShapeDtypeStruct((width, modes), F32)],
         in_specs=[SMEM] + [VMEM] * 3,
         out_specs=[VMEM] * 2,
+        scratch_shapes=[pltpu.VMEM((modes, modes), F32)],
         compiler_params=pltpu.CompilerParams(vmem_limit_bytes=16 << 20),
         cost_estimate=pl.CostEstimate(flops=1 << 30, bytes_accessed=16 << 20, transcendentals=0),
     )(own, parts, everyone, w)
-
-
-def ritz_kernel(groups, scale, own_ref, parts_ref, inv_ref, o_ref):
-    copies, half, wide = parts_ref.shape
-    modes = wide // 2
-    width = 2 * half
-    turned = []
-    for c in range(groups):
-        total = parts_ref[c]
-        for r in range(1, copies // groups):
-            total = total + parts_ref[r * groups + c]
-        turned += [total[:, :modes], total[:, modes:]]
-    turned = jnp.concatenate(turned, axis=0) * scale
-    highest = lax.Precision.HIGHEST
-    start = pl.multiple_of(own_ref[0] * width, width)
-    mine = inv_ref[pl.ds(start, width)]
-    part = lax.dot_general(mine, turned, NN, precision=highest, preferred_element_type=F32)
-    o_ref[...] = lax.dot_general(part, inv_ref[...], NT, precision=highest, preferred_element_type=F32)
 
 
 def ask_kernel(rows, far_ref, o_ref):
@@ -428,19 +414,10 @@
     other = lax.ppermute(to_other, "rows", others)
     t, = local_part(blocks, x)
     own = lax.axis_index("cols").reshape(1)
-    pieces, t, pair, other = lax.optimization_barrier((pieces, t, pair, other))
-    grams, everyone = gram_part(own, pieces, devices)
-    gram_parts = exchange(grams, "rows")
-    parts = product_part(odd, loc, t, recv, pair, other, blocks, everyone, devices * groups)
-    parts = exchange(parts, both)
-    basis_out, inverse = finish(own, gram_parts, everyone, w, scale)
-    turned = pl.pallas_call(
-        functools.partial(ritz_kernel, groups, scale),
-        out_shape=jax.ShapeDtypeStruct((width, groups * width), F32),
-        in_specs=[SMEM, VMEM, VMEM],
-        out_specs=VMEM,
-        compiler_params=pltpu.CompilerParams(vmem_limit_bytes=4 << 20),
-    )(own, parts, inverse)
+    z = applied(odd, loc, t, recv, pair, other, blocks)
+    pieces, z = lax.optimization_barrier((pieces, z))
+    parts, everyone = sums(own, z, pieces, devices * groups)
+    basis_out, turned = finish(own, exchange(parts, both), everyone, w, scale)
     ritz = turned.T
     return (basis_out, ritz)
 

time: 162 us -> 156 us (0.963)
  blocking collectives: 0 us -> 25.3 us
  waiting for transfers between devices: 19.1 us -> 6.91 us
  starting transfers between devices: 71.1 us -> 59.1 us
  Pallas kernels: 63.7 us -> 57.6 us
    all_to_all x0 -> x1, blocking collectives: none -> 25.3 us  [exchange(): return lax.all_to_all(x, axes, split_axis=0, concat_axis=0, tiled=True)]
    all_to_all x8 -> x6, starting transfers between devices: 39.9 us -> 27.9 us  [exchange(): return lax.all_to_all(x, axes, split_axis=0, concat_axis=0, tiled=True)]
    all_to_all x8 -> x6, waiting for transfers between devices: 16.2 us -> 6.59 us  [exchange(): return lax.all_to_all(x, axes, split_axis=0, concat_axis=0, tiled=True)]
    pallas_call x3 -> x2, Pallas kernels: 7.78 us -> 4.39 us  [the longest x1 3.77 us: applied(): pl.pallas_call(functools.partial(applied_kernel, rows, size), out_shape=j...]
    pallas_call x1, Pallas kernels: 7.51 us -> 4.82 us  [finish(): pl.pallas_call(functools.partial(finish_kernel, scale), out_shape=[jax.Sh...]
    ppermute x3, waiting for transfers between devices: 2.5 us -> 0.01 us  [body(): lax.ppermute(x, 'cols', [(i, (i + k) % groups) for i in range(groups)])]
  transfers between devices with their start and end apart: 21 -> 19, of which waited for: 10 -> 7; matrix products, arithmetic and copies ran while one was open for 1% -> 1% of each run, Pallas kernels for 28% -> 22%
where the time goes in v4:
time: 156 us; the launch traced here: 154 us
  starting transfers between devices  59.1 us (38%)
  Pallas kernels  57.6 us (37%)
  blocking collectives  25.3 us (16%)
  waiting for transfers between devices  6.91 us (4%)
  local copies, waits for them, and re-layouts  2.58 us (2%)
  other arithmetic  1.99 us (1%)
    pallas_call x5, Pallas kernels, local_part(): pl.pallas_call(functools.partial(local_kernel, rows, size, not w), out_sh...  28.4 us
    all_to_all x6, starting transfers between devices, exchange(): return lax.all_to_all(x, axes, split_axis=0, concat_axis=0, tiled=True)  27.9 us
    ppermute x5, starting transfers between devices, body(): other = lax.ppermute(to_other, 'rows', others)  25.8 us
    all_to_all x1, blocking collectives, exchange(): return lax.all_to_all(x, axes, split_axis=0, concat_axis=0, tiled=True)  25.3 us
    pallas_call x4, Pallas kernels, far_part(): pl.pallas_call(functools.partial(far_kernel, rows, size), out_shape=shape...  17.4 us
    all_to_all x6, waiting for transfers between devices, exchange(): return lax.all_to_all(x, axes, split_axis=0, concat_axis=0, tiled=True)  6.59 us
    pallas_call x1, Pallas kernels, finish(): pl.pallas_call(functools.partial(finish_kernel, scale), out_shape=[jax.Sh...  4.82 us
    ppermute x3, starting transfers between devices, body(): lax.ppermute(x, 'cols', [(i, (i + k) % groups) for i in range(groups)])  4.51 us
  transfers between devices with their start and end apart: 19, of which 7 were waited for; matrix products, arithmetic and copies ran while one was open for 1% of the time, Pallas kernels for 22%

profile of v4, /device:TPU:0, one launch (start us, length us, event | category | flops | bytes accessed | tf_op | source)
XLA Modules:
  0.0 154.4 jit_solution(124233649814520014)
XLA Ops:
  1.3 0.8 shard_map.50
  2.1 8.4 %all-to-all-start = ((s32[32,1,128]{2,1,0:T(1,128)}), s32[32,1,128]{2,1,0:T(1,128)S(1)}, u32[]{:S(2)}, u32[]{:S(2)}) async-start(s32[32,1,128]{2,1,0:T(1,128)} %bitcast.3), calls=%async_computation | async-start | bytes 32768 | tf_op jit(solution)/shard_map/all_to_all | solution.py:30
  10.5 1.1 convert_element_type.7.x_ref
  11.6 5.0 %collective-permute-start.1 = (bf16[16,256]{1,0:T(8,128)(2,1)S(1)}, bf16[16,256]{1,0:T(8,128)(2,1)S(1)}, u32[]{:S(2)}, u32[]{:S(2)}) collective-permute-start(bf16[16,256]{1,0:T(8,128)(2,1)S(1)} %get-tuple-element.76), channel_id=1, source_target_pairs={{0,124},{4,8},{8,4},{12,16},{16,12},{20,24},{24,20},{28,32},{32,28... | collective-permute-start | bytes 24584 | tf_op jit(solution)/shard_map/ppermute | solution.py:406
  16.6 1.1 all-to-all-done.answer_ref
  17.8 1.8 %shard_map.52 = bf16[64,16,256]{2,1,0:T(8,128)(2,1)} custom-call(s32[32,1,128]{2,1,0:T(1,128)S(1)} %all-to-all-done.answer_ref, bf16[16,8192]{1,0:T(8,128)(2,1)S(1)} %convert_element_type.7.x_ref), custom_call_target="tpu_custom_call" | custom-call | tf_op jit(solution)/shard_map/pallas_call | solution.py:392
  19.5 3.9 %all-to-all-start.1 = ((bf16[64,16,256]{2,1,0:T(8,128)(2,1)}), bf16[64,16,256]{2,1,0:T(8,128)(2,1)S(1)}, u32[]{:S(2)}, u32[]{:S(2)}) async-start(bf16[64,16,256]{2,1,0:T(8,128)(2,1)} %shard_map.52), calls=%async_computation.1 | async-start | bytes 1048576 | tf_op jit(solution)/shard_map/all_to_all | solution.py:30
  24.1 1.0 copy-done
  25.1 5.7 %shard_map.51 = (f32[16,8192]{1,0:T(8,128)S(1)}, bf16[8,256,256]{2,1,0:T(8,128)(2,1)S(1)}) custom-call(bf16[16,8192]{1,0:T(8,128)(2,1)S(1)} %convert_element_type.7.x_ref, f32[16,8192]{1,0:T(8,128)S(1)} %copy-done, bf16[32,4,256,256]{3,2,1,0:T(8,128)(2,1)} %blocks_ref.9), custom_call_target="tpu_custom_call" | custom-call | flops 201326592 | bytes 12582912 | tf_op jit(solution)/shard_map/pallas_call | solution.py:76
  31.2 4.0 %all-to-all-done.1.recv_ref = bf16[64,16,256]{2,1,0:T(8,128)(2,1)S(1)} async-done(((bf16[64,16,256]{2,1,0:T(8,128)(2,1)}), bf16[64,16,256]{2,1,0:T(8,128)(2,1)S(1)}, u32[]{:S(2)}, u32[]{:S(2)}) %all-to-all-start.1) | async-done | bytes 524320 | tf_op jit(solution)/shard_map/all_to_all | solution.py:30
  35.2 4.4 %shard_map.53 = (f32[16,8192]{1,0:T(8,128)S(1)}, bf16[16,8192]{1,0:T(8,128)(2,1)S(1)}, bf16[64,16,256]{2,1,0:T(8,128)(2,1)}, bf16[16,256]{1,0:T(8,128)(2,1)S(1)}, bf16[16,256]{1,0:T(8,128)(2,1)S(1)}) custom-call(s32[1]{0:T(128)} %bitcast.1.odd_ref, s32[64]{0:T(128)S(1)} %min.20.want_ref, s32[32]{0:T(128)S(1)} %add_clamp_fusion.loc_ref, ...), custom_call_target="tpu_custom_call" | custom-call | flops 67108864 | bytes 4194304 | tf_op jit(solution)/shard_map/pallas_call | solution.py:172
  39.6 3.9 %all-to-all-start.2 = ((bf16[64,16,256]{2,1,0:T(8,128)(2,1)}), bf16[64,16,256]{2,1,0:T(8,128)(2,1)S(1)}, u32[]{:S(2)}, u32[]{:S(2)}) async-start(bf16[64,16,256]{2,1,0:T(8,128)(2,1)} %get-tuple-element.44), calls=%async_computation.2 | async-start | bytes 1048576 | tf_op jit(solution)/shard_map/all_to_all | solution.py:30
  43.7 5.1 %collective-permute-start.3 = (bf16[16,256]{1,0:T(8,128)(2,1)S(1)}, bf16[16,256]{1,0:T(8,128)(2,1)S(1)}, u32[]{:S(2)}, u32[]{:S(2)}) collective-permute-start(bf16[16,256]{1,0:T(8,128)(2,1)S(1)} %get-tuple-element.46), channel_id=1, source_target_pairs={{0,124},{4,8},{8,4},{12,16},{16,12},{20,24},{24,20},{28,32},{32,28... | collective-permute-start | bytes 24584 | tf_op jit(solution)/shard_map/ppermute | solution.py:406
  48.9 5.7 %shard_map.54 = (f32[16,8192]{1,0:T(8,128)S(1)}, bf16[8,256,256]{2,1,0:T(8,128)(2,1)S(1)}) custom-call(bf16[16,8192]{1,0:T(8,128)(2,1)S(1)} %get-tuple-element.41.x_ref, f32[16,8192]{1,0:T(8,128)S(1)} %get-tuple-element.42.refs_0_, bf16[32,4,256,256]{3,2,1,0:T(8,128)(2,1)} %blocks_ref.9), custom_call_target="tpu_custom_call" | custom-call | flops 201326592 | bytes 12582912 | tf_op jit(solution)/shard_map/pallas_call | solution.py:76
  55.2 4.4 %shard_map.55 = (f32[16,8192]{1,0:T(8,128)S(1)}, bf16[16,8192]{1,0:T(8,128)(2,1)S(1)}, bf16[64,16,256]{2,1,0:T(8,128)(2,1)}, bf16[16,256]{1,0:T(8,128)(2,1)S(1)}, bf16[16,256]{1,0:T(8,128)(2,1)S(1)}) custom-call(s32[1]{0:T(128)} %bitcast.1.odd_ref, s32[64]{0:T(128)S(1)} %min.20.want_ref, s32[32]{0:T(128)S(1)} %add_clamp_fusion.loc_ref, ...), custom_call_target="tpu_custom_call" | custom-call | flops 67108864 | bytes 4194304 | tf_op jit(solution)/shard_map/pallas_call | solution.py:172
  59.6 3.9 %all-to-all-start.3 = ((bf16[64,16,256]{2,1,0:T(8,128)(2,1)}), bf16[64,16,256]{2,1,0:T(8,128)(2,1)S(1)}, u32[]{:S(2)}, u32[]{:S(2)}) async-start(bf16[64,16,256]{2,1,0:T(8,128)(2,1)} %get-tuple-element.51), calls=%async_computation.3 | async-start | bytes 1048576 | tf_op jit(solution)/shard_map/all_to_all | solution.py:30
  63.7 5.1 %collective-permute-start.5 = (bf16[16,256]{1,0:T(8,128)(2,1)S(1)}, bf16[16,256]{1,0:T(8,128)(2,1)S(1)}, u32[]{:S(2)}, u32[]{:S(2)}) collective-permute-start(bf16[16,256]{1,0:T(8,128)(2,1)S(1)} %get-tuple-element.53), channel_id=1, source_target_pairs={{0,124},{4,8},{8,4},{12,16},{16,12},{20,24},{24,20},{28,32},{32,28... | collective-permute-start | bytes 24584 | tf_op jit(solution)/shard_map/ppermute | solution.py:406
  68.9 5.7 %shard_map.56 = (f32[16,8192]{1,0:T(8,128)S(1)}, bf16[8,256,256]{2,1,0:T(8,128)(2,1)S(1)}) custom-call(bf16[16,8192]{1,0:T(8,128)(2,1)S(1)} %get-tuple-element.48.x_ref, f32[16,8192]{1,0:T(8,128)S(1)} %get-tuple-element.49.refs_0_, bf16[32,4,256,256]{3,2,1,0:T(8,128)(2,1)} %blocks_ref.9), custom_call_target="tpu_custom_call" | custom-call | flops 201326592 | bytes 12582912 | tf_op jit(solution)/shard_map/pallas_call | solution.py:76
  75.3 4.4 %shard_map.57 = (f32[16,8192]{1,0:T(8,128)S(1)}, bf16[16,8192]{1,0:T(8,128)(2,1)S(1)}, bf16[64,16,256]{2,1,0:T(8,128)(2,1)}, bf16[16,256]{1,0:T(8,128)(2,1)S(1)}, bf16[16,256]{1,0:T(8,128)(2,1)S(1)}) custom-call(s32[1]{0:T(128)} %bitcast.1.odd_ref, s32[64]{0:T(128)S(1)} %min.20.want_ref, s32[32]{0:T(128)S(1)} %add_clamp_fusion.loc_ref, ...), custom_call_target="tpu_custom_call" | custom-call | flops 67108864 | bytes 4194304 | tf_op jit(solution)/shard_map/pallas_call | solution.py:172
  79.6 3.9 %all-to-all-start.4 = ((bf16[64,16,256]{2,1,0:T(8,128)(2,1)}), bf16[64,16,256]{2,1,0:T(8,128)(2,1)S(1)}, u32[]{:S(2)}, u32[]{:S(2)}) async-start(bf16[64,16,256]{2,1,0:T(8,128)(2,1)} %get-tuple-element.58), calls=%async_computation.4 | async-start | bytes 1048576 | tf_op jit(solution)/shard_map/all_to_all | solution.py:30
  84.0 5.1 %collective-permute-start.7 = (bf16[16,256]{1,0:T(8,128)(2,1)S(1)}, bf16[16,256]{1,0:T(8,128)(2,1)S(1)}, u32[]{:S(2)}, u32[]{:S(2)}) collective-permute-start(bf16[16,256]{1,0:T(8,128)(2,1)S(1)} %get-tuple-element.60), channel_id=1, source_target_pairs={{0,124},{4,8},{8,4},{12,16},{16,12},{20,24},{24,20},{28,32},{32,28... | collective-permute-start | bytes 24584 | tf_op jit(solution)/shard_map/ppermute | solution.py:406
  89.1 5.7 %shard_map.58 = (f32[16,8192]{1,0:T(8,128)S(1)}, bf16[8,256,256]{2,1,0:T(8,128)(2,1)S(1)}) custom-call(bf16[16,8192]{1,0:T(8,128)(2,1)S(1)} %get-tuple-element.55.x_ref, f32[16,8192]{1,0:T(8,128)S(1)} %get-tuple-element.56.refs_0_, bf16[32,4,256,256]{3,2,1,0:T(8,128)(2,1)} %blocks_ref.9), custom_call_target="tpu_custom_call" | custom-call | flops 201326592 | bytes 12582912 | tf_op jit(solution)/shard_map/pallas_call | solution.py:76
  95.3 4.4 %shard_map.59 = (f32[16,8192]{1,0:T(8,128)S(1)}, bf16[16,8192]{1,0:T(8,128)(2,1)S(1)}, bf16[64,16,256]{2,1,0:T(8,128)(2,1)}, bf16[16,256]{1,0:T(8,128)(2,1)S(1)}, bf16[16,256]{1,0:T(8,128)(2,1)S(1)}) custom-call(s32[1]{0:T(128)} %bitcast.1.odd_ref, s32[64]{0:T(128)S(1)} %min.20.want_ref, s32[32]{0:T(128)S(1)} %add_clamp_fusion.loc_ref, ...), custom_call_target="tpu_custom_call" | custom-call | flops 67108864 | bytes 4194304 | tf_op jit(solution)/shard_map/pallas_call | solution.py:172
  100.5 3.9 %all-to-all-start.5 = ((bf16[64,16,256]{2,1,0:T(8,128)(2,1)}), bf16[64,16,256]{2,1,0:T(8,128)(2,1)S(1)}, u32[]{:S(2)}, u32[]{:S(2)}) async-start(bf16[64,16,256]{2,1,0:T(8,128)(2,1)} %get-tuple-element.63), calls=%async_computation.5 | async-start | bytes 1048576 | tf_op jit(solution)/shard_map/all_to_all | solution.py:30
  104.4 2.8 %collective-permute-start.10 = (bf16[16,8192]{1,0:T(8,128)(2,1)S(1)}, bf16[16,8192]{1,0:T(8,128)(2,1)S(1)}, u32[]{:S(2)}, u32[]{:S(2)}) collective-permute-start(bf16[16,8192]{1,0:T(8,128)(2,1)S(1)} %get-tuple-element.67.x_ref.refs_0_), channel_id=1, source_target_pairs={{0,3},{1,0},{2,1},{3,2},{4,7},{5,4},{6,5},{7,6},{8,11},{9,8},{10,9... | collective-permute-start | bytes 786440 | tf_op jit(solution)/shard_map/ppermute | solution.py:412
  107.2 0.8 collective-permute-start.9
  108.0 0.9 collective-permute-start.8
  108.9 5.3 %collective-permute-start.12 = (bf16[16,256]{1,0:T(8,128)(2,1)S(1)}, bf16[16,256]{1,0:T(8,128)(2,1)S(1)}, u32[]{:S(2)}, u32[]{:S(2)}) collective-permute-start(bf16[16,256]{1,0:T(8,128)(2,1)S(1)} %get-tuple-element.65), channel_id=1, source_target_pairs={{0,124},{4,8},{8,4},{12,16},{16,12},{20,24},{24,20},{28,32},{32,28... | collective-permute-start | bytes 24584 | tf_op jit(solution)/shard_map/ppermute | solution.py:414
  114.2 5.7 %shard_map.60.t_ref = f32[16,8192]{1,0:T(8,128)S(1)} custom-call(bf16[16,8192]{1,0:T(8,128)(2,1)S(1)} %get-tuple-element.67.x_ref.refs_0_, bf16[32,4,256,256]{3,2,1,0:T(8,128)(2,1)} %blocks_ref.9), custom_call_target="tpu_custom_call" | custom-call | flops 201326592 | bytes 12582912 | tf_op jit(solution)/shard_map/pallas_call | solution.py:76
  119.9 3.8 %shard_map.61.z_ref = bf16[32,8192]{1,0:T(8,128)(2,1)S(1)} custom-call(s32[1]{0:T(128)} %bitcast.1.odd_ref, s32[32]{0:T(128)S(1)} %add_clamp_fusion.loc_ref, f32[16,8192]{1,0:T(8,128)S(1)} %shard_map.60.t_ref, bf16[64,16,256]{2,1,0:T(8,128)(2,1)S(1)} %all-to-all-done.5.recv_ref, bf16[16,256]{1,0:T(8,128)(2,1)S(1)} %collective-permute-done.11.pair_ref, ...), custom_call_target="tpu_custom_call" | custom-call | flops 67108864 | bytes 4194304 | tf_op jit(solution)/shard_map/pallas_call | solution.py:203
  124.3 25.3 %all_to_all.35.parts_ref = f32[128,16,128]{2,1,0:T(8,128)S(1)} all-to-all(f32[128,16,128]{2,1,0:T(8,128)S(1)} %get-tuple-element.71), channel_id=1, replica_groups=mesh['rows'=32,'cols'=4] {'rows','cols'}, dimensions={0} | all-to-all | bytes 2097152 | tf_op jit(solution)/shard_map/all_to_all | solution.py:30
  149.6 4.8 %shard_map.63 = (f32[16,8192]{1,0:T(8,128)}, f32[16,64]{1,0:T(8,128)}) custom-call(s32[1]{0:T(128)} %bitcast.own_ref, f32[128,16,128]{2,1,0:T(8,128)S(1)} %all_to_all.35.parts_ref, bf16[4,16,8192]{2,1,0:T(8,128)(2,1)S(1)} %get-tuple-element.72.all_ref, f32[16,8192]{1,0:T(8,128)S(1)} %copy-done.3), custom_call_target="tpu_custom_call" | custom-call | flops 1073741824 | bytes 16777216 | tf_op jit(solution)/shard_map/pallas_call | solution.py:333
  (36 shorter events, 5.8 us)
Async XLA Ops:
  0.6 0.7 copy-start.1
  2.1 15.7 %all-to-all-start = ((s32[32,1,128]{2,1,0:T(1,128)}), s32[32,1,128]{2,1,0:T(1,128)S(1)}, u32[]{:S(2)}, u32[]{:S(2)}) async-start(s32[32,1,128]{2,1,0:T(1,128)} %bitcast.3), calls=%async_computation | async-start | bytes 32768 | tf_op jit(solution)/shard_map/all_to_all | solution.py:30
  11.6 19.6 %collective-permute-start.1 = (bf16[16,256]{1,0:T(8,128)(2,1)S(1)}, bf16[16,256]{1,0:T(8,128)(2,1)S(1)}, u32[]{:S(2)}, u32[]{:S(2)}) collective-permute-start(bf16[16,256]{1,0:T(8,128)(2,1)S(1)} %get-tuple-element.76), channel_id=1, source_target_pairs={{0,124},{4,8},{8,4},{12,16},{16,12},{20,24},{24,20},{28,32},{32,28... | collective-permute-start | bytes 24584 | tf_op jit(solution)/shard_map/ppermute | solution.py:406
  16.6 14.6 %collective-permute-start = (bf16[16,256]{1,0:T(8,128)(2,1)S(1)}, bf16[16,256]{1,0:T(8,128)(2,1)S(1)}, u32[]{:S(2)}, u32[]{:S(2)}) collective-permute-start(bf16[16,256]{1,0:T(8,128)(2,1)S(1)} %get-tuple-element.77), channel_id=1, source_target_pairs={{0,4},{4,0},{8,12},{12,8},{16,20},{20,16},{24,28},{28,24},{32,36},... | collective-permute-start | bytes 24584 | tf_op jit(solution)/shard_map/ppermute | solution.py:405
  19.5 15.7 %all-to-all-start.1 = ((bf16[64,16,256]{2,1,0:T(8,128)(2,1)}), bf16[64,16,256]{2,1,0:T(8,128)(2,1)S(1)}, u32[]{:S(2)}, u32[]{:S(2)}) async-start(bf16[64,16,256]{2,1,0:T(8,128)(2,1)} %shard_map.52), calls=%async_computation.1 | async-start | bytes 1048576 | tf_op jit(solution)/shard_map/all_to_all | solution.py:30
  24.1 1.0 copy-start
  39.6 15.7 %all-to-all-start.2 = ((bf16[64,16,256]{2,1,0:T(8,128)(2,1)}), bf16[64,16,256]{2,1,0:T(8,128)(2,1)S(1)}, u32[]{:S(2)}, u32[]{:S(2)}) async-start(bf16[64,16,256]{2,1,0:T(8,128)(2,1)} %get-tuple-element.44), calls=%async_computation.2 | async-start | bytes 1048576 | tf_op jit(solution)/shard_map/all_to_all | solution.py:30
  43.5 11.1 %collective-permute-start.2 = (bf16[16,256]{1,0:T(8,128)(2,1)S(1)}, bf16[16,256]{1,0:T(8,128)(2,1)S(1)}, u32[]{:S(2)}, u32[]{:S(2)}) collective-permute-start(bf16[16,256]{1,0:T(8,128)(2,1)S(1)} %get-tuple-element.45), channel_id=1, source_target_pairs={{0,4},{4,0},{8,12},{12,8},{16,20},{20,16},{24,28},{28,24},{32,36},... | collective-permute-start | bytes 24584 | tf_op jit(solution)/shard_map/ppermute | solution.py:405
  43.7 11.0 %collective-permute-start.3 = (bf16[16,256]{1,0:T(8,128)(2,1)S(1)}, bf16[16,256]{1,0:T(8,128)(2,1)S(1)}, u32[]{:S(2)}, u32[]{:S(2)}) collective-permute-start(bf16[16,256]{1,0:T(8,128)(2,1)S(1)} %get-tuple-element.46), channel_id=1, source_target_pairs={{0,124},{4,8},{8,4},{12,16},{16,12},{20,24},{24,20},{28,32},{32,28... | collective-permute-start | bytes 24584 | tf_op jit(solution)/shard_map/ppermute | solution.py:406
  59.6 15.7 %all-to-all-start.3 = ((bf16[64,16,256]{2,1,0:T(8,128)(2,1)}), bf16[64,16,256]{2,1,0:T(8,128)(2,1)S(1)}, u32[]{:S(2)}, u32[]{:S(2)}) async-start(bf16[64,16,256]{2,1,0:T(8,128)(2,1)} %get-tuple-element.51), calls=%async_computation.3 | async-start | bytes 1048576 | tf_op jit(solution)/shard_map/all_to_all | solution.py:30
  63.5 11.1 %collective-permute-start.4 = (bf16[16,256]{1,0:T(8,128)(2,1)S(1)}, bf16[16,256]{1,0:T(8,128)(2,1)S(1)}, u32[]{:S(2)}, u32[]{:S(2)}) collective-permute-start(bf16[16,256]{1,0:T(8,128)(2,1)S(1)} %get-tuple-element.52), channel_id=1, source_target_pairs={{0,4},{4,0},{8,12},{12,8},{16,20},{20,16},{24,28},{28,24},{32,36},... | collective-permute-start | bytes 24584 | tf_op jit(solution)/shard_map/ppermute | solution.py:405
  63.7 11.0 %collective-permute-start.5 = (bf16[16,256]{1,0:T(8,128)(2,1)S(1)}, bf16[16,256]{1,0:T(8,128)(2,1)S(1)}, u32[]{:S(2)}, u32[]{:S(2)}) collective-permute-start(bf16[16,256]{1,0:T(8,128)(2,1)S(1)} %get-tuple-element.53), channel_id=1, source_target_pairs={{0,124},{4,8},{8,4},{12,16},{16,12},{20,24},{24,20},{28,32},{32,28... | collective-permute-start | bytes 24584 | tf_op jit(solution)/shard_map/ppermute | solution.py:406
  79.6 15.7 %all-to-all-start.4 = ((bf16[64,16,256]{2,1,0:T(8,128)(2,1)}), bf16[64,16,256]{2,1,0:T(8,128)(2,1)S(1)}, u32[]{:S(2)}, u32[]{:S(2)}) async-start(bf16[64,16,256]{2,1,0:T(8,128)(2,1)} %get-tuple-element.58), calls=%async_computation.4 | async-start | bytes 1048576 | tf_op jit(solution)/shard_map/all_to_all | solution.py:30
  83.5 11.3 %collective-permute-start.6 = (bf16[16,256]{1,0:T(8,128)(2,1)S(1)}, bf16[16,256]{1,0:T(8,128)(2,1)S(1)}, u32[]{:S(2)}, u32[]{:S(2)}) collective-permute-start(bf16[16,256]{1,0:T(8,128)(2,1)S(1)} %get-tuple-element.59), channel_id=1, source_target_pairs={{0,4},{4,0},{8,12},{12,8},{16,20},{20,16},{24,28},{28,24},{32,36},... | collective-permute-start | bytes 24584 | tf_op jit(solution)/shard_map/ppermute | solution.py:405
  84.0 10.9 %collective-permute-start.7 = (bf16[16,256]{1,0:T(8,128)(2,1)S(1)}, bf16[16,256]{1,0:T(8,128)(2,1)S(1)}, u32[]{:S(2)}, u32[]{:S(2)}) collective-permute-start(bf16[16,256]{1,0:T(8,128)(2,1)S(1)} %get-tuple-element.60), channel_id=1, source_target_pairs={{0,124},{4,8},{8,4},{12,16},{16,12},{20,24},{24,20},{28,32},{32,28... | collective-permute-start | bytes 24584 | tf_op jit(solution)/shard_map/ppermute | solution.py:406
  99.7 0.8 copy-start.2
  100.5 19.4 %all-to-all-start.5 = ((bf16[64,16,256]{2,1,0:T(8,128)(2,1)}), bf16[64,16,256]{2,1,0:T(8,128)(2,1)S(1)}, u32[]{:S(2)}, u32[]{:S(2)}) async-start(bf16[64,16,256]{2,1,0:T(8,128)(2,1)} %get-tuple-element.63), calls=%async_computation.5 | async-start | bytes 1048576 | tf_op jit(solution)/shard_map/all_to_all | solution.py:30
  104.4 19.3 %collective-permute-start.10 = (bf16[16,8192]{1,0:T(8,128)(2,1)S(1)}, bf16[16,8192]{1,0:T(8,128)(2,1)S(1)}, u32[]{:S(2)}, u32[]{:S(2)}) collective-permute-start(bf16[16,8192]{1,0:T(8,128)(2,1)S(1)} %get-tuple-element.67.x_ref.refs_0_), channel_id=1, source_target_pairs={{0,3},{1,0},{2,1},{3,2},{4,7},{5,4},{6,5},{7,6},{8,11},{9,8},{10,9... | collective-permute-start | bytes 786440 | tf_op jit(solution)/shard_map/ppermute | solution.py:412
  107.2 16.5 %collective-permute-start.9 = (bf16[16,8192]{1,0:T(8,128)(2,1)S(1)}, bf16[16,8192]{1,0:T(8,128)(2,1)S(1)}, u32[]{:S(2)}, u32[]{:S(2)}) collective-permute-start(bf16[16,8192]{1,0:T(8,128)(2,1)S(1)} %get-tuple-element.67.x_ref.refs_0_), channel_id=1, source_target_pairs={{0,2},{1,3},{2,0},{3,1},{4,6},{5,7},{6,4},{7,5},{8,10},{9,11},{10,... | collective-permute-start | bytes 786440 | tf_op jit(solution)/shard_map/ppermute | solution.py:412
  108.0 15.7 %collective-permute-start.8 = (bf16[16,8192]{1,0:T(8,128)(2,1)S(1)}, bf16[16,8192]{1,0:T(8,128)(2,1)S(1)}, u32[]{:S(2)}, u32[]{:S(2)}) collective-permute-start(bf16[16,8192]{1,0:T(8,128)(2,1)S(1)} %get-tuple-element.67.x_ref.refs_0_), channel_id=1, source_target_pairs={{0,1},{1,2},{2,3},{3,0},{4,5},{5,6},{6,7},{7,4},{8,9},{9,10},{10,1... | collective-permute-start | bytes 786440 | tf_op jit(solution)/shard_map/ppermute | solution.py:412
  108.9 11.0 %collective-permute-start.11 = (bf16[16,256]{1,0:T(8,128)(2,1)S(1)}, bf16[16,256]{1,0:T(8,128)(2,1)S(1)}, u32[]{:S(2)}, u32[]{:S(2)}) collective-permute-start(bf16[16,256]{1,0:T(8,128)(2,1)S(1)} %get-tuple-element.64), channel_id=1, source_target_pairs={{0,4},{4,0},{8,12},{12,8},{16,20},{20,16},{24,28},{28,24},{32,36},... | collective-permute-start | bytes 24584 | tf_op jit(solution)/shard_map/ppermute | solution.py:413
  108.9 40.7 %copy-start.3 = (f32[16,8192]{1,0:T(8,128)S(1)}, f32[16,8192]{1,0:T(8,128)}, u32[]{:S(2)}) copy-start(f32[16,8192]{1,0:T(8,128)} %copy-done.2) | copy-start | bytes 1572868
  108.9 11.0 %collective-permute-start.12 = (bf16[16,256]{1,0:T(8,128)(2,1)S(1)}, bf16[16,256]{1,0:T(8,128)(2,1)S(1)}, u32[]{:S(2)}, u32[]{:S(2)}) collective-permute-start(bf16[16,256]{1,0:T(8,128)(2,1)S(1)} %get-tuple-element.65), channel_id=1, source_target_pairs={{0,124},{4,8},{8,4},{12,16},{16,12},{20,24},{24,20},{28,32},{32,28... | collective-permute-start | bytes 24584 | tf_op jit(solution)/shard_map/ppermute | solution.py:414

commit v5 on v4

--- a/solution.py
+++ b/solution.py
@@ -12,6 +12,7 @@
 GROUPS = 4
 AHEAD = 8
 LATER = 2
+PIVOTS = 8
 STEP = 0.2
 NT = (((1,), (1,)), ((), ()))
 NN = (((1,), (0,)), ((), ()))
@@ -141,7 +142,7 @@
         send_ref[s] = x_ref[:, pl.ds(at, size)]
 
 
-def far_kernel(rows, size, odd_ref, want_ref, loc_ref, t_ref, recv_ref, pair_ref, other_ref, far_ref, blocks_ref,
+def far_kernel(rows, size, last_one, odd_ref, want_ref, loc_ref, t_ref, recv_ref, pair_ref, other_ref, far_ref, blocks_ref,
                w_ref, x_ref, send_ref, to_pair_ref, to_other_ref, held_ref, edge_ref, sems):
     wait = stream_far(blocks_ref, held_ref, edge_ref, sems)
     for b in block_order(rows):
@@ -150,27 +151,28 @@
         acc = far_sum(b, rows, odd_ref, loc_ref, recv_ref, pair_ref, other_ref, edge_ref, block)
         at = pl.ds(b * size, size)
         new = t_ref[:, at] + STEP * acc
-        w_ref[:, at] = new
-        x_ref[:, at] = new.astype(BF)
+        rounded = new.astype(BF)
+        x_ref[:, at] = rounded
+        w_ref[:, at] = (new - rounded.astype(F32)).astype(BF) if last_one else new
     last = (rows - 1) * size
     to_pair_ref[...] = x_ref[:, pl.ds(pl.multiple_of((1 - odd_ref[0]) * last, size), size)]
     to_other_ref[...] = x_ref[:, pl.ds(pl.multiple_of(odd_ref[0] * last, size), size)]
     pack(want_ref, x_ref, send_ref, size)
 
 
-def far_part(odd, want, loc, t, recv, pair, other, far, blocks):
+def far_part(odd, want, loc, t, recv, pair, other, far, blocks, last_one):
     width, states = t.shape
     size = far.shape[2]
     rows = states // size
     shapes = [
-        jax.ShapeDtypeStruct((width, states), F32),
+        jax.ShapeDtypeStruct((width, states), BF if last_one else F32),
         jax.ShapeDtypeStruct((width, states), BF),
         jax.ShapeDtypeStruct(recv.shape, BF),
         jax.ShapeDtypeStruct((width, size), BF),
         jax.ShapeDtypeStruct((width, size), BF),
     ]
     return pl.pallas_call(
-        functools.partial(far_kernel, rows, size),
+        functools.partial(far_kernel, rows, size, last_one),
         out_shape=shapes,
         in_specs=[SMEM] * 3 + [VMEM] * 5 + [HBM],
         out_specs=[VMEM] * len(shapes),
@@ -272,29 +274,34 @@
     work = jnp.concatenate([gram, unit[:, n:]], axis=1)
     slabs = [work[i:i + high] for i in range(0, n, high)]
     within = lax.broadcasted_iota(jnp.int32, (high, 1), 0)
-    for j in range(0, n, 2):
+    for j in range(0, n, PIVOTS):
         at, place = divmod(j, high)
-        ones = [jnp.broadcast_to(slabs[i][:, j:j + 1], (high, 2 * n)) for i in range(at, n // high)]
-        twos = [jnp.broadcast_to(slabs[i][:, j + 1:j + 2], (high, 2 * n)) for i in range(at, n // high)]
-        first, second = slabs[at][place:place + 1], slabs[at][place + 1:place + 2]
-        over = 1.0 / ones[0][place:place + 1]
-        beside = ones[0][place + 1:place + 2]
-        ratio = beside * over
-        over_next = 1.0 / (twos[0][place + 1:place + 2] - beside * ratio)
-        scaled = first * over
-        scaled_next = (second - beside * scaled) * over_next
-        for i in range(at, n // high):
-            one, two = ones[i - at], twos[i - at] - ones[i - at] * ratio
-            if i == at:
-                one = jnp.where(within > place, one, 0.0)
-                two = jnp.where(within > place + 1, two, 0.0)
-            slabs[i] = slabs[i] - one * scaled - two * scaled_next
+        count = n // high - at
+        columns = [
+            [jnp.broadcast_to(slabs[at + i][:, j + m:j + m + 1], (high, 2 * n)) for i in range(count)]
+            for m in range(PIVOTS)
+        ]
+        rows = [slabs[at][place + m:place + m + 1] for m in range(PIVOTS)]
+        for m in range(PIVOTS):
+            column = columns[m]
+            over = 1.0 / column[0][place + m:place + m + 1]
+            rows[m] = rows[m] * over
+            for k in range(m + 1, PIVOTS):
+                rows[k] = rows[k] - column[0][place + k:place + k + 1] * rows[m]
+                ratio = columns[k][0][place + m:place + m + 1] * over
+                columns[k] = [c - d * ratio for c, d in zip(columns[k], column)]
+        for i in range(count):
+            for m in range(PIVOTS):
+                column = columns[m][i]
+                if i == 0:
+                    column = jnp.where(within > place + m, column, 0.0)
+                slabs[at + i] = slabs[at + i] - column * rows[m]
     work = jnp.concatenate(slabs, axis=0)
     pivots = jnp.sum(jnp.where(lane == row_id, work, 0.0), axis=1, keepdims=True)
     return work[:, n:] * lax.rsqrt(pivots)
 
 
-def finish_kernel(scale, own_ref, parts_ref, all_ref, w_ref, out_ref, ritz_ref, inv_ref):
+def finish_kernel(scale, own_ref, parts_ref, all_ref, low_ref, out_ref, ritz_ref, inv_ref):
     groups, width, _ = all_ref.shape
     modes = groups * width
     half = width // 2
@@ -321,14 +328,12 @@
     small = within.astype(BF)
     for first, w in strips(all_ref, 1024):
         at = pl.ds(first, w.shape[1])
-        own = w_ref[:, at]
-        low = (own - own.astype(BF).astype(F32)).astype(BF)
         acc = dot(left, jnp.concatenate([w, w], axis=0), NN)
-        out_ref[:, at] = acc + dot(small, low, NN)
-
-
-def finish(own, parts, everyone, w, scale):
-    width, states = w.shape
+        out_ref[:, at] = acc + dot(small, low_ref[:, at], NN)
+
+
+def finish(own, parts, everyone, low, scale):
+    width, states = low.shape
     modes = everyone.shape[0] * width
     return pl.pallas_call(
         functools.partial(finish_kernel, scale),
@@ -338,7 +343,7 @@
         scratch_shapes=[pltpu.VMEM((modes, modes), F32)],
         compiler_params=pltpu.CompilerParams(vmem_limit_bytes=16 << 20),
         cost_estimate=pl.CostEstimate(flops=1 << 30, bytes_accessed=16 << 20, transcendentals=0),
-    )(own, parts, everyone, w)
+    )(own, parts, everyone, low)
 
 
 def ask_kernel(rows, far_ref, o_ref):
@@ -400,12 +405,14 @@
     to_pair = lax.dynamic_slice_in_dim(x, (1 - odd) * last, size, 1)
     to_other = lax.dynamic_slice_in_dim(x, odd * last, size, 1)
     odd = odd.reshape(1)
-    for _ in range(ITERS):
+    for step in range(ITERS):
         recv = exchange(send, "rows")
         pair = lax.ppermute(to_pair, "rows", pairs)
         other = lax.ppermute(to_other, "rows", others)
         t, far = local_part(blocks, x, w)
-        w, x, send, to_pair, to_other = far_part(odd, want, loc, t, recv, pair, other, far, blocks)
+        w, x, send, to_pair, to_other = far_part(
+            odd, want, loc, t, recv, pair, other, far, blocks, step == ITERS - 1
+        )
     recv = exchange(send, "rows")
     pieces = [x]
     for k in range(1, groups):

time: 156 us -> 154 us (0.987)
  Pallas kernels: 57.6 us -> 56 us
    pallas_call x1, Pallas kernels: 4.82 us -> 3.18 us  [finish(): pl.pallas_call(functools.partial(finish_kernel, scale), out_shape=[jax.Sh...]
where the time goes in v5:
time: 154 us; the launch traced here: 152 us
  starting transfers between devices  59.1 us (38%)
  Pallas kernels  56 us (36%)
  blocking collectives  25.3 us (16%)
  waiting for transfers between devices  6.91 us (4%)
  other arithmetic  1.99 us (1%)
  local copies, waits for them, and re-layouts  1.8 us (1%)
    pallas_call x5, Pallas kernels, local_part(): pl.pallas_call(functools.partial(local_kernel, rows, size, not w), out_sh...  28.4 us
    all_to_all x6, starting transfers between devices, exchange(): return lax.all_to_all(x, axes, split_axis=0, concat_axis=0, tiled=True)  27.9 us
    ppermute x5, starting transfers between devices, body(): other = lax.ppermute(to_other, 'rows', others)  25.8 us
    all_to_all x1, blocking collectives, exchange(): return lax.all_to_all(x, axes, split_axis=0, concat_axis=0, tiled=True)  25.3 us
    pallas_call x4, Pallas kernels, far_part(): pl.pallas_call(functools.partial(far_kernel, rows, size, last_one), out_s...  17.4 us
    all_to_all x6, waiting for transfers between devices, exchange(): return lax.all_to_all(x, axes, split_axis=0, concat_axis=0, tiled=True)  6.59 us
    ppermute x3, starting transfers between devices, body(): lax.ppermute(x, 'cols', [(i, (i + k) % groups) for i in range(groups)])  4.51 us
    pallas_call x1, Pallas kernels, applied(): pl.pallas_call(functools.partial(applied_kernel, rows, size), out_shape=j...  3.77 us
  transfers between devices with their start and end apart: 19, of which 7 were waited for; matrix products, arithmetic and copies ran while one was open for 1% of the time, Pallas kernels for 22%

profile of v5, /device:TPU:0, one launch (start us, length us, event | category | flops | bytes accessed | tf_op | source)
XLA Modules:
  0.0 152.0 jit_solution(10313761916082009260)
XLA Ops:
  1.3 0.8 shard_map.50
  2.1 8.4 %all-to-all-start = ((s32[32,1,128]{2,1,0:T(1,128)}), s32[32,1,128]{2,1,0:T(1,128)S(1)}, u32[]{:S(2)}, u32[]{:S(2)}) async-start(s32[32,1,128]{2,1,0:T(1,128)} %bitcast.3), calls=%async_computation | async-start | bytes 32768 | tf_op jit(solution)/shard_map/all_to_all | solution.py:31
  10.5 1.1 convert_element_type.7.x_ref
  11.6 5.0 %collective-permute-start.1 = (bf16[16,256]{1,0:T(8,128)(2,1)S(1)}, bf16[16,256]{1,0:T(8,128)(2,1)S(1)}, u32[]{:S(2)}, u32[]{:S(2)}) collective-permute-start(bf16[16,256]{1,0:T(8,128)(2,1)S(1)} %get-tuple-element.76), channel_id=1, source_target_pairs={{0,124},{4,8},{8,4},{12,16},{16,12},{20,24},{24,20},{28,32},{32,28... | collective-permute-start | bytes 24584 | tf_op jit(solution)/shard_map/ppermute | solution.py:411
  16.6 1.1 all-to-all-done.answer_ref
  17.8 1.8 %shard_map.52 = bf16[64,16,256]{2,1,0:T(8,128)(2,1)} custom-call(s32[32,1,128]{2,1,0:T(1,128)S(1)} %all-to-all-done.answer_ref, bf16[16,8192]{1,0:T(8,128)(2,1)S(1)} %convert_element_type.7.x_ref), custom_call_target="tpu_custom_call" | custom-call | tf_op jit(solution)/shard_map/pallas_call | solution.py:397
  19.5 3.9 %all-to-all-start.1 = ((bf16[64,16,256]{2,1,0:T(8,128)(2,1)}), bf16[64,16,256]{2,1,0:T(8,128)(2,1)S(1)}, u32[]{:S(2)}, u32[]{:S(2)}) async-start(bf16[64,16,256]{2,1,0:T(8,128)(2,1)} %shard_map.52), calls=%async_computation.1 | async-start | bytes 1048576 | tf_op jit(solution)/shard_map/all_to_all | solution.py:31
  24.1 1.0 copy-done
  25.1 5.7 %shard_map.51 = (f32[16,8192]{1,0:T(8,128)S(1)}, bf16[8,256,256]{2,1,0:T(8,128)(2,1)S(1)}) custom-call(bf16[16,8192]{1,0:T(8,128)(2,1)S(1)} %convert_element_type.7.x_ref, f32[16,8192]{1,0:T(8,128)S(1)} %copy-done, bf16[32,4,256,256]{3,2,1,0:T(8,128)(2,1)} %blocks_ref.9), custom_call_target="tpu_custom_call" | custom-call | flops 201326592 | bytes 12582912 | tf_op jit(solution)/shard_map/pallas_call | solution.py:77
  31.2 4.0 %all-to-all-done.1.recv_ref = bf16[64,16,256]{2,1,0:T(8,128)(2,1)S(1)} async-done(((bf16[64,16,256]{2,1,0:T(8,128)(2,1)}), bf16[64,16,256]{2,1,0:T(8,128)(2,1)S(1)}, u32[]{:S(2)}, u32[]{:S(2)}) %all-to-all-start.1) | async-done | bytes 524320 | tf_op jit(solution)/shard_map/all_to_all | solution.py:31
  35.2 4.4 %shard_map.53 = (f32[16,8192]{1,0:T(8,128)S(1)}, bf16[16,8192]{1,0:T(8,128)(2,1)S(1)}, bf16[64,16,256]{2,1,0:T(8,128)(2,1)}, bf16[16,256]{1,0:T(8,128)(2,1)S(1)}, bf16[16,256]{1,0:T(8,128)(2,1)S(1)}) custom-call(s32[1]{0:T(128)} %bitcast.1.odd_ref, s32[64]{0:T(128)S(1)} %min.20.want_ref, s32[32]{0:T(128)S(1)} %add_clamp_fusion.loc_ref, ...), custom_call_target="tpu_custom_call" | custom-call | flops 67108864 | bytes 4194304 | tf_op jit(solution)/shard_map/pallas_call | solution.py:174
  39.6 3.9 %all-to-all-start.2 = ((bf16[64,16,256]{2,1,0:T(8,128)(2,1)}), bf16[64,16,256]{2,1,0:T(8,128)(2,1)S(1)}, u32[]{:S(2)}, u32[]{:S(2)}) async-start(bf16[64,16,256]{2,1,0:T(8,128)(2,1)} %get-tuple-element.44), calls=%async_computation.2 | async-start | bytes 1048576 | tf_op jit(solution)/shard_map/all_to_all | solution.py:31
  43.7 5.1 %collective-permute-start.3 = (bf16[16,256]{1,0:T(8,128)(2,1)S(1)}, bf16[16,256]{1,0:T(8,128)(2,1)S(1)}, u32[]{:S(2)}, u32[]{:S(2)}) collective-permute-start(bf16[16,256]{1,0:T(8,128)(2,1)S(1)} %get-tuple-element.46), channel_id=1, source_target_pairs={{0,124},{4,8},{8,4},{12,16},{16,12},{20,24},{24,20},{28,32},{32,28... | collective-permute-start | bytes 24584 | tf_op jit(solution)/shard_map/ppermute | solution.py:411
  48.9 5.7 %shard_map.54 = (f32[16,8192]{1,0:T(8,128)S(1)}, bf16[8,256,256]{2,1,0:T(8,128)(2,1)S(1)}) custom-call(bf16[16,8192]{1,0:T(8,128)(2,1)S(1)} %get-tuple-element.41.x_ref, f32[16,8192]{1,0:T(8,128)S(1)} %get-tuple-element.42.refs_0_, bf16[32,4,256,256]{3,2,1,0:T(8,128)(2,1)} %blocks_ref.9), custom_call_target="tpu_custom_call" | custom-call | flops 201326592 | bytes 12582912 | tf_op jit(solution)/shard_map/pallas_call | solution.py:77
  55.2 4.4 %shard_map.55 = (f32[16,8192]{1,0:T(8,128)S(1)}, bf16[16,8192]{1,0:T(8,128)(2,1)S(1)}, bf16[64,16,256]{2,1,0:T(8,128)(2,1)}, bf16[16,256]{1,0:T(8,128)(2,1)S(1)}, bf16[16,256]{1,0:T(8,128)(2,1)S(1)}) custom-call(s32[1]{0:T(128)} %bitcast.1.odd_ref, s32[64]{0:T(128)S(1)} %min.20.want_ref, s32[32]{0:T(128)S(1)} %add_clamp_fusion.loc_ref, ...), custom_call_target="tpu_custom_call" | custom-call | flops 67108864 | bytes 4194304 | tf_op jit(solution)/shard_map/pallas_call | solution.py:174
  59.6 3.9 %all-to-all-start.3 = ((bf16[64,16,256]{2,1,0:T(8,128)(2,1)}), bf16[64,16,256]{2,1,0:T(8,128)(2,1)S(1)}, u32[]{:S(2)}, u32[]{:S(2)}) async-start(bf16[64,16,256]{2,1,0:T(8,128)(2,1)} %get-tuple-element.51), calls=%async_computation.3 | async-start | bytes 1048576 | tf_op jit(solution)/shard_map/all_to_all | solution.py:31
  63.7 5.1 %collective-permute-start.5 = (bf16[16,256]{1,0:T(8,128)(2,1)S(1)}, bf16[16,256]{1,0:T(8,128)(2,1)S(1)}, u32[]{:S(2)}, u32[]{:S(2)}) collective-permute-start(bf16[16,256]{1,0:T(8,128)(2,1)S(1)} %get-tuple-element.53), channel_id=1, source_target_pairs={{0,124},{4,8},{8,4},{12,16},{16,12},{20,24},{24,20},{28,32},{32,28... | collective-permute-start | bytes 24584 | tf_op jit(solution)/shard_map/ppermute | solution.py:411
  68.9 5.7 %shard_map.56 = (f32[16,8192]{1,0:T(8,128)S(1)}, bf16[8,256,256]{2,1,0:T(8,128)(2,1)S(1)}) custom-call(bf16[16,8192]{1,0:T(8,128)(2,1)S(1)} %get-tuple-element.48.x_ref, f32[16,8192]{1,0:T(8,128)S(1)} %get-tuple-element.49.refs_0_, bf16[32,4,256,256]{3,2,1,0:T(8,128)(2,1)} %blocks_ref.9), custom_call_target="tpu_custom_call" | custom-call | flops 201326592 | bytes 12582912 | tf_op jit(solution)/shard_map/pallas_call | solution.py:77
  75.3 4.4 %shard_map.57 = (f32[16,8192]{1,0:T(8,128)S(1)}, bf16[16,8192]{1,0:T(8,128)(2,1)S(1)}, bf16[64,16,256]{2,1,0:T(8,128)(2,1)}, bf16[16,256]{1,0:T(8,128)(2,1)S(1)}, bf16[16,256]{1,0:T(8,128)(2,1)S(1)}) custom-call(s32[1]{0:T(128)} %bitcast.1.odd_ref, s32[64]{0:T(128)S(1)} %min.20.want_ref, s32[32]{0:T(128)S(1)} %add_clamp_fusion.loc_ref, ...), custom_call_target="tpu_custom_call" | custom-call | flops 67108864 | bytes 4194304 | tf_op jit(solution)/shard_map/pallas_call | solution.py:174
  79.6 3.9 %all-to-all-start.4 = ((bf16[64,16,256]{2,1,0:T(8,128)(2,1)}), bf16[64,16,256]{2,1,0:T(8,128)(2,1)S(1)}, u32[]{:S(2)}, u32[]{:S(2)}) async-start(bf16[64,16,256]{2,1,0:T(8,128)(2,1)} %get-tuple-element.58), calls=%async_computation.4 | async-start | bytes 1048576 | tf_op jit(solution)/shard_map/all_to_all | solution.py:31
  84.0 5.1 %collective-permute-start.7 = (bf16[16,256]{1,0:T(8,128)(2,1)S(1)}, bf16[16,256]{1,0:T(8,128)(2,1)S(1)}, u32[]{:S(2)}, u32[]{:S(2)}) collective-permute-start(bf16[16,256]{1,0:T(8,128)(2,1)S(1)} %get-tuple-element.60), channel_id=1, source_target_pairs={{0,124},{4,8},{8,4},{12,16},{16,12},{20,24},{24,20},{28,32},{32,28... | collective-permute-start | bytes 24584 | tf_op jit(solution)/shard_map/ppermute | solution.py:411
  89.1 5.7 %shard_map.58 = (f32[16,8192]{1,0:T(8,128)S(1)}, bf16[8,256,256]{2,1,0:T(8,128)(2,1)S(1)}) custom-call(bf16[16,8192]{1,0:T(8,128)(2,1)S(1)} %get-tuple-element.55.x_ref, f32[16,8192]{1,0:T(8,128)S(1)} %get-tuple-element.56.refs_0_, bf16[32,4,256,256]{3,2,1,0:T(8,128)(2,1)} %blocks_ref.9), custom_call_target="tpu_custom_call" | custom-call | flops 201326592 | bytes 12582912 | tf_op jit(solution)/shard_map/pallas_call | solution.py:77
  95.3 4.4 %shard_map.59 = (bf16[16,8192]{1,0:T(8,128)(2,1)S(1)}, bf16[16,8192]{1,0:T(8,128)(2,1)S(1)}, bf16[64,16,256]{2,1,0:T(8,128)(2,1)}, bf16[16,256]{1,0:T(8,128)(2,1)S(1)}, bf16[16,256]{1,0:T(8,128)(2,1)S(1)}) custom-call(s32[1]{0:T(128)} %bitcast.1.odd_ref, s32[64]{0:T(128)S(1)} %min.20.want_ref, s32[32]{0:T(128)S(1)} %add_clamp_fusion.loc_ref, ...), custom_call_target="tpu_custom_call" | custom-call | flops 67108864 | bytes 4194304 | tf_op jit(solution)/shard_map/pallas_call | solution.py:174
  99.7 3.9 %all-to-all-start.5 = ((bf16[64,16,256]{2,1,0:T(8,128)(2,1)}), bf16[64,16,256]{2,1,0:T(8,128)(2,1)S(1)}, u32[]{:S(2)}, u32[]{:S(2)}) async-start(bf16[64,16,256]{2,1,0:T(8,128)(2,1)} %get-tuple-element.63), calls=%async_computation.5 | async-start | bytes 1048576 | tf_op jit(solution)/shard_map/all_to_all | solution.py:31
  103.6 2.8 %collective-permute-start.10 = (bf16[16,8192]{1,0:T(8,128)(2,1)S(1)}, bf16[16,8192]{1,0:T(8,128)(2,1)S(1)}, u32[]{:S(2)}, u32[]{:S(2)}) collective-permute-start(bf16[16,8192]{1,0:T(8,128)(2,1)S(1)} %get-tuple-element.67.x_ref.refs_0_), channel_id=1, source_target_pairs={{0,3},{1,0},{2,1},{3,2},{4,7},{5,4},{6,5},{7,6},{8,11},{9,8},{10,9... | collective-permute-start | bytes 786440 | tf_op jit(solution)/shard_map/ppermute | solution.py:419
  106.4 0.8 collective-permute-start.9
  107.2 0.9 collective-permute-start.8
  108.1 5.3 %collective-permute-start.12 = (bf16[16,256]{1,0:T(8,128)(2,1)S(1)}, bf16[16,256]{1,0:T(8,128)(2,1)S(1)}, u32[]{:S(2)}, u32[]{:S(2)}) collective-permute-start(bf16[16,256]{1,0:T(8,128)(2,1)S(1)} %get-tuple-element.65), channel_id=1, source_target_pairs={{0,124},{4,8},{8,4},{12,16},{16,12},{20,24},{24,20},{28,32},{32,28... | collective-permute-start | bytes 24584 | tf_op jit(solution)/shard_map/ppermute | solution.py:421
  113.4 5.7 %shard_map.60.t_ref = f32[16,8192]{1,0:T(8,128)S(1)} custom-call(bf16[16,8192]{1,0:T(8,128)(2,1)S(1)} %get-tuple-element.67.x_ref.refs_0_, bf16[32,4,256,256]{3,2,1,0:T(8,128)(2,1)} %blocks_ref.9), custom_call_target="tpu_custom_call" | custom-call | flops 201326592 | bytes 12582912 | tf_op jit(solution)/shard_map/pallas_call | solution.py:77
  119.1 3.8 %shard_map.61.z_ref = bf16[32,8192]{1,0:T(8,128)(2,1)S(1)} custom-call(s32[1]{0:T(128)} %bitcast.1.odd_ref, s32[32]{0:T(128)S(1)} %add_clamp_fusion.loc_ref, f32[16,8192]{1,0:T(8,128)S(1)} %shard_map.60.t_ref, bf16[64,16,256]{2,1,0:T(8,128)(2,1)S(1)} %all-to-all-done.5.recv_ref, bf16[16,256]{1,0:T(8,128)(2,1)S(1)} %collective-permute-done.11.pair_ref, ...), custom_call_target="tpu_custom_call" | custom-call | flops 67108864 | bytes 4194304 | tf_op jit(solution)/shard_map/pallas_call | solution.py:205
  123.6 25.3 %all_to_all.35.parts_ref = f32[128,16,128]{2,1,0:T(8,128)S(1)} all-to-all(f32[128,16,128]{2,1,0:T(8,128)S(1)} %get-tuple-element.71), channel_id=1, replica_groups=mesh['rows'=32,'cols'=4] {'rows','cols'}, dimensions={0} | all-to-all | bytes 2097152 | tf_op jit(solution)/shard_map/all_to_all | solution.py:31
  148.8 3.2 %shard_map.63 = (f32[16,8192]{1,0:T(8,128)}, f32[16,64]{1,0:T(8,128)}) custom-call(s32[1]{0:T(128)} %bitcast.own_ref, f32[128,16,128]{2,1,0:T(8,128)S(1)} %all_to_all.35.parts_ref, bf16[4,16,8192]{2,1,0:T(8,128)(2,1)S(1)} %get-tuple-element.72.all_ref, bf16[16,8192]{1,0:T(8,128)(2,1)S(1)} %get-tuple-element.73.low_ref), custom_call_target="tpu_custom_call" | custom-call | flops 1073741824 | bytes 16777216 | tf_op jit(solution)/shard_map/pallas_call | solution.py:338
  (32 shorter events, 5.0 us)
Async XLA Ops:
  0.6 0.7 copy-start.1
  2.1 15.7 %all-to-all-start = ((s32[32,1,128]{2,1,0:T(1,128)}), s32[32,1,128]{2,1,0:T(1,128)S(1)}, u32[]{:S(2)}, u32[]{:S(2)}) async-start(s32[32,1,128]{2,1,0:T(1,128)} %bitcast.3), calls=%async_computation | async-start | bytes 32768 | tf_op jit(solution)/shard_map/all_to_all | solution.py:31
  11.6 19.6 %collective-permute-start.1 = (bf16[16,256]{1,0:T(8,128)(2,1)S(1)}, bf16[16,256]{1,0:T(8,128)(2,1)S(1)}, u32[]{:S(2)}, u32[]{:S(2)}) collective-permute-start(bf16[16,256]{1,0:T(8,128)(2,1)S(1)} %get-tuple-element.76), channel_id=1, source_target_pairs={{0,124},{4,8},{8,4},{12,16},{16,12},{20,24},{24,20},{28,32},{32,28... | collective-permute-start | bytes 24584 | tf_op jit(solution)/shard_map/ppermute | solution.py:411
  16.6 14.6 %collective-permute-start = (bf16[16,256]{1,0:T(8,128)(2,1)S(1)}, bf16[16,256]{1,0:T(8,128)(2,1)S(1)}, u32[]{:S(2)}, u32[]{:S(2)}) collective-permute-start(bf16[16,256]{1,0:T(8,128)(2,1)S(1)} %get-tuple-element.77), channel_id=1, source_target_pairs={{0,4},{4,0},{8,12},{12,8},{16,20},{20,16},{24,28},{28,24},{32,36},... | collective-permute-start | bytes 24584 | tf_op jit(solution)/shard_map/ppermute | solution.py:410
  19.5 15.7 %all-to-all-start.1 = ((bf16[64,16,256]{2,1,0:T(8,128)(2,1)}), bf16[64,16,256]{2,1,0:T(8,128)(2,1)S(1)}, u32[]{:S(2)}, u32[]{:S(2)}) async-start(bf16[64,16,256]{2,1,0:T(8,128)(2,1)} %shard_map.52), calls=%async_computation.1 | async-start | bytes 1048576 | tf_op jit(solution)/shard_map/all_to_all | solution.py:31
  24.1 1.0 copy-start
  39.6 15.7 %all-to-all-start.2 = ((bf16[64,16,256]{2,1,0:T(8,128)(2,1)}), bf16[64,16,256]{2,1,0:T(8,128)(2,1)S(1)}, u32[]{:S(2)}, u32[]{:S(2)}) async-start(bf16[64,16,256]{2,1,0:T(8,128)(2,1)} %get-tuple-element.44), calls=%async_computation.2 | async-start | bytes 1048576 | tf_op jit(solution)/shard_map/all_to_all | solution.py:31
  43.5 11.1 %collective-permute-start.2 = (bf16[16,256]{1,0:T(8,128)(2,1)S(1)}, bf16[16,256]{1,0:T(8,128)(2,1)S(1)}, u32[]{:S(2)}, u32[]{:S(2)}) collective-permute-start(bf16[16,256]{1,0:T(8,128)(2,1)S(1)} %get-tuple-element.45), channel_id=1, source_target_pairs={{0,4},{4,0},{8,12},{12,8},{16,20},{20,16},{24,28},{28,24},{32,36},... | collective-permute-start | bytes 24584 | tf_op jit(solution)/shard_map/ppermute | solution.py:410
  43.7 11.0 %collective-permute-start.3 = (bf16[16,256]{1,0:T(8,128)(2,1)S(1)}, bf16[16,256]{1,0:T(8,128)(2,1)S(1)}, u32[]{:S(2)}, u32[]{:S(2)}) collective-permute-start(bf16[16,256]{1,0:T(8,128)(2,1)S(1)} %get-tuple-element.46), channel_id=1, source_target_pairs={{0,124},{4,8},{8,4},{12,16},{16,12},{20,24},{24,20},{28,32},{32,28... | collective-permute-start | bytes 24584 | tf_op jit(solution)/shard_map/ppermute | solution.py:411
  59.6 15.7 %all-to-all-start.3 = ((bf16[64,16,256]{2,1,0:T(8,128)(2,1)}), bf16[64,16,256]{2,1,0:T(8,128)(2,1)S(1)}, u32[]{:S(2)}, u32[]{:S(2)}) async-start(bf16[64,16,256]{2,1,0:T(8,128)(2,1)} %get-tuple-element.51), calls=%async_computation.3 | async-start | bytes 1048576 | tf_op jit(solution)/shard_map/all_to_all | solution.py:31
  63.5 11.1 %collective-permute-start.4 = (bf16[16,256]{1,0:T(8,128)(2,1)S(1)}, bf16[16,256]{1,0:T(8,128)(2,1)S(1)}, u32[]{:S(2)}, u32[]{:S(2)}) collective-permute-start(bf16[16,256]{1,0:T(8,128)(2,1)S(1)} %get-tuple-element.52), channel_id=1, source_target_pairs={{0,4},{4,0},{8,12},{12,8},{16,20},{20,16},{24,28},{28,24},{32,36},... | collective-permute-start | bytes 24584 | tf_op jit(solution)/shard_map/ppermute | solution.py:410
  63.7 11.0 %collective-permute-start.5 = (bf16[16,256]{1,0:T(8,128)(2,1)S(1)}, bf16[16,256]{1,0:T(8,128)(2,1)S(1)}, u32[]{:S(2)}, u32[]{:S(2)}) collective-permute-start(bf16[16,256]{1,0:T(8,128)(2,1)S(1)} %get-tuple-element.53), channel_id=1, source_target_pairs={{0,124},{4,8},{8,4},{12,16},{16,12},{20,24},{24,20},{28,32},{32,28... | collective-permute-start | bytes 24584 | tf_op jit(solution)/shard_map/ppermute | solution.py:411
  79.6 15.7 %all-to-all-start.4 = ((bf16[64,16,256]{2,1,0:T(8,128)(2,1)}), bf16[64,16,256]{2,1,0:T(8,128)(2,1)S(1)}, u32[]{:S(2)}, u32[]{:S(2)}) async-start(bf16[64,16,256]{2,1,0:T(8,128)(2,1)} %get-tuple-element.58), calls=%async_computation.4 | async-start | bytes 1048576 | tf_op jit(solution)/shard_map/all_to_all | solution.py:31
  83.5 11.3 %collective-permute-start.6 = (bf16[16,256]{1,0:T(8,128)(2,1)S(1)}, bf16[16,256]{1,0:T(8,128)(2,1)S(1)}, u32[]{:S(2)}, u32[]{:S(2)}) collective-permute-start(bf16[16,256]{1,0:T(8,128)(2,1)S(1)} %get-tuple-element.59), channel_id=1, source_target_pairs={{0,4},{4,0},{8,12},{12,8},{16,20},{20,16},{24,28},{28,24},{32,36},... | collective-permute-start | bytes 24584 | tf_op jit(solution)/shard_map/ppermute | solution.py:410
  84.0 10.9 %collective-permute-start.7 = (bf16[16,256]{1,0:T(8,128)(2,1)S(1)}, bf16[16,256]{1,0:T(8,128)(2,1)S(1)}, u32[]{:S(2)}, u32[]{:S(2)}) collective-permute-start(bf16[16,256]{1,0:T(8,128)(2,1)S(1)} %get-tuple-element.60), channel_id=1, source_target_pairs={{0,124},{4,8},{8,4},{12,16},{16,12},{20,24},{24,20},{28,32},{32,28... | collective-permute-start | bytes 24584 | tf_op jit(solution)/shard_map/ppermute | solution.py:411
  99.7 19.4 %all-to-all-start.5 = ((bf16[64,16,256]{2,1,0:T(8,128)(2,1)}), bf16[64,16,256]{2,1,0:T(8,128)(2,1)S(1)}, u32[]{:S(2)}, u32[]{:S(2)}) async-start(bf16[64,16,256]{2,1,0:T(8,128)(2,1)} %get-tuple-element.63), calls=%async_computation.5 | async-start | bytes 1048576 | tf_op jit(solution)/shard_map/all_to_all | solution.py:31
  103.6 19.3 %collective-permute-start.10 = (bf16[16,8192]{1,0:T(8,128)(2,1)S(1)}, bf16[16,8192]{1,0:T(8,128)(2,1)S(1)}, u32[]{:S(2)}, u32[]{:S(2)}) collective-permute-start(bf16[16,8192]{1,0:T(8,128)(2,1)S(1)} %get-tuple-element.67.x_ref.refs_0_), channel_id=1, source_target_pairs={{0,3},{1,0},{2,1},{3,2},{4,7},{5,4},{6,5},{7,6},{8,11},{9,8},{10,9... | collective-permute-start | bytes 786440 | tf_op jit(solution)/shard_map/ppermute | solution.py:419
  106.4 16.5 %collective-permute-start.9 = (bf16[16,8192]{1,0:T(8,128)(2,1)S(1)}, bf16[16,8192]{1,0:T(8,128)(2,1)S(1)}, u32[]{:S(2)}, u32[]{:S(2)}) collective-permute-start(bf16[16,8192]{1,0:T(8,128)(2,1)S(1)} %get-tuple-element.67.x_ref.refs_0_), channel_id=1, source_target_pairs={{0,2},{1,3},{2,0},{3,1},{4,6},{5,7},{6,4},{7,5},{8,10},{9,11},{10,... | collective-permute-start | bytes 786440 | tf_op jit(solution)/shard_map/ppermute | solution.py:419
  107.2 15.7 %collective-permute-start.8 = (bf16[16,8192]{1,0:T(8,128)(2,1)S(1)}, bf16[16,8192]{1,0:T(8,128)(2,1)S(1)}, u32[]{:S(2)}, u32[]{:S(2)}) collective-permute-start(bf16[16,8192]{1,0:T(8,128)(2,1)S(1)} %get-tuple-element.67.x_ref.refs_0_), channel_id=1, source_target_pairs={{0,1},{1,2},{2,3},{3,0},{4,5},{5,6},{6,7},{7,4},{8,9},{9,10},{10,1... | collective-permute-start | bytes 786440 | tf_op jit(solution)/shard_map/ppermute | solution.py:419
  108.1 11.0 %collective-permute-start.11 = (bf16[16,256]{1,0:T(8,128)(2,1)S(1)}, bf16[16,256]{1,0:T(8,128)(2,1)S(1)}, u32[]{:S(2)}, u32[]{:S(2)}) collective-permute-start(bf16[16,256]{1,0:T(8,128)(2,1)S(1)} %get-tuple-element.64), channel_id=1, source_target_pairs={{0,4},{4,0},{8,12},{12,8},{16,20},{20,16},{24,28},{28,24},{32,36},... | collective-permute-start | bytes 24584 | tf_op jit(solution)/shard_map/ppermute | solution.py:420
  108.1 11.0 %collective-permute-start.12 = (bf16[16,256]{1,0:T(8,128)(2,1)S(1)}, bf16[16,256]{1,0:T(8,128)(2,1)S(1)}, u32[]{:S(2)}, u32[]{:S(2)}) collective-permute-start(bf16[16,256]{1,0:T(8,128)(2,1)S(1)} %get-tuple-element.65), channel_id=1, source_target_pairs={{0,124},{4,8},{8,4},{12,16},{16,12},{20,24},{24,20},{28,32},{32,28... | collective-permute-start | bytes 24584 | tf_op jit(solution)/shard_map/ppermute | solution.py:421

commit v6 on v5

--- a/solution.py
+++ b/solution.py
@@ -357,11 +357,8 @@
     o_ref[...] = jnp.where(lane == 0, first, second)
 
 
-def first_pack_kernel(size, rows, answer_ref, x_ref, send_ref):
-    for s in range(send_ref.shape[0]):
-        block = jnp.clip(answer_ref[s // CAP, 0, s % CAP], 0, rows - 1)
-        at = pl.multiple_of(block * size, size)
-        send_ref[s] = x_ref[:, pl.ds(at, size)]
+def first_pack_kernel(size, want_ref, x_ref, send_ref):
+    pack(want_ref, x_ref, send_ref, size)
 
 
 def body(basis, blocks, far_cols):
@@ -395,12 +392,12 @@
     w = basis
     x = w.astype(BF)
     send = pl.pallas_call(
-        functools.partial(first_pack_kernel, size, rows),
+        functools.partial(first_pack_kernel, size),
         out_shape=jax.ShapeDtypeStruct((devices * CAP, width, size), BF),
         in_specs=[SMEM, VMEM],
         out_specs=VMEM,
         compiler_params=pltpu.CompilerParams(vmem_limit_bytes=2 << 20),
-    )(answer, x)
+    )(want, x)
     last = states - size
     to_pair = lax.dynamic_slice_in_dim(x, (1 - odd) * last, size, 1)
     to_other = lax.dynamic_slice_in_dim(x, odd * last, size, 1)

time: 154 us -> 154 us (level)
  transfers between devices with their start and end apart: 19 -> 19, of which waited for: 7 -> 8; matrix products, arithmetic and copies ran while one was open for 1% -> 1% of each run, Pallas kernels for 22% -> 22%
where the time goes in v6:
time: 154 us; the launch traced here: 152 us
  starting transfers between devices  58.9 us (38%)
  Pallas kernels  55.6 us (36%)
  blocking collectives  25.3 us (16%)
  waiting for transfers between devices  7.26 us (5%)
  other arithmetic  1.99 us (1%)
  local copies, waits for them, and re-layouts  1.8 us (1%)
    pallas_call x5, Pallas kernels, local_part(): pl.pallas_call(functools.partial(local_kernel, rows, size, not w), out_sh...  28.4 us
    all_to_all x6, starting transfers between devices, exchange(): return lax.all_to_all(x, axes, split_axis=0, concat_axis=0, tiled=True)  27.9 us
    ppermute x5, starting transfers between devices, body(): other = lax.ppermute(to_other, 'rows', others)  25.8 us
    all_to_all x1, blocking collectives, exchange(): return lax.all_to_all(x, axes, split_axis=0, concat_axis=0, tiled=True)  25.3 us
    pallas_call x4, Pallas kernels, far_part(): pl.pallas_call(functools.partial(far_kernel, rows, size, last_one), out_s...  17.4 us
    all_to_all x6, waiting for transfers between devices, exchange(): return lax.all_to_all(x, axes, split_axis=0, concat_axis=0, tiled=True)  6.8 us
    ppermute x3, starting transfers between devices, body(): lax.ppermute(x, 'cols', [(i, (i + k) % groups) for i in range(groups)])  4.51 us
    pallas_call x1, Pallas kernels, applied(): pl.pallas_call(functools.partial(applied_kernel, rows, size), out_shape=j...  3.77 us
  transfers between devices with their start and end apart: 19, of which 8 were waited for; matrix products, arithmetic and copies ran while one was open for 1% of the time, Pallas kernels for 22%

profile of v6, /device:TPU:0, one launch (start us, length us, event | category | flops | bytes accessed | tf_op | source)
XLA Modules:
  0.0 151.8 jit_solution(13660929354090493616)
XLA Ops:
  1.3 0.8 shard_map.50
  2.1 8.4 %all-to-all-start = ((s32[32,1,128]{2,1,0:T(1,128)}), s32[32,1,128]{2,1,0:T(1,128)S(1)}, u32[]{:S(2)}, u32[]{:S(2)}) async-start(s32[32,1,128]{2,1,0:T(1,128)} %bitcast.4), calls=%async_computation | async-start | bytes 32768 | tf_op jit(solution)/shard_map/all_to_all | solution.py:31
  10.5 1.1 convert_element_type.7.x_ref
  11.6 5.0 %collective-permute-start.1 = (bf16[16,256]{1,0:T(8,128)(2,1)S(1)}, bf16[16,256]{1,0:T(8,128)(2,1)S(1)}, u32[]{:S(2)}, u32[]{:S(2)}) collective-permute-start(bf16[16,256]{1,0:T(8,128)(2,1)S(1)} %get-tuple-element.76), channel_id=1, source_target_pairs={{0,124},{4,8},{8,4},{12,16},{16,12},{20,24},{24,20},{28,32},{32,28... | collective-permute-start | bytes 24584 | tf_op jit(solution)/shard_map/ppermute | solution.py:408
  16.6 1.1 all-to-all-done
  17.9 1.4 shard_map.52
  19.4 3.9 %all-to-all-start.1 = ((bf16[64,16,256]{2,1,0:T(8,128)(2,1)}), bf16[64,16,256]{2,1,0:T(8,128)(2,1)S(1)}, u32[]{:S(2)}, u32[]{:S(2)}) async-start(bf16[64,16,256]{2,1,0:T(8,128)(2,1)} %shard_map.52), calls=%async_computation.1 | async-start | bytes 1048576 | tf_op jit(solution)/shard_map/all_to_all | solution.py:31
  24.1 1.0 copy-done
  25.2 5.7 %shard_map.51 = (f32[16,8192]{1,0:T(8,128)S(1)}, bf16[8,256,256]{2,1,0:T(8,128)(2,1)S(1)}) custom-call(bf16[16,8192]{1,0:T(8,128)(2,1)S(1)} %convert_element_type.7.x_ref, f32[16,8192]{1,0:T(8,128)S(1)} %copy-done, bf16[32,4,256,256]{3,2,1,0:T(8,128)(2,1)} %blocks_ref.9), custom_call_target="tpu_custom_call" | custom-call | flops 201326592 | bytes 12582912 | tf_op jit(solution)/shard_map/pallas_call | solution.py:77
  30.9 4.1 %all-to-all-done.1.recv_ref = bf16[64,16,256]{2,1,0:T(8,128)(2,1)S(1)} async-done(((bf16[64,16,256]{2,1,0:T(8,128)(2,1)}), bf16[64,16,256]{2,1,0:T(8,128)(2,1)S(1)}, u32[]{:S(2)}, u32[]{:S(2)}) %all-to-all-start.1) | async-done | bytes 524320 | tf_op jit(solution)/shard_map/all_to_all | solution.py:31
  35.0 4.4 %shard_map.53 = (f32[16,8192]{1,0:T(8,128)S(1)}, bf16[16,8192]{1,0:T(8,128)(2,1)S(1)}, bf16[64,16,256]{2,1,0:T(8,128)(2,1)}, bf16[16,256]{1,0:T(8,128)(2,1)S(1)}, bf16[16,256]{1,0:T(8,128)(2,1)S(1)}) custom-call(s32[1]{0:T(128)} %bitcast.1.odd_ref, s32[64]{0:T(128)S(1)} %min.20.want_ref, s32[32]{0:T(128)S(1)} %add_clamp_fusion.loc_ref, ...), custom_call_target="tpu_custom_call" | custom-call | flops 67108864 | bytes 4194304 | tf_op jit(solution)/shard_map/pallas_call | solution.py:174
  39.4 3.9 %all-to-all-start.2 = ((bf16[64,16,256]{2,1,0:T(8,128)(2,1)}), bf16[64,16,256]{2,1,0:T(8,128)(2,1)S(1)}, u32[]{:S(2)}, u32[]{:S(2)}) async-start(bf16[64,16,256]{2,1,0:T(8,128)(2,1)} %get-tuple-element.44), calls=%async_computation.2 | async-start | bytes 1048576 | tf_op jit(solution)/shard_map/all_to_all | solution.py:31
  43.5 5.1 %collective-permute-start.3 = (bf16[16,256]{1,0:T(8,128)(2,1)S(1)}, bf16[16,256]{1,0:T(8,128)(2,1)S(1)}, u32[]{:S(2)}, u32[]{:S(2)}) collective-permute-start(bf16[16,256]{1,0:T(8,128)(2,1)S(1)} %get-tuple-element.46), channel_id=1, source_target_pairs={{0,124},{4,8},{8,4},{12,16},{16,12},{20,24},{24,20},{28,32},{32,28... | collective-permute-start | bytes 24584 | tf_op jit(solution)/shard_map/ppermute | solution.py:408
  48.7 5.7 %shard_map.54 = (f32[16,8192]{1,0:T(8,128)S(1)}, bf16[8,256,256]{2,1,0:T(8,128)(2,1)S(1)}) custom-call(bf16[16,8192]{1,0:T(8,128)(2,1)S(1)} %get-tuple-element.41.x_ref, f32[16,8192]{1,0:T(8,128)S(1)} %get-tuple-element.42.refs_0_, bf16[32,4,256,256]{3,2,1,0:T(8,128)(2,1)} %blocks_ref.9), custom_call_target="tpu_custom_call" | custom-call | flops 201326592 | bytes 12582912 | tf_op jit(solution)/shard_map/pallas_call | solution.py:77
  55.1 4.4 %shard_map.55 = (f32[16,8192]{1,0:T(8,128)S(1)}, bf16[16,8192]{1,0:T(8,128)(2,1)S(1)}, bf16[64,16,256]{2,1,0:T(8,128)(2,1)}, bf16[16,256]{1,0:T(8,128)(2,1)S(1)}, bf16[16,256]{1,0:T(8,128)(2,1)S(1)}) custom-call(s32[1]{0:T(128)} %bitcast.1.odd_ref, s32[64]{0:T(128)S(1)} %min.20.want_ref, s32[32]{0:T(128)S(1)} %add_clamp_fusion.loc_ref, ...), custom_call_target="tpu_custom_call" | custom-call | flops 67108864 | bytes 4194304 | tf_op jit(solution)/shard_map/pallas_call | solution.py:174
  59.4 3.9 %all-to-all-start.3 = ((bf16[64,16,256]{2,1,0:T(8,128)(2,1)}), bf16[64,16,256]{2,1,0:T(8,128)(2,1)S(1)}, u32[]{:S(2)}, u32[]{:S(2)}) async-start(bf16[64,16,256]{2,1,0:T(8,128)(2,1)} %get-tuple-element.51), calls=%async_computation.3 | async-start | bytes 1048576 | tf_op jit(solution)/shard_map/all_to_all | solution.py:31
  63.6 5.1 %collective-permute-start.5 = (bf16[16,256]{1,0:T(8,128)(2,1)S(1)}, bf16[16,256]{1,0:T(8,128)(2,1)S(1)}, u32[]{:S(2)}, u32[]{:S(2)}) collective-permute-start(bf16[16,256]{1,0:T(8,128)(2,1)S(1)} %get-tuple-element.53), channel_id=1, source_target_pairs={{0,124},{4,8},{8,4},{12,16},{16,12},{20,24},{24,20},{28,32},{32,28... | collective-permute-start | bytes 24584 | tf_op jit(solution)/shard_map/ppermute | solution.py:408
  68.7 5.7 %shard_map.56 = (f32[16,8192]{1,0:T(8,128)S(1)}, bf16[8,256,256]{2,1,0:T(8,128)(2,1)S(1)}) custom-call(bf16[16,8192]{1,0:T(8,128)(2,1)S(1)} %get-tuple-element.48.x_ref, f32[16,8192]{1,0:T(8,128)S(1)} %get-tuple-element.49.refs_0_, bf16[32,4,256,256]{3,2,1,0:T(8,128)(2,1)} %blocks_ref.9), custom_call_target="tpu_custom_call" | custom-call | flops 201326592 | bytes 12582912 | tf_op jit(solution)/shard_map/pallas_call | solution.py:77
  75.1 4.4 %shard_map.57 = (f32[16,8192]{1,0:T(8,128)S(1)}, bf16[16,8192]{1,0:T(8,128)(2,1)S(1)}, bf16[64,16,256]{2,1,0:T(8,128)(2,1)}, bf16[16,256]{1,0:T(8,128)(2,1)S(1)}, bf16[16,256]{1,0:T(8,128)(2,1)S(1)}) custom-call(s32[1]{0:T(128)} %bitcast.1.odd_ref, s32[64]{0:T(128)S(1)} %min.20.want_ref, s32[32]{0:T(128)S(1)} %add_clamp_fusion.loc_ref, ...), custom_call_target="tpu_custom_call" | custom-call | flops 67108864 | bytes 4194304 | tf_op jit(solution)/shard_map/pallas_call | solution.py:174
  79.5 3.9 %all-to-all-start.4 = ((bf16[64,16,256]{2,1,0:T(8,128)(2,1)}), bf16[64,16,256]{2,1,0:T(8,128)(2,1)S(1)}, u32[]{:S(2)}, u32[]{:S(2)}) async-start(bf16[64,16,256]{2,1,0:T(8,128)(2,1)} %get-tuple-element.58), calls=%async_computation.4 | async-start | bytes 1048576 | tf_op jit(solution)/shard_map/all_to_all | solution.py:31
  83.6 5.1 %collective-permute-start.7 = (bf16[16,256]{1,0:T(8,128)(2,1)S(1)}, bf16[16,256]{1,0:T(8,128)(2,1)S(1)}, u32[]{:S(2)}, u32[]{:S(2)}) collective-permute-start(bf16[16,256]{1,0:T(8,128)(2,1)S(1)} %get-tuple-element.60), channel_id=1, source_target_pairs={{0,124},{4,8},{8,4},{12,16},{16,12},{20,24},{24,20},{28,32},{32,28... | collective-permute-start | bytes 24584 | tf_op jit(solution)/shard_map/ppermute | solution.py:408
  88.8 5.7 %shard_map.58 = (f32[16,8192]{1,0:T(8,128)S(1)}, bf16[8,256,256]{2,1,0:T(8,128)(2,1)S(1)}) custom-call(bf16[16,8192]{1,0:T(8,128)(2,1)S(1)} %get-tuple-element.55.x_ref, f32[16,8192]{1,0:T(8,128)S(1)} %get-tuple-element.56.refs_0_, bf16[32,4,256,256]{3,2,1,0:T(8,128)(2,1)} %blocks_ref.9), custom_call_target="tpu_custom_call" | custom-call | flops 201326592 | bytes 12582912 | tf_op jit(solution)/shard_map/pallas_call | solution.py:77
  95.1 4.4 %shard_map.59 = (bf16[16,8192]{1,0:T(8,128)(2,1)S(1)}, bf16[16,8192]{1,0:T(8,128)(2,1)S(1)}, bf16[64,16,256]{2,1,0:T(8,128)(2,1)}, bf16[16,256]{1,0:T(8,128)(2,1)S(1)}, bf16[16,256]{1,0:T(8,128)(2,1)S(1)}) custom-call(s32[1]{0:T(128)} %bitcast.1.odd_ref, s32[64]{0:T(128)S(1)} %min.20.want_ref, s32[32]{0:T(128)S(1)} %add_clamp_fusion.loc_ref, ...), custom_call_target="tpu_custom_call" | custom-call | flops 67108864 | bytes 4194304 | tf_op jit(solution)/shard_map/pallas_call | solution.py:174
  99.5 3.9 %all-to-all-start.5 = ((bf16[64,16,256]{2,1,0:T(8,128)(2,1)}), bf16[64,16,256]{2,1,0:T(8,128)(2,1)S(1)}, u32[]{:S(2)}, u32[]{:S(2)}) async-start(bf16[64,16,256]{2,1,0:T(8,128)(2,1)} %get-tuple-element.63), calls=%async_computation.5 | async-start | bytes 1048576 | tf_op jit(solution)/shard_map/all_to_all | solution.py:31
  103.4 2.8 %collective-permute-start.10 = (bf16[16,8192]{1,0:T(8,128)(2,1)S(1)}, bf16[16,8192]{1,0:T(8,128)(2,1)S(1)}, u32[]{:S(2)}, u32[]{:S(2)}) collective-permute-start(bf16[16,8192]{1,0:T(8,128)(2,1)S(1)} %get-tuple-element.67.x_ref.refs_0_), channel_id=1, source_target_pairs={{0,3},{1,0},{2,1},{3,2},{4,7},{5,4},{6,5},{7,6},{8,11},{9,8},{10,9... | collective-permute-start | bytes 786440 | tf_op jit(solution)/shard_map/ppermute | solution.py:416
  106.2 0.8 collective-permute-start.9
  107.0 0.9 collective-permute-start.8
  107.9 5.3 %collective-permute-start.12 = (bf16[16,256]{1,0:T(8,128)(2,1)S(1)}, bf16[16,256]{1,0:T(8,128)(2,1)S(1)}, u32[]{:S(2)}, u32[]{:S(2)}) collective-permute-start(bf16[16,256]{1,0:T(8,128)(2,1)S(1)} %get-tuple-element.65), channel_id=1, source_target_pairs={{0,124},{4,8},{8,4},{12,16},{16,12},{20,24},{24,20},{28,32},{32,28... | collective-permute-start | bytes 24584 | tf_op jit(solution)/shard_map/ppermute | solution.py:418
  113.2 5.7 %shard_map.60.t_ref = f32[16,8192]{1,0:T(8,128)S(1)} custom-call(bf16[16,8192]{1,0:T(8,128)(2,1)S(1)} %get-tuple-element.67.x_ref.refs_0_, bf16[32,4,256,256]{3,2,1,0:T(8,128)(2,1)} %blocks_ref.9), custom_call_target="tpu_custom_call" | custom-call | flops 201326592 | bytes 12582912 | tf_op jit(solution)/shard_map/pallas_call | solution.py:77
  119.0 3.8 %shard_map.61.z_ref = bf16[32,8192]{1,0:T(8,128)(2,1)S(1)} custom-call(s32[1]{0:T(128)} %bitcast.1.odd_ref, s32[32]{0:T(128)S(1)} %add_clamp_fusion.loc_ref, f32[16,8192]{1,0:T(8,128)S(1)} %shard_map.60.t_ref, bf16[64,16,256]{2,1,0:T(8,128)(2,1)S(1)} %all-to-all-done.5.recv_ref, bf16[16,256]{1,0:T(8,128)(2,1)S(1)} %collective-permute-done.11.pair_ref, ...), custom_call_target="tpu_custom_call" | custom-call | flops 67108864 | bytes 4194304 | tf_op jit(solution)/shard_map/pallas_call | solution.py:205
  123.4 25.3 %all_to_all.35.parts_ref = f32[128,16,128]{2,1,0:T(8,128)S(1)} all-to-all(f32[128,16,128]{2,1,0:T(8,128)S(1)} %get-tuple-element.71), channel_id=1, replica_groups=mesh['rows'=32,'cols'=4] {'rows','cols'}, dimensions={0} | all-to-all | bytes 2097152 | tf_op jit(solution)/shard_map/all_to_all | solution.py:31
  148.7 3.2 %shard_map.63 = (f32[16,8192]{1,0:T(8,128)}, f32[16,64]{1,0:T(8,128)}) custom-call(s32[1]{0:T(128)} %bitcast.own_ref, f32[128,16,128]{2,1,0:T(8,128)S(1)} %all_to_all.35.parts_ref, bf16[4,16,8192]{2,1,0:T(8,128)(2,1)S(1)} %get-tuple-element.72.all_ref, bf16[16,8192]{1,0:T(8,128)(2,1)S(1)} %get-tuple-element.73.low_ref), custom_call_target="tpu_custom_call" | custom-call | flops 1073741824 | bytes 16777216 | tf_op jit(solution)/shard_map/pallas_call | solution.py:338
  (32 shorter events, 5.0 us)
Async XLA Ops:
  0.6 0.7 copy-start.1
  2.1 15.7 %all-to-all-start = ((s32[32,1,128]{2,1,0:T(1,128)}), s32[32,1,128]{2,1,0:T(1,128)S(1)}, u32[]{:S(2)}, u32[]{:S(2)}) async-start(s32[32,1,128]{2,1,0:T(1,128)} %bitcast.4), calls=%async_computation | async-start | bytes 32768 | tf_op jit(solution)/shard_map/all_to_all | solution.py:31
  11.6 19.3 %collective-permute-start.1 = (bf16[16,256]{1,0:T(8,128)(2,1)S(1)}, bf16[16,256]{1,0:T(8,128)(2,1)S(1)}, u32[]{:S(2)}, u32[]{:S(2)}) collective-permute-start(bf16[16,256]{1,0:T(8,128)(2,1)S(1)} %get-tuple-element.76), channel_id=1, source_target_pairs={{0,124},{4,8},{8,4},{12,16},{16,12},{20,24},{24,20},{28,32},{32,28... | collective-permute-start | bytes 24584 | tf_op jit(solution)/shard_map/ppermute | solution.py:408
  16.6 14.2 %collective-permute-start = (bf16[16,256]{1,0:T(8,128)(2,1)S(1)}, bf16[16,256]{1,0:T(8,128)(2,1)S(1)}, u32[]{:S(2)}, u32[]{:S(2)}) collective-permute-start(bf16[16,256]{1,0:T(8,128)(2,1)S(1)} %get-tuple-element.77), channel_id=1, source_target_pairs={{0,4},{4,0},{8,12},{12,8},{16,20},{20,16},{24,28},{28,24},{32,36},... | collective-permute-start | bytes 24584 | tf_op jit(solution)/shard_map/ppermute | solution.py:407
  19.4 15.7 %all-to-all-start.1 = ((bf16[64,16,256]{2,1,0:T(8,128)(2,1)}), bf16[64,16,256]{2,1,0:T(8,128)(2,1)S(1)}, u32[]{:S(2)}, u32[]{:S(2)}) async-start(bf16[64,16,256]{2,1,0:T(8,128)(2,1)} %shard_map.52), calls=%async_computation.1 | async-start | bytes 1048576 | tf_op jit(solution)/shard_map/all_to_all | solution.py:31
  24.1 1.0 copy-start
  39.4 15.7 %all-to-all-start.2 = ((bf16[64,16,256]{2,1,0:T(8,128)(2,1)}), bf16[64,16,256]{2,1,0:T(8,128)(2,1)S(1)}, u32[]{:S(2)}, u32[]{:S(2)}) async-start(bf16[64,16,256]{2,1,0:T(8,128)(2,1)} %get-tuple-element.44), calls=%async_computation.2 | async-start | bytes 1048576 | tf_op jit(solution)/shard_map/all_to_all | solution.py:31
  43.3 11.1 %collective-permute-start.2 = (bf16[16,256]{1,0:T(8,128)(2,1)S(1)}, bf16[16,256]{1,0:T(8,128)(2,1)S(1)}, u32[]{:S(2)}, u32[]{:S(2)}) collective-permute-start(bf16[16,256]{1,0:T(8,128)(2,1)S(1)} %get-tuple-element.45), channel_id=1, source_target_pairs={{0,4},{4,0},{8,12},{12,8},{16,20},{20,16},{24,28},{28,24},{32,36},... | collective-permute-start | bytes 24584 | tf_op jit(solution)/shard_map/ppermute | solution.py:407
  43.5 11.0 %collective-permute-start.3 = (bf16[16,256]{1,0:T(8,128)(2,1)S(1)}, bf16[16,256]{1,0:T(8,128)(2,1)S(1)}, u32[]{:S(2)}, u32[]{:S(2)}) collective-permute-start(bf16[16,256]{1,0:T(8,128)(2,1)S(1)} %get-tuple-element.46), channel_id=1, source_target_pairs={{0,124},{4,8},{8,4},{12,16},{16,12},{20,24},{24,20},{28,32},{32,28... | collective-permute-start | bytes 24584 | tf_op jit(solution)/shard_map/ppermute | solution.py:408
  59.4 15.7 %all-to-all-start.3 = ((bf16[64,16,256]{2,1,0:T(8,128)(2,1)}), bf16[64,16,256]{2,1,0:T(8,128)(2,1)S(1)}, u32[]{:S(2)}, u32[]{:S(2)}) async-start(bf16[64,16,256]{2,1,0:T(8,128)(2,1)} %get-tuple-element.51), calls=%async_computation.3 | async-start | bytes 1048576 | tf_op jit(solution)/shard_map/all_to_all | solution.py:31
  63.3 11.1 %collective-permute-start.4 = (bf16[16,256]{1,0:T(8,128)(2,1)S(1)}, bf16[16,256]{1,0:T(8,128)(2,1)S(1)}, u32[]{:S(2)}, u32[]{:S(2)}) collective-permute-start(bf16[16,256]{1,0:T(8,128)(2,1)S(1)} %get-tuple-element.52), channel_id=1, source_target_pairs={{0,4},{4,0},{8,12},{12,8},{16,20},{20,16},{24,28},{28,24},{32,36},... | collective-permute-start | bytes 24584 | tf_op jit(solution)/shard_map/ppermute | solution.py:407
  63.6 11.0 %collective-permute-start.5 = (bf16[16,256]{1,0:T(8,128)(2,1)S(1)}, bf16[16,256]{1,0:T(8,128)(2,1)S(1)}, u32[]{:S(2)}, u32[]{:S(2)}) collective-permute-start(bf16[16,256]{1,0:T(8,128)(2,1)S(1)} %get-tuple-element.53), channel_id=1, source_target_pairs={{0,124},{4,8},{8,4},{12,16},{16,12},{20,24},{24,20},{28,32},{32,28... | collective-permute-start | bytes 24584 | tf_op jit(solution)/shard_map/ppermute | solution.py:408
  79.5 15.7 %all-to-all-start.4 = ((bf16[64,16,256]{2,1,0:T(8,128)(2,1)}), bf16[64,16,256]{2,1,0:T(8,128)(2,1)S(1)}, u32[]{:S(2)}, u32[]{:S(2)}) async-start(bf16[64,16,256]{2,1,0:T(8,128)(2,1)} %get-tuple-element.58), calls=%async_computation.4 | async-start | bytes 1048576 | tf_op jit(solution)/shard_map/all_to_all | solution.py:31
  83.4 11.1 %collective-permute-start.6 = (bf16[16,256]{1,0:T(8,128)(2,1)S(1)}, bf16[16,256]{1,0:T(8,128)(2,1)S(1)}, u32[]{:S(2)}, u32[]{:S(2)}) collective-permute-start(bf16[16,256]{1,0:T(8,128)(2,1)S(1)} %get-tuple-element.59), channel_id=1, source_target_pairs={{0,4},{4,0},{8,12},{12,8},{16,20},{20,16},{24,28},{28,24},{32,36},... | collective-permute-start | bytes 24584 | tf_op jit(solution)/shard_map/ppermute | solution.py:407
  83.6 11.0 %collective-permute-start.7 = (bf16[16,256]{1,0:T(8,128)(2,1)S(1)}, bf16[16,256]{1,0:T(8,128)(2,1)S(1)}, u32[]{:S(2)}, u32[]{:S(2)}) collective-permute-start(bf16[16,256]{1,0:T(8,128)(2,1)S(1)} %get-tuple-element.60), channel_id=1, source_target_pairs={{0,124},{4,8},{8,4},{12,16},{16,12},{20,24},{24,20},{28,32},{32,28... | collective-permute-start | bytes 24584 | tf_op jit(solution)/shard_map/ppermute | solution.py:408
  99.5 19.4 %all-to-all-start.5 = ((bf16[64,16,256]{2,1,0:T(8,128)(2,1)}), bf16[64,16,256]{2,1,0:T(8,128)(2,1)S(1)}, u32[]{:S(2)}, u32[]{:S(2)}) async-start(bf16[64,16,256]{2,1,0:T(8,128)(2,1)} %get-tuple-element.63), calls=%async_computation.5 | async-start | bytes 1048576 | tf_op jit(solution)/shard_map/all_to_all | solution.py:31
  103.4 19.3 %collective-permute-start.10 = (bf16[16,8192]{1,0:T(8,128)(2,1)S(1)}, bf16[16,8192]{1,0:T(8,128)(2,1)S(1)}, u32[]{:S(2)}, u32[]{:S(2)}) collective-permute-start(bf16[16,8192]{1,0:T(8,128)(2,1)S(1)} %get-tuple-element.67.x_ref.refs_0_), channel_id=1, source_target_pairs={{0,3},{1,0},{2,1},{3,2},{4,7},{5,4},{6,5},{7,6},{8,11},{9,8},{10,9... | collective-permute-start | bytes 786440 | tf_op jit(solution)/shard_map/ppermute | solution.py:416
  106.2 16.5 %collective-permute-start.9 = (bf16[16,8192]{1,0:T(8,128)(2,1)S(1)}, bf16[16,8192]{1,0:T(8,128)(2,1)S(1)}, u32[]{:S(2)}, u32[]{:S(2)}) collective-permute-start(bf16[16,8192]{1,0:T(8,128)(2,1)S(1)} %get-tuple-element.67.x_ref.refs_0_), channel_id=1, source_target_pairs={{0,2},{1,3},{2,0},{3,1},{4,6},{5,7},{6,4},{7,5},{8,10},{9,11},{10,... | collective-permute-start | bytes 786440 | tf_op jit(solution)/shard_map/ppermute | solution.py:416
  107.0 15.7 %collective-permute-start.8 = (bf16[16,8192]{1,0:T(8,128)(2,1)S(1)}, bf16[16,8192]{1,0:T(8,128)(2,1)S(1)}, u32[]{:S(2)}, u32[]{:S(2)}) collective-permute-start(bf16[16,8192]{1,0:T(8,128)(2,1)S(1)} %get-tuple-element.67.x_ref.refs_0_), channel_id=1, source_target_pairs={{0,1},{1,2},{2,3},{3,0},{4,5},{5,6},{6,7},{7,4},{8,9},{9,10},{10,1... | collective-permute-start | bytes 786440 | tf_op jit(solution)/shard_map/ppermute | solution.py:416
  107.9 11.0 %collective-permute-start.11 = (bf16[16,256]{1,0:T(8,128)(2,1)S(1)}, bf16[16,256]{1,0:T(8,128)(2,1)S(1)}, u32[]{:S(2)}, u32[]{:S(2)}) collective-permute-start(bf16[16,256]{1,0:T(8,128)(2,1)S(1)} %get-tuple-element.64), channel_id=1, source_target_pairs={{0,4},{4,0},{8,12},{12,8},{16,20},{20,16},{24,28},{28,24},{32,36},... | collective-permute-start | bytes 24584 | tf_op jit(solution)/shard_map/ppermute | solution.py:417
  107.9 11.0 %collective-permute-start.12 = (bf16[16,256]{1,0:T(8,128)(2,1)S(1)}, bf16[16,256]{1,0:T(8,128)(2,1)S(1)}, u32[]{:S(2)}, u32[]{:S(2)}) collective-permute-start(bf16[16,256]{1,0:T(8,128)(2,1)S(1)} %get-tuple-element.65), channel_id=1, source_target_pairs={{0,124},{4,8},{8,4},{12,16},{16,12},{20,24},{24,20},{28,32},{32,28... | collective-permute-start | bytes 24584 | tf_op jit(solution)/shard_map/ppermute | solution.py:418

commit v7 on v6

--- a/solution.py
+++ b/solution.py
@@ -9,7 +9,7 @@
 
 ITERS = 4
 CAP = 2
-GROUPS = 4
+GROUPS = 8
 AHEAD = 8
 LATER = 2
 PIVOTS = 8

time: 154 us -> 154 us (level)
  transfers between devices with their start and end apart: 19 -> 19, of which waited for: 8 -> 7; matrix products, arithmetic and copies ran while one was open for 1% -> 1% of each run, Pallas kernels for 22% -> 22%
where the time goes in v7:
time: 154 us; the launch traced here: 152 us
  starting transfers between devices  59.1 us (38%)
  Pallas kernels  55.7 us (36%)
  blocking collectives  25.3 us (16%)
  waiting for transfers between devices  7.04 us (5%)
  other arithmetic  1.99 us (1%)
  local copies, waits for them, and re-layouts  1.8 us (1%)
    pallas_call x5, Pallas kernels, local_part(): pl.pallas_call(functools.partial(local_kernel, rows, size, not w), out_sh...  28.5 us
    all_to_all x6, starting transfers between devices, exchange(): return lax.all_to_all(x, axes, split_axis=0, concat_axis=0, tiled=True)  27.9 us
    ppermute x5, starting transfers between devices, body(): other = lax.ppermute(to_other, 'rows', others)  25.8 us
    all_to_all x1, blocking collectives, exchange(): return lax.all_to_all(x, axes, split_axis=0, concat_axis=0, tiled=True)  25.3 us
    pallas_call x4, Pallas kernels, far_part(): pl.pallas_call(functools.partial(far_kernel, rows, size, last_one), out_s...  17.4 us
    all_to_all x6, waiting for transfers between devices, exchange(): return lax.all_to_all(x, axes, split_axis=0, concat_axis=0, tiled=True)  6.74 us
    ppermute x3, starting transfers between devices, body(): lax.ppermute(x, 'cols', [(i, (i + k) % groups) for i in range(groups)])  4.51 us
    pallas_call x1, Pallas kernels, applied(): pl.pallas_call(functools.partial(applied_kernel, rows, size), out_shape=j...  3.77 us
  transfers between devices with their start and end apart: 19, of which 7 were waited for; matrix products, arithmetic and copies ran while one was open for 1% of the time, Pallas kernels for 22%

profile of v7, /device:TPU:0, one launch (start us, length us, event | category | flops | bytes accessed | tf_op | source)
XLA Modules:
  0.0 151.9 jit_solution(7614663188738117603)
XLA Ops:
  1.3 0.8 shard_map.50
  2.1 8.4 %all-to-all-start = ((s32[32,1,128]{2,1,0:T(1,128)}), s32[32,1,128]{2,1,0:T(1,128)S(1)}, u32[]{:S(2)}, u32[]{:S(2)}) async-start(s32[32,1,128]{2,1,0:T(1,128)} %bitcast.4), calls=%async_computation | async-start | bytes 32768 | tf_op jit(solution)/shard_map/all_to_all | solution.py:31
  10.5 1.1 convert_element_type.7.x_ref
  11.6 5.0 %collective-permute-start.1 = (bf16[16,256]{1,0:T(8,128)(2,1)S(1)}, bf16[16,256]{1,0:T(8,128)(2,1)S(1)}, u32[]{:S(2)}, u32[]{:S(2)}) collective-permute-start(bf16[16,256]{1,0:T(8,128)(2,1)S(1)} %get-tuple-element.76), channel_id=1, source_target_pairs={{0,124},{4,8},{8,4},{12,16},{16,12},{20,24},{24,20},{28,32},{32,28... | collective-permute-start | bytes 24584 | tf_op jit(solution)/shard_map/ppermute | solution.py:408
  16.6 1.1 all-to-all-done
  17.9 1.4 shard_map.52
  19.4 3.9 %all-to-all-start.1 = ((bf16[64,16,256]{2,1,0:T(8,128)(2,1)}), bf16[64,16,256]{2,1,0:T(8,128)(2,1)S(1)}, u32[]{:S(2)}, u32[]{:S(2)}) async-start(bf16[64,16,256]{2,1,0:T(8,128)(2,1)} %shard_map.52), calls=%async_computation.1 | async-start | bytes 1048576 | tf_op jit(solution)/shard_map/all_to_all | solution.py:31
  24.1 1.0 copy-done
  25.2 5.7 %shard_map.51 = (f32[16,8192]{1,0:T(8,128)S(1)}, bf16[8,256,256]{2,1,0:T(8,128)(2,1)S(1)}) custom-call(bf16[16,8192]{1,0:T(8,128)(2,1)S(1)} %convert_element_type.7.x_ref, f32[16,8192]{1,0:T(8,128)S(1)} %copy-done, bf16[32,4,256,256]{3,2,1,0:T(8,128)(2,1)} %blocks_ref.9), custom_call_target="tpu_custom_call" | custom-call | flops 201326592 | bytes 12582912 | tf_op jit(solution)/shard_map/pallas_call | solution.py:77
  30.9 4.1 %all-to-all-done.1.recv_ref = bf16[64,16,256]{2,1,0:T(8,128)(2,1)S(1)} async-done(((bf16[64,16,256]{2,1,0:T(8,128)(2,1)}), bf16[64,16,256]{2,1,0:T(8,128)(2,1)S(1)}, u32[]{:S(2)}, u32[]{:S(2)}) %all-to-all-start.1) | async-done | bytes 524320 | tf_op jit(solution)/shard_map/all_to_all | solution.py:31
  35.0 4.4 %shard_map.53 = (f32[16,8192]{1,0:T(8,128)S(1)}, bf16[16,8192]{1,0:T(8,128)(2,1)S(1)}, bf16[64,16,256]{2,1,0:T(8,128)(2,1)}, bf16[16,256]{1,0:T(8,128)(2,1)S(1)}, bf16[16,256]{1,0:T(8,128)(2,1)S(1)}) custom-call(s32[1]{0:T(128)} %bitcast.1.odd_ref, s32[64]{0:T(128)S(1)} %min.20.want_ref, s32[32]{0:T(128)S(1)} %add_clamp_fusion.loc_ref, ...), custom_call_target="tpu_custom_call" | custom-call | flops 67108864 | bytes 4194304 | tf_op jit(solution)/shard_map/pallas_call | solution.py:174
  39.4 3.9 %all-to-all-start.2 = ((bf16[64,16,256]{2,1,0:T(8,128)(2,1)}), bf16[64,16,256]{2,1,0:T(8,128)(2,1)S(1)}, u32[]{:S(2)}, u32[]{:S(2)}) async-start(bf16[64,16,256]{2,1,0:T(8,128)(2,1)} %get-tuple-element.44), calls=%async_computation.2 | async-start | bytes 1048576 | tf_op jit(solution)/shard_map/all_to_all | solution.py:31
  43.5 5.1 %collective-permute-start.3 = (bf16[16,256]{1,0:T(8,128)(2,1)S(1)}, bf16[16,256]{1,0:T(8,128)(2,1)S(1)}, u32[]{:S(2)}, u32[]{:S(2)}) collective-permute-start(bf16[16,256]{1,0:T(8,128)(2,1)S(1)} %get-tuple-element.46), channel_id=1, source_target_pairs={{0,124},{4,8},{8,4},{12,16},{16,12},{20,24},{24,20},{28,32},{32,28... | collective-permute-start | bytes 24584 | tf_op jit(solution)/shard_map/ppermute | solution.py:408
  48.7 5.7 %shard_map.54 = (f32[16,8192]{1,0:T(8,128)S(1)}, bf16[8,256,256]{2,1,0:T(8,128)(2,1)S(1)}) custom-call(bf16[16,8192]{1,0:T(8,128)(2,1)S(1)} %get-tuple-element.41.x_ref, f32[16,8192]{1,0:T(8,128)S(1)} %get-tuple-element.42.refs_0_, bf16[32,4,256,256]{3,2,1,0:T(8,128)(2,1)} %blocks_ref.9), custom_call_target="tpu_custom_call" | custom-call | flops 201326592 | bytes 12582912 | tf_op jit(solution)/shard_map/pallas_call | solution.py:77
  55.1 4.4 %shard_map.55 = (f32[16,8192]{1,0:T(8,128)S(1)}, bf16[16,8192]{1,0:T(8,128)(2,1)S(1)}, bf16[64,16,256]{2,1,0:T(8,128)(2,1)}, bf16[16,256]{1,0:T(8,128)(2,1)S(1)}, bf16[16,256]{1,0:T(8,128)(2,1)S(1)}) custom-call(s32[1]{0:T(128)} %bitcast.1.odd_ref, s32[64]{0:T(128)S(1)} %min.20.want_ref, s32[32]{0:T(128)S(1)} %add_clamp_fusion.loc_ref, ...), custom_call_target="tpu_custom_call" | custom-call | flops 67108864 | bytes 4194304 | tf_op jit(solution)/shard_map/pallas_call | solution.py:174
  59.4 3.9 %all-to-all-start.3 = ((bf16[64,16,256]{2,1,0:T(8,128)(2,1)}), bf16[64,16,256]{2,1,0:T(8,128)(2,1)S(1)}, u32[]{:S(2)}, u32[]{:S(2)}) async-start(bf16[64,16,256]{2,1,0:T(8,128)(2,1)} %get-tuple-element.51), calls=%async_computation.3 | async-start | bytes 1048576 | tf_op jit(solution)/shard_map/all_to_all | solution.py:31
  63.6 5.1 %collective-permute-start.5 = (bf16[16,256]{1,0:T(8,128)(2,1)S(1)}, bf16[16,256]{1,0:T(8,128)(2,1)S(1)}, u32[]{:S(2)}, u32[]{:S(2)}) collective-permute-start(bf16[16,256]{1,0:T(8,128)(2,1)S(1)} %get-tuple-element.53), channel_id=1, source_target_pairs={{0,124},{4,8},{8,4},{12,16},{16,12},{20,24},{24,20},{28,32},{32,28... | collective-permute-start | bytes 24584 | tf_op jit(solution)/shard_map/ppermute | solution.py:408
  68.7 5.7 %shard_map.56 = (f32[16,8192]{1,0:T(8,128)S(1)}, bf16[8,256,256]{2,1,0:T(8,128)(2,1)S(1)}) custom-call(bf16[16,8192]{1,0:T(8,128)(2,1)S(1)} %get-tuple-element.48.x_ref, f32[16,8192]{1,0:T(8,128)S(1)} %get-tuple-element.49.refs_0_, bf16[32,4,256,256]{3,2,1,0:T(8,128)(2,1)} %blocks_ref.9), custom_call_target="tpu_custom_call" | custom-call | flops 201326592 | bytes 12582912 | tf_op jit(solution)/shard_map/pallas_call | solution.py:77
  75.1 4.4 %shard_map.57 = (f32[16,8192]{1,0:T(8,128)S(1)}, bf16[16,8192]{1,0:T(8,128)(2,1)S(1)}, bf16[64,16,256]{2,1,0:T(8,128)(2,1)}, bf16[16,256]{1,0:T(8,128)(2,1)S(1)}, bf16[16,256]{1,0:T(8,128)(2,1)S(1)}) custom-call(s32[1]{0:T(128)} %bitcast.1.odd_ref, s32[64]{0:T(128)S(1)} %min.20.want_ref, s32[32]{0:T(128)S(1)} %add_clamp_fusion.loc_ref, ...), custom_call_target="tpu_custom_call" | custom-call | flops 67108864 | bytes 4194304 | tf_op jit(solution)/shard_map/pallas_call | solution.py:174
  79.5 3.9 %all-to-all-start.4 = ((bf16[64,16,256]{2,1,0:T(8,128)(2,1)}), bf16[64,16,256]{2,1,0:T(8,128)(2,1)S(1)}, u32[]{:S(2)}, u32[]{:S(2)}) async-start(bf16[64,16,256]{2,1,0:T(8,128)(2,1)} %get-tuple-element.58), calls=%async_computation.4 | async-start | bytes 1048576 | tf_op jit(solution)/shard_map/all_to_all | solution.py:31
  83.8 5.1 %collective-permute-start.7 = (bf16[16,256]{1,0:T(8,128)(2,1)S(1)}, bf16[16,256]{1,0:T(8,128)(2,1)S(1)}, u32[]{:S(2)}, u32[]{:S(2)}) collective-permute-start(bf16[16,256]{1,0:T(8,128)(2,1)S(1)} %get-tuple-element.60), channel_id=1, source_target_pairs={{0,124},{4,8},{8,4},{12,16},{16,12},{20,24},{24,20},{28,32},{32,28... | collective-permute-start | bytes 24584 | tf_op jit(solution)/shard_map/ppermute | solution.py:408
  88.9 5.7 %shard_map.58 = (f32[16,8192]{1,0:T(8,128)S(1)}, bf16[8,256,256]{2,1,0:T(8,128)(2,1)S(1)}) custom-call(bf16[16,8192]{1,0:T(8,128)(2,1)S(1)} %get-tuple-element.55.x_ref, f32[16,8192]{1,0:T(8,128)S(1)} %get-tuple-element.56.refs_0_, bf16[32,4,256,256]{3,2,1,0:T(8,128)(2,1)} %blocks_ref.9), custom_call_target="tpu_custom_call" | custom-call | flops 201326592 | bytes 12582912 | tf_op jit(solution)/shard_map/pallas_call | solution.py:77
  95.1 4.4 %shard_map.59 = (bf16[16,8192]{1,0:T(8,128)(2,1)S(1)}, bf16[16,8192]{1,0:T(8,128)(2,1)S(1)}, bf16[64,16,256]{2,1,0:T(8,128)(2,1)}, bf16[16,256]{1,0:T(8,128)(2,1)S(1)}, bf16[16,256]{1,0:T(8,128)(2,1)S(1)}) custom-call(s32[1]{0:T(128)} %bitcast.1.odd_ref, s32[64]{0:T(128)S(1)} %min.20.want_ref, s32[32]{0:T(128)S(1)} %add_clamp_fusion.loc_ref, ...), custom_call_target="tpu_custom_call" | custom-call | flops 67108864 | bytes 4194304 | tf_op jit(solution)/shard_map/pallas_call | solution.py:174
  99.5 3.9 %all-to-all-start.5 = ((bf16[64,16,256]{2,1,0:T(8,128)(2,1)}), bf16[64,16,256]{2,1,0:T(8,128)(2,1)S(1)}, u32[]{:S(2)}, u32[]{:S(2)}) async-start(bf16[64,16,256]{2,1,0:T(8,128)(2,1)} %get-tuple-element.63), calls=%async_computation.5 | async-start | bytes 1048576 | tf_op jit(solution)/shard_map/all_to_all | solution.py:31
  103.4 2.8 %collective-permute-start.10 = (bf16[16,8192]{1,0:T(8,128)(2,1)S(1)}, bf16[16,8192]{1,0:T(8,128)(2,1)S(1)}, u32[]{:S(2)}, u32[]{:S(2)}) collective-permute-start(bf16[16,8192]{1,0:T(8,128)(2,1)S(1)} %get-tuple-element.67.x_ref.refs_0_), channel_id=1, source_target_pairs={{0,3},{1,0},{2,1},{3,2},{4,7},{5,4},{6,5},{7,6},{8,11},{9,8},{10,9... | collective-permute-start | bytes 786440 | tf_op jit(solution)/shard_map/ppermute | solution.py:416
  106.2 0.8 collective-permute-start.9
  107.0 0.9 collective-permute-start.8
  107.9 5.3 %collective-permute-start.12 = (bf16[16,256]{1,0:T(8,128)(2,1)S(1)}, bf16[16,256]{1,0:T(8,128)(2,1)S(1)}, u32[]{:S(2)}, u32[]{:S(2)}) collective-permute-start(bf16[16,256]{1,0:T(8,128)(2,1)S(1)} %get-tuple-element.65), channel_id=1, source_target_pairs={{0,124},{4,8},{8,4},{12,16},{16,12},{20,24},{24,20},{28,32},{32,28... | collective-permute-start | bytes 24584 | tf_op jit(solution)/shard_map/ppermute | solution.py:418
  113.2 5.7 %shard_map.60.t_ref = f32[16,8192]{1,0:T(8,128)S(1)} custom-call(bf16[16,8192]{1,0:T(8,128)(2,1)S(1)} %get-tuple-element.67.x_ref.refs_0_, bf16[32,4,256,256]{3,2,1,0:T(8,128)(2,1)} %blocks_ref.9), custom_call_target="tpu_custom_call" | custom-call | flops 201326592 | bytes 12582912 | tf_op jit(solution)/shard_map/pallas_call | solution.py:77
  119.0 3.8 %shard_map.61.z_ref = bf16[32,8192]{1,0:T(8,128)(2,1)S(1)} custom-call(s32[1]{0:T(128)} %bitcast.1.odd_ref, s32[32]{0:T(128)S(1)} %add_clamp_fusion.loc_ref, f32[16,8192]{1,0:T(8,128)S(1)} %shard_map.60.t_ref, bf16[64,16,256]{2,1,0:T(8,128)(2,1)S(1)} %all-to-all-done.5.recv_ref, bf16[16,256]{1,0:T(8,128)(2,1)S(1)} %collective-permute-done.11.pair_ref, ...), custom_call_target="tpu_custom_call" | custom-call | flops 67108864 | bytes 4194304 | tf_op jit(solution)/shard_map/pallas_call | solution.py:205
  123.4 25.3 %all_to_all.35.parts_ref = f32[128,16,128]{2,1,0:T(8,128)S(1)} all-to-all(f32[128,16,128]{2,1,0:T(8,128)S(1)} %get-tuple-element.71), channel_id=1, replica_groups=mesh['rows'=32,'cols'=4] {'rows','cols'}, dimensions={0} | all-to-all | bytes 2097152 | tf_op jit(solution)/shard_map/all_to_all | solution.py:31
  148.7 3.2 %shard_map.63 = (f32[16,8192]{1,0:T(8,128)}, f32[16,64]{1,0:T(8,128)}) custom-call(s32[1]{0:T(128)} %bitcast.own_ref, f32[128,16,128]{2,1,0:T(8,128)S(1)} %all_to_all.35.parts_ref, bf16[4,16,8192]{2,1,0:T(8,128)(2,1)S(1)} %get-tuple-element.72.all_ref, bf16[16,8192]{1,0:T(8,128)(2,1)S(1)} %get-tuple-element.73.low_ref), custom_call_target="tpu_custom_call" | custom-call | flops 1073741824 | bytes 16777216 | tf_op jit(solution)/shard_map/pallas_call | solution.py:338
  (32 shorter events, 5.0 us)
Async XLA Ops:
  0.6 0.7 copy-start.1
  2.1 15.7 %all-to-all-start = ((s32[32,1,128]{2,1,0:T(1,128)}), s32[32,1,128]{2,1,0:T(1,128)S(1)}, u32[]{:S(2)}, u32[]{:S(2)}) async-start(s32[32,1,128]{2,1,0:T(1,128)} %bitcast.4), calls=%async_computation | async-start | bytes 32768 | tf_op jit(solution)/shard_map/all_to_all | solution.py:31
  11.6 19.3 %collective-permute-start.1 = (bf16[16,256]{1,0:T(8,128)(2,1)S(1)}, bf16[16,256]{1,0:T(8,128)(2,1)S(1)}, u32[]{:S(2)}, u32[]{:S(2)}) collective-permute-start(bf16[16,256]{1,0:T(8,128)(2,1)S(1)} %get-tuple-element.76), channel_id=1, source_target_pairs={{0,124},{4,8},{8,4},{12,16},{16,12},{20,24},{24,20},{28,32},{32,28... | collective-permute-start | bytes 24584 | tf_op jit(solution)/shard_map/ppermute | solution.py:408
  16.6 14.2 %collective-permute-start = (bf16[16,256]{1,0:T(8,128)(2,1)S(1)}, bf16[16,256]{1,0:T(8,128)(2,1)S(1)}, u32[]{:S(2)}, u32[]{:S(2)}) collective-permute-start(bf16[16,256]{1,0:T(8,128)(2,1)S(1)} %get-tuple-element.77), channel_id=1, source_target_pairs={{0,4},{4,0},{8,12},{12,8},{16,20},{20,16},{24,28},{28,24},{32,36},... | collective-permute-start | bytes 24584 | tf_op jit(solution)/shard_map/ppermute | solution.py:407
  19.4 15.7 %all-to-all-start.1 = ((bf16[64,16,256]{2,1,0:T(8,128)(2,1)}), bf16[64,16,256]{2,1,0:T(8,128)(2,1)S(1)}, u32[]{:S(2)}, u32[]{:S(2)}) async-start(bf16[64,16,256]{2,1,0:T(8,128)(2,1)} %shard_map.52), calls=%async_computation.1 | async-start | bytes 1048576 | tf_op jit(solution)/shard_map/all_to_all | solution.py:31
  24.1 1.0 copy-start
  39.4 15.7 %all-to-all-start.2 = ((bf16[64,16,256]{2,1,0:T(8,128)(2,1)}), bf16[64,16,256]{2,1,0:T(8,128)(2,1)S(1)}, u32[]{:S(2)}, u32[]{:S(2)}) async-start(bf16[64,16,256]{2,1,0:T(8,128)(2,1)} %get-tuple-element.44), calls=%async_computation.2 | async-start | bytes 1048576 | tf_op jit(solution)/shard_map/all_to_all | solution.py:31
  43.3 11.1 %collective-permute-start.2 = (bf16[16,256]{1,0:T(8,128)(2,1)S(1)}, bf16[16,256]{1,0:T(8,128)(2,1)S(1)}, u32[]{:S(2)}, u32[]{:S(2)}) collective-permute-start(bf16[16,256]{1,0:T(8,128)(2,1)S(1)} %get-tuple-element.45), channel_id=1, source_target_pairs={{0,4},{4,0},{8,12},{12,8},{16,20},{20,16},{24,28},{28,24},{32,36},... | collective-permute-start | bytes 24584 | tf_op jit(solution)/shard_map/ppermute | solution.py:407
  43.5 11.0 %collective-permute-start.3 = (bf16[16,256]{1,0:T(8,128)(2,1)S(1)}, bf16[16,256]{1,0:T(8,128)(2,1)S(1)}, u32[]{:S(2)}, u32[]{:S(2)}) collective-permute-start(bf16[16,256]{1,0:T(8,128)(2,1)S(1)} %get-tuple-element.46), channel_id=1, source_target_pairs={{0,124},{4,8},{8,4},{12,16},{16,12},{20,24},{24,20},{28,32},{32,28... | collective-permute-start | bytes 24584 | tf_op jit(solution)/shard_map/ppermute | solution.py:408
  59.4 15.7 %all-to-all-start.3 = ((bf16[64,16,256]{2,1,0:T(8,128)(2,1)}), bf16[64,16,256]{2,1,0:T(8,128)(2,1)S(1)}, u32[]{:S(2)}, u32[]{:S(2)}) async-start(bf16[64,16,256]{2,1,0:T(8,128)(2,1)} %get-tuple-element.51), calls=%async_computation.3 | async-start | bytes 1048576 | tf_op jit(solution)/shard_map/all_to_all | solution.py:31
  63.3 11.1 %collective-permute-start.4 = (bf16[16,256]{1,0:T(8,128)(2,1)S(1)}, bf16[16,256]{1,0:T(8,128)(2,1)S(1)}, u32[]{:S(2)}, u32[]{:S(2)}) collective-permute-start(bf16[16,256]{1,0:T(8,128)(2,1)S(1)} %get-tuple-element.52), channel_id=1, source_target_pairs={{0,4},{4,0},{8,12},{12,8},{16,20},{20,16},{24,28},{28,24},{32,36},... | collective-permute-start | bytes 24584 | tf_op jit(solution)/shard_map/ppermute | solution.py:407
  63.6 11.0 %collective-permute-start.5 = (bf16[16,256]{1,0:T(8,128)(2,1)S(1)}, bf16[16,256]{1,0:T(8,128)(2,1)S(1)}, u32[]{:S(2)}, u32[]{:S(2)}) collective-permute-start(bf16[16,256]{1,0:T(8,128)(2,1)S(1)} %get-tuple-element.53), channel_id=1, source_target_pairs={{0,124},{4,8},{8,4},{12,16},{16,12},{20,24},{24,20},{28,32},{32,28... | collective-permute-start | bytes 24584 | tf_op jit(solution)/shard_map/ppermute | solution.py:408
  79.5 15.7 %all-to-all-start.4 = ((bf16[64,16,256]{2,1,0:T(8,128)(2,1)}), bf16[64,16,256]{2,1,0:T(8,128)(2,1)S(1)}, u32[]{:S(2)}, u32[]{:S(2)}) async-start(bf16[64,16,256]{2,1,0:T(8,128)(2,1)} %get-tuple-element.58), calls=%async_computation.4 | async-start | bytes 1048576 | tf_op jit(solution)/shard_map/all_to_all | solution.py:31
  83.4 11.3 %collective-permute-start.6 = (bf16[16,256]{1,0:T(8,128)(2,1)S(1)}, bf16[16,256]{1,0:T(8,128)(2,1)S(1)}, u32[]{:S(2)}, u32[]{:S(2)}) collective-permute-start(bf16[16,256]{1,0:T(8,128)(2,1)S(1)} %get-tuple-element.59), channel_id=1, source_target_pairs={{0,4},{4,0},{8,12},{12,8},{16,20},{20,16},{24,28},{28,24},{32,36},... | collective-permute-start | bytes 24584 | tf_op jit(solution)/shard_map/ppermute | solution.py:407
  83.8 10.9 %collective-permute-start.7 = (bf16[16,256]{1,0:T(8,128)(2,1)S(1)}, bf16[16,256]{1,0:T(8,128)(2,1)S(1)}, u32[]{:S(2)}, u32[]{:S(2)}) collective-permute-start(bf16[16,256]{1,0:T(8,128)(2,1)S(1)} %get-tuple-element.60), channel_id=1, source_target_pairs={{0,124},{4,8},{8,4},{12,16},{16,12},{20,24},{24,20},{28,32},{32,28... | collective-permute-start | bytes 24584 | tf_op jit(solution)/shard_map/ppermute | solution.py:408
  99.5 19.4 %all-to-all-start.5 = ((bf16[64,16,256]{2,1,0:T(8,128)(2,1)}), bf16[64,16,256]{2,1,0:T(8,128)(2,1)S(1)}, u32[]{:S(2)}, u32[]{:S(2)}) async-start(bf16[64,16,256]{2,1,0:T(8,128)(2,1)} %get-tuple-element.63), calls=%async_computation.5 | async-start | bytes 1048576 | tf_op jit(solution)/shard_map/all_to_all | solution.py:31
  103.4 19.3 %collective-permute-start.10 = (bf16[16,8192]{1,0:T(8,128)(2,1)S(1)}, bf16[16,8192]{1,0:T(8,128)(2,1)S(1)}, u32[]{:S(2)}, u32[]{:S(2)}) collective-permute-start(bf16[16,8192]{1,0:T(8,128)(2,1)S(1)} %get-tuple-element.67.x_ref.refs_0_), channel_id=1, source_target_pairs={{0,3},{1,0},{2,1},{3,2},{4,7},{5,4},{6,5},{7,6},{8,11},{9,8},{10,9... | collective-permute-start | bytes 786440 | tf_op jit(solution)/shard_map/ppermute | solution.py:416
  106.2 16.5 %collective-permute-start.9 = (bf16[16,8192]{1,0:T(8,128)(2,1)S(1)}, bf16[16,8192]{1,0:T(8,128)(2,1)S(1)}, u32[]{:S(2)}, u32[]{:S(2)}) collective-permute-start(bf16[16,8192]{1,0:T(8,128)(2,1)S(1)} %get-tuple-element.67.x_ref.refs_0_), channel_id=1, source_target_pairs={{0,2},{1,3},{2,0},{3,1},{4,6},{5,7},{6,4},{7,5},{8,10},{9,11},{10,... | collective-permute-start | bytes 786440 | tf_op jit(solution)/shard_map/ppermute | solution.py:416
  107.0 15.7 %collective-permute-start.8 = (bf16[16,8192]{1,0:T(8,128)(2,1)S(1)}, bf16[16,8192]{1,0:T(8,128)(2,1)S(1)}, u32[]{:S(2)}, u32[]{:S(2)}) collective-permute-start(bf16[16,8192]{1,0:T(8,128)(2,1)S(1)} %get-tuple-element.67.x_ref.refs_0_), channel_id=1, source_target_pairs={{0,1},{1,2},{2,3},{3,0},{4,5},{5,6},{6,7},{7,4},{8,9},{9,10},{10,1... | collective-permute-start | bytes 786440 | tf_op jit(solution)/shard_map/ppermute | solution.py:416
  107.9 11.0 %collective-permute-start.11 = (bf16[16,256]{1,0:T(8,128)(2,1)S(1)}, bf16[16,256]{1,0:T(8,128)(2,1)S(1)}, u32[]{:S(2)}, u32[]{:S(2)}) collective-permute-start(bf16[16,256]{1,0:T(8,128)(2,1)S(1)} %get-tuple-element.64), channel_id=1, source_target_pairs={{0,4},{4,0},{8,12},{12,8},{16,20},{20,16},{24,28},{28,24},{32,36},... | collective-permute-start | bytes 24584 | tf_op jit(solution)/shard_map/ppermute | solution.py:417
  107.9 11.0 %collective-permute-start.12 = (bf16[16,256]{1,0:T(8,128)(2,1)S(1)}, bf16[16,256]{1,0:T(8,128)(2,1)S(1)}, u32[]{:S(2)}, u32[]{:S(2)}) collective-permute-start(bf16[16,256]{1,0:T(8,128)(2,1)S(1)} %get-tuple-element.65), channel_id=1, source_target_pairs={{0,124},{4,8},{8,4},{12,16},{16,12},{20,24},{24,20},{28,32},{32,28... | collective-permute-start | bytes 24584 | tf_op jit(solution)/shard_map/ppermute | solution.py:418
